TPU v7x, 32 devices: a whole 2x2x4 slice. The times are simulated.
32 devices in a mesh: section: 4 (over y, x), seq: 8 (over z, core).
Axes of the slice: x: 2, y: 2, z: 4, core: 2. Of those that a mesh axis runs over, the one named last changes fastest.
Arguments:
- embeds: bfloat16 [4, 1024, 768], P(None, 'seq'), may hold values from -6 to 6
- row_lengths: int32 [4, 4], replicated, may hold values from 1 to 1021, as said below
- qkv_weight: bfloat16 [2, 768, 2304], P(None, 'seq'), may hold values from -0.21875 to 0.21875
- out_weight: bfloat16 [2, 768, 768], P(None, 'seq'), may hold values from -0.21875 to 0.21875
- up_weight: bfloat16 [2, 768, 3072], P(None, 'seq'), may hold values from -0.21875 to 0.21875
- down_weight: bfloat16 [2, 3072, 768], P(None, 'seq'), may hold values from -0.109375 to 0.109375
- model_gains: bfloat16 [2, 3, 768], P(None, None, 'seq'), may hold values from 0.5 to 1.5
- model_biases: bfloat16 [2, 6, 768], P(None, None, 'seq'), may hold values from -1.796875 to 1.796875
- hidden_gains: bfloat16 [2, 3072], P(None, 'seq'), may hold values from 0.5 to 1.5
- hidden_biases: bfloat16 [2, 2, 3072], P(None, None, 'seq'), may hold values from -1.796875 to 1.796875
- cotangent: bfloat16 [4, 1024, 768], P(None, 'seq'), may hold values from -6 to 6
Outputs:
- sublayer_outputs: bfloat16 [4, 4, 1024, 768], P('section', None, 'seq')
- sublayer_grads: bfloat16 [4, 4, 1024, 768], P('section', None, 'seq')
- qkv_grad: float32 [2, 768, 2304], P(None, 'seq')
- out_grad: float32 [2, 768, 768], P(None, 'seq')
- up_grad: float32 [2, 768, 3072], P(None, 'seq')
- down_grad: float32 [2, 3072, 768], P(None, 'seq')
- model_gains_grad: float32 [2, 3, 768], P(None, None, 'seq')
- model_biases_grad: float32 [2, 6, 768], P(None, None, 'seq')
- hidden_gains_grad: float32 [2, 3072], P(None, 'seq')
- hidden_biases_grad: float32 [2, 2, 3072], P(None, None, 'seq')
- pattern_means: float32 [2, 5], replicated
Inputs may be any that keep to these rules, and one draw needn't show every extreme that they name: `row_lengths`: in every micro-batch the 4 lengths sum to 1024; in one micro-batch the first row holds all but 4 - 1 of its tokens.
All inputs are finite; a program needn't handle non-finite values.
Results may differ from a plain program's by a relative error of at most 0.019.
Values may be sent and summed in bfloat16 or wider, within the bound.
A program may use at most 320 MiB of HBM per device.

v0:
```python
import jax
import jax.numpy as jnp
from jax import lax
from jax.sharding import PartitionSpec as P

D = 768
HEADS = 12
HEAD_DIM = 64
FF = 3072


WIDTHS = (2048, 4096, 8192, 16384, 32768)
RATIOS = (1, 2, 4, 6, 12)
EPSILON = 1e-05


def passed_along(value, axis, steps):
    count = lax.axis_size(axis)
    initial, last = (max(0, -steps), min(count, count - steps))
    return lax.ppermute(value, axis, [(source, source + steps) for source in range(initial, last)])


def norm_rows(inputs, gain_row, offset):
    center = inputs - jnp.mean(inputs, -1, keepdims=True)
    spread = jnp.mean(center * center, -1, keepdims=True)
    return center * lax.rsqrt(spread + EPSILON) * gain_row + offset


def place_rows(lengths, token_index):
    row_ends = jnp.cumsum(lengths)
    passed = token_index[:, None] >= row_ends[None, :]
    row_ids = jnp.sum(passed.astype(jnp.int32), 1)
    offsets = token_index - jnp.sum(jnp.where(passed, lengths[None, :], 0), 1)
    return (row_ids, offsets)


def query_chosen(query_pos):
    head_ids = jnp.arange(HEADS, dtype=jnp.int32)
    chosen = []
    for seg_width, seg_ratio in zip(WIDTHS, RATIOS):
        query_pick = query_pos % seg_width % seg_ratio
        chosen.append(query_pick[None, :] == (head_ids % seg_ratio)[:, None])
    return chosen


def pattern_allow(query_rows, query_pos, key_rows, key_pos):
    widths = jnp.array(WIDTHS, jnp.int32)[:, None]
    ratios = jnp.array(RATIOS, jnp.int32)[:, None]
    residue = jnp.arange(HEADS, dtype=jnp.int32)[None, :] % ratios
    query_mod = query_pos[None, :] % widths % ratios
    key_mod = key_pos[None, :] % widths % ratios
    query_ok = query_mod[:, None, :] == residue[:, :, None]
    key_ok = key_mod[:, None, :] == residue[:, :, None]
    common = (query_rows[:, None] == key_rows[None, :]) & (key_pos[None, :] <= query_pos[:, None])
    inside = common[None] & (
        (query_pos[None, :] // widths)[:, :, None] == (key_pos[None, :] // widths)[:, None, :]
    )
    return inside[:, None] & query_ok[:, :, :, None] & key_ok[:, :, None, :]


def block_rows(total_rows):
    step_rows = min(total_rows, 512)
    return step_rows


def split_heads(matrix):
    return matrix.reshape(matrix.shape[0], HEADS, HEAD_DIM)


def pair_terms(query_block, keys_block, query_rows, query_pos, key_rows, key_pos):
    scores = jnp.einsum(
        "qhe,khe->hqk", query_block, keys_block, preferred_element_type=jnp.float32
    ) * HEAD_DIM ** (-0.5)
    allowed = pattern_allow(query_rows, query_pos, key_rows, key_pos)
    counts = jnp.sum(allowed.astype(jnp.float32), 0)
    raised = jnp.exp(scores)
    return (raised, counts * raised, allowed)


def project_tokens(inputs, qkv_matrix, norm_gains, norm_biases):
    hidden = norm_rows(inputs, norm_gains[0], norm_biases[0]).astype(jnp.bfloat16)
    bias_row = jnp.concatenate(
        [jnp.zeros_like(norm_biases[3]), jnp.zeros_like(norm_biases[3]), norm_biases[3]]
    )
    projected = (jnp.dot(hidden, qkv_matrix, preferred_element_type=jnp.float32) + bias_row).astype(
        jnp.bfloat16
    )
    return (hidden, projected)


def attention_forward(section_in, projected, whole_keys, lengths, params, seq_index):
    out_matrix, norm_gains, norm_biases = (params[1], params[4], params[5])
    tok_rows = section_in.shape[0]
    inputs = section_in.astype(jnp.float32)
    queries = split_heads(projected[:, :D])
    query_rows, query_pos = place_rows(
        lengths, seq_index * tok_rows + jnp.arange(tok_rows, dtype=jnp.int32)
    )
    group_rows = whole_keys.shape[0]
    step_rows = block_rows(group_rows)

    def one_block(running, block_start):
        totals, pattern_sums, accumulated = running
        kv_block = lax.dynamic_slice_in_dim(whole_keys, block_start, step_rows, 0)
        key_rows, key_pos = place_rows(
            lengths, block_start + jnp.arange(step_rows, dtype=jnp.int32)
        )
        raised, weighted, allowed = pair_terms(
            queries, split_heads(kv_block[:, :D]), query_rows, query_pos, key_rows, key_pos
        )
        totals = totals + jnp.sum(weighted, -1)
        pattern_sums = pattern_sums + jnp.sum(jnp.where(allowed, raised[None], 0.0), -1)
        accumulated = accumulated + jnp.einsum(
            "hqk,khe->hqe",
            weighted.astype(jnp.bfloat16),
            split_heads(kv_block[:, D:]),
            preferred_element_type=jnp.float32,
        )
        return ((totals, pattern_sums, accumulated), None)

    start_sums = (
        jnp.zeros((HEADS, tok_rows), jnp.float32),
        jnp.zeros((len(WIDTHS), HEADS, tok_rows), jnp.float32),
        jnp.zeros((HEADS, tok_rows, HEAD_DIM), jnp.float32),
    )
    folded, unused = lax.scan(
        one_block, start_sums, jnp.arange(0, group_rows, step_rows, dtype=jnp.int32)
    )
    totals, pattern_sums, accumulated = folded
    attended = jnp.transpose(accumulated / totals[:, :, None], (1, 0, 2)).reshape(tok_rows, D)
    inner_norm = norm_rows(attended, norm_gains[1], norm_biases[1]).astype(jnp.bfloat16)
    branch = jnp.dot(inner_norm, out_matrix, preferred_element_type=jnp.float32) + norm_biases[4]
    section_out = (inputs + branch).astype(jnp.bfloat16)
    chosen = query_chosen(query_pos)
    log_terms = jnp.stack(
        [
            jnp.sum(
                jnp.where(pick_row, jnp.log(jnp.where(pick_row, pattern_sums[number], 1.0)), 0.0)
            )
            for number, pick_row in enumerate(chosen)
        ]
    )
    pick_counts = jnp.stack([jnp.sum(pick_row.astype(jnp.float32)) for pick_row in chosen])
    return (section_out, attended, totals, log_terms, pick_counts)


def feed_forward(section_in, params):
    up_matrix, down_matrix, norm_gains, norm_biases, hidden_gain, hidden_bias = (
        params[2],
        params[3],
        params[4],
        params[5],
        params[6],
        params[7],
    )
    tok_rows = section_in.shape[0]
    inputs = section_in.astype(jnp.float32)
    hidden = norm_rows(inputs, norm_gains[2], norm_biases[2]).astype(jnp.bfloat16)
    upward = jnp.dot(hidden, up_matrix, preferred_element_type=jnp.float32) + hidden_bias[0]
    inner_norm = norm_rows(
        jax.nn.gelu(upward, approximate=False), hidden_gain, hidden_bias[1]
    ).astype(jnp.bfloat16)
    branch = jnp.dot(inner_norm, down_matrix, preferred_element_type=jnp.float32) + norm_biases[5]
    section_out = (inputs + branch).astype(jnp.bfloat16)
    empty_terms = jnp.zeros((len(WIDTHS),), jnp.float32)
    return (
        section_out,
        jnp.zeros((tok_rows, D), jnp.float32),
        jnp.zeros((HEADS, tok_rows), jnp.float32),
        empty_terms,
        empty_terms,
    )


def attention_middle(
    section_in, grad_out, attended, totals, lengths, all_keys, projected, params, seq_index
):
    out_matrix, norm_gains, norm_biases = (params[1], params[4], params[5])
    scale_factor = HEAD_DIM ** (-0.5)
    tok_rows = section_in.shape[0]
    queries = split_heads(projected[:, :D])
    query_rows, query_pos = place_rows(
        lengths, seq_index * tok_rows + jnp.arange(tok_rows, dtype=jnp.int32)
    )
    inner_norm = norm_rows(attended, norm_gains[1], norm_biases[1]).astype(jnp.bfloat16)
    out_step = jnp.einsum("td,tf->df", inner_norm, grad_out, preferred_element_type=jnp.float32)
    inner_grad = jnp.einsum("tf,df->td", grad_out, out_matrix, preferred_element_type=jnp.float32)
    unused, inner_back = jax.vjp(norm_rows, attended, norm_gains[1], norm_biases[1])
    attended_grad, inner_gain_grad, inner_bias_grad = inner_back(inner_grad)
    low_attended = attended_grad.astype(jnp.bfloat16)
    head_grad = split_heads(low_attended)
    row_dots = jnp.einsum("qhe,qhe->hq", head_grad.astype(jnp.float32), split_heads(attended))
    scaled_grad = head_grad.astype(jnp.float32) / jnp.transpose(totals)[:, :, None]
    group_rows = all_keys.shape[0]
    step_rows = block_rows(group_rows)

    def grad_block(query_grad, block_start):
        kv_block = lax.dynamic_slice_in_dim(all_keys, block_start, step_rows, 0)
        keys_block = split_heads(kv_block[:, :D])
        values_block = split_heads(kv_block[:, D:])
        key_rows, key_pos = place_rows(
            lengths, block_start + jnp.arange(step_rows, dtype=jnp.int32)
        )
        raised, weighted, allowed = pair_terms(
            queries, keys_block, query_rows, query_pos, key_rows, key_pos
        )
        prob_grad = jnp.einsum(
            "qhe,khe->hqk", head_grad, values_block, preferred_element_type=jnp.float32
        )
        score_grad = (weighted / totals[:, :, None] * (prob_grad - row_dots[:, :, None])).astype(
            jnp.bfloat16
        )
        query_grad = (
            query_grad
            + jnp.einsum("hqk,khe->qhe", score_grad, keys_block, preferred_element_type=jnp.float32)
            * scale_factor
        )
        key_grad = (
            jnp.einsum("hqk,qhe->khe", score_grad, queries, preferred_element_type=jnp.float32)
            * scale_factor
        )
        value_grad = jnp.einsum(
            "hqk,qhe->khe",
            weighted.astype(jnp.bfloat16),
            scaled_grad,
            preferred_element_type=jnp.float32,
        )
        block_grad = jnp.concatenate(
            [key_grad.reshape(step_rows, D), value_grad.reshape(step_rows, D)], 1
        )
        return (query_grad, block_grad)

    query_grad, block_grads = lax.scan(
        grad_block,
        jnp.zeros((tok_rows, HEADS, HEAD_DIM), jnp.float32),
        jnp.arange(0, group_rows, step_rows, dtype=jnp.int32),
    )
    block_grads = block_grads.reshape(group_rows, 2 * D)
    return (
        query_grad.reshape(tok_rows, D),
        low_attended,
        row_dots,
        block_grads,
        out_step,
        inner_gain_grad,
        inner_bias_grad,
    )


def attention_finish(section_in, grad_out, middle, extra, params, grad_sums):
    qkv_matrix, norm_gains, norm_biases = (params[0], params[4], params[5])
    inputs = section_in.astype(jnp.float32)
    grad_float = grad_out.astype(jnp.float32)
    hidden = norm_rows(inputs, norm_gains[0], norm_biases[0]).astype(jnp.bfloat16)
    query_grad, low_attended, row_dots, block_grads, out_step, inner_gain_grad, inner_bias_grad = (
        middle
    )
    own_grads = extra[0]
    proj_grad = jnp.concatenate([query_grad, own_grads], 1).astype(jnp.bfloat16)
    qkv_step = jnp.einsum("td,tf->df", hidden, proj_grad, preferred_element_type=jnp.float32)
    value_bias_sums = jnp.sum(proj_grad[:, 2 * D :].astype(jnp.float32), 0)
    hidden_grad = jnp.einsum("tf,df->td", proj_grad, qkv_matrix, preferred_element_type=jnp.float32)
    unused_first, first_back = jax.vjp(norm_rows, inputs, norm_gains[0], norm_biases[0])
    input_grad, first_gain_grad, first_bias_grad = first_back(hidden_grad)
    qkv_sum, out_sum, up_sum, down_sum, gain_sum, bias_sum, hgain_sum, hbias_sum = grad_sums
    gain_sum = gain_sum.at[0].add(first_gain_grad).at[1].add(inner_gain_grad)
    bias_sum = (
        bias_sum.at[0]
        .add(first_bias_grad)
        .at[1]
        .add(inner_bias_grad)
        .at[3]
        .add(value_bias_sums)
        .at[4]
        .add(jnp.sum(grad_float, 0))
    )
    return (
        grad_float + input_grad,
        (
            qkv_sum + qkv_step,
            out_sum + out_step,
            up_sum,
            down_sum,
            gain_sum,
            bias_sum,
            hgain_sum,
            hbias_sum,
        ),
    )


def feed_backward(section_in, grad_out, params, grad_sums):
    up_matrix, down_matrix, norm_gains, norm_biases, hidden_gain, hidden_bias = (
        params[2],
        params[3],
        params[4],
        params[5],
        params[6],
        params[7],
    )
    inputs = section_in.astype(jnp.float32)
    grad_float = grad_out.astype(jnp.float32)
    hidden = norm_rows(inputs, norm_gains[2], norm_biases[2]).astype(jnp.bfloat16)
    upward = jnp.dot(hidden, up_matrix, preferred_element_type=jnp.float32) + hidden_bias[0]

    def inner_rows(upward_in, gain_row, bias_row):
        return norm_rows(jax.nn.gelu(upward_in, approximate=False), gain_row, bias_row)

    inner_value, inner_back = jax.vjp(inner_rows, upward, hidden_gain, hidden_bias[1])
    inner_norm = inner_value.astype(jnp.bfloat16)
    down_step = jnp.einsum("tf,td->fd", inner_norm, grad_out, preferred_element_type=jnp.float32)
    inner_grad = jnp.einsum("td,fd->tf", grad_out, down_matrix, preferred_element_type=jnp.float32)
    upward_grad, hgain_step, hbias_step = inner_back(inner_grad)
    low_upward = upward_grad.astype(jnp.bfloat16)
    up_step = jnp.einsum("td,tf->df", hidden, low_upward, preferred_element_type=jnp.float32)
    hidden_grad = jnp.einsum("tf,df->td", low_upward, up_matrix, preferred_element_type=jnp.float32)
    unused, first_back = jax.vjp(norm_rows, inputs, norm_gains[2], norm_biases[2])
    input_grad, first_gain_grad, first_bias_grad = first_back(hidden_grad)
    qkv_sum, out_sum, up_sum, down_sum, gain_sum, bias_sum, hgain_sum, hbias_sum = grad_sums
    gain_sum = gain_sum.at[2].add(first_gain_grad)
    bias_sum = bias_sum.at[2].add(first_bias_grad).at[5].add(jnp.sum(grad_float, 0))
    hbias_sum = (
        hbias_sum.at[0].add(jnp.sum(low_upward.astype(jnp.float32), 0)).at[1].add(hbias_step)
    )
    return (
        grad_float + input_grad,
        (
            qkv_sum,
            out_sum,
            up_sum + up_step,
            down_sum + down_step,
            gain_sum,
            bias_sum,
            hgain_sum + hgain_step,
            hbias_sum,
        ),
    )


def keep_slot(store, fresh, slot_id, in_range):
    previous = lax.dynamic_index_in_dim(store, slot_id, 0, False)
    return lax.dynamic_update_index_in_dim(store, jnp.where(in_range, fresh, previous), slot_id, 0)


def body(
    embeds,
    row_lengths,
    qkv_weight,
    out_weight,
    up_weight,
    down_weight,
    model_gains,
    model_biases,
    hidden_gains,
    hidden_biases,
    cotangent,
):
    section_id = lax.axis_index("section")
    seq_index = lax.axis_index("seq")
    section_count = lax.axis_size("section")
    micro_count = embeds.shape[0]
    tok_rows = embeds.shape[1]
    group_rows = tok_rows * lax.axis_size("seq")
    layer_id = section_id // 2
    attends = section_id % 2 == 0
    bias_count = model_biases.shape[1]

    def pick_layer(stacked):
        return lax.dynamic_index_in_dim(stacked, layer_id, 0, False)

    gathered = (
        lax.all_gather(pick_layer(qkv_weight), "seq", axis=0, tiled=True),
        lax.all_gather(pick_layer(out_weight), "seq", axis=0, tiled=True),
        lax.all_gather(pick_layer(up_weight), "seq", axis=0, tiled=True),
        lax.all_gather(pick_layer(down_weight), "seq", axis=0, tiled=True),
        lax.all_gather(pick_layer(model_gains), "seq", axis=1, tiled=True),
        lax.all_gather(pick_layer(model_biases), "seq", axis=1, tiled=True),
        lax.all_gather(pick_layer(hidden_gains), "seq", axis=0, tiled=True),
        lax.all_gather(pick_layer(hidden_biases), "seq", axis=1, tiled=True),
    )
    params = tuple(gathered[:4]) + tuple((vector.astype(jnp.float32) for vector in gathered[4:]))
    whole_shape = (0,)

    def make_projected(section_in):
        return project_tokens(section_in.astype(jnp.float32), params[0], params[4], params[5])[1]

    def skip_projected(section_in):
        return jnp.zeros((tok_rows, 3 * D), jnp.bfloat16)

    def run_attention(section_in, projected, whole_keys, lengths):
        return attention_forward(section_in, projected, whole_keys, lengths, params, seq_index)

    def run_feed(section_in, projected, whole_keys, lengths):
        return feed_forward(section_in, params)

    def forward_tick(running, tick_id):
        (
            incoming,
            kept_inputs,
            kept_attended,
            kept_totals,
            kept_whole,
            outputs,
            log_sums,
            pick_sums,
        ) = running
        micro_id = tick_id - section_id
        in_range = (micro_id >= 0) & (micro_id < micro_count)
        slot_id = jnp.clip(micro_id, 0, micro_count - 1)
        lengths = lax.dynamic_index_in_dim(row_lengths, slot_id, 0, False)
        section_in = jnp.where(
            section_id == 0, lax.dynamic_index_in_dim(embeds, slot_id, 0, False), incoming
        )
        projected = lax.cond(attends, make_projected, skip_projected, section_in)
        whole_keys = lax.all_gather(projected[:, D:], "seq", axis=0, tiled=True)
        section_out, attended, totals, log_terms, pick_counts = lax.cond(
            attends, run_attention, run_feed, section_in, projected, whole_keys, lengths
        )
        kept_inputs = keep_slot(kept_inputs, section_in, slot_id, in_range)
        kept_attended = keep_slot(kept_attended, attended, slot_id, in_range)
        kept_totals = keep_slot(kept_totals, totals, slot_id, in_range)
        outputs = keep_slot(outputs, section_out, slot_id, in_range)
        log_sums = log_sums + jnp.where(in_range, log_terms, 0.0)
        pick_sums = pick_sums + jnp.where(in_range, pick_counts, 0.0)
        incoming = passed_along(section_out, "section", 1)
        return (
            (
                incoming,
                kept_inputs,
                kept_attended,
                kept_totals,
                kept_whole,
                outputs,
                log_sums,
                pick_sums,
            ),
            None,
        )

    forward_start = (
        jnp.zeros((tok_rows, D), jnp.bfloat16),
        jnp.zeros((micro_count, tok_rows, D), jnp.bfloat16),
        jnp.zeros((micro_count, tok_rows, D), jnp.float32),
        jnp.zeros((micro_count, HEADS, tok_rows), jnp.float32),
        jnp.zeros((micro_count,) + whole_shape, jnp.bfloat16),
        jnp.zeros((micro_count, tok_rows, D), jnp.bfloat16),
        jnp.zeros((len(WIDTHS),), jnp.float32),
        jnp.zeros((len(WIDTHS),), jnp.float32),
    )
    ticks = jnp.arange(micro_count + section_count - 1, dtype=jnp.int32)
    forward_end, unused = lax.scan(forward_tick, forward_start, ticks)
    unused_in, kept_inputs, kept_attended, kept_totals, kept_whole, outputs, log_sums, pick_sums = (
        forward_end
    )
    block_shape = (group_rows, 2 * D)

    def middle_attention(section_in, grad_out, attended, totals, lengths, all_keys, projected):
        return attention_middle(
            section_in, grad_out, attended, totals, lengths, all_keys, projected, params, seq_index
        )

    def middle_feed(section_in, grad_out, attended, totals, lengths, all_keys, projected):
        return (
            jnp.zeros((tok_rows, D), jnp.float32),
            jnp.zeros((tok_rows, D), jnp.bfloat16),
            jnp.zeros((HEADS, tok_rows), jnp.float32),
            jnp.zeros(block_shape, jnp.float32),
            jnp.zeros((D, D), jnp.float32),
            jnp.zeros((D,), jnp.float32),
            jnp.zeros((D,), jnp.float32),
        )

    def finish_attention(section_in, grad_out, projected, middle, extra, lengths, grad_sums):
        return attention_finish(section_in, grad_out, middle, extra, params, grad_sums)

    def finish_feed(section_in, grad_out, projected, middle, extra, lengths, grad_sums):
        return feed_backward(section_in, grad_out, params, grad_sums)

    def backward_tick(running, tick_id):
        incoming, grad_sums, input_grads = running
        micro_id = micro_count - 1 - tick_id + (section_count - 1 - section_id)
        in_range = (micro_id >= 0) & (micro_id < micro_count)
        slot_id = jnp.clip(micro_id, 0, micro_count - 1)
        from_next = jnp.where(
            section_id == section_count - 1,
            lax.dynamic_index_in_dim(cotangent, slot_id, 0, False),
            incoming,
        )
        grad_out = jnp.where(in_range, from_next, jnp.zeros_like(from_next))
        section_in = lax.dynamic_index_in_dim(kept_inputs, slot_id, 0, False)
        attended = lax.dynamic_index_in_dim(kept_attended, slot_id, 0, False)
        totals = lax.dynamic_index_in_dim(kept_totals, slot_id, 0, False)
        lengths = lax.dynamic_index_in_dim(row_lengths, slot_id, 0, False)
        projected = lax.cond(attends, make_projected, skip_projected, section_in)
        all_keys = lax.all_gather(projected[:, D:], "seq", axis=0, tiled=True)
        middle = lax.cond(
            attends,
            middle_attention,
            middle_feed,
            section_in,
            grad_out,
            attended,
            totals,
            lengths,
            all_keys,
            projected,
        )
        extra = (lax.psum_scatter(middle[3], "seq", scatter_dimension=0, tiled=True),)
        section_grad, grad_sums = lax.cond(
            attends,
            finish_attention,
            finish_feed,
            section_in,
            grad_out,
            projected,
            middle,
            extra,
            lengths,
            grad_sums,
        )
        low_grad = section_grad.astype(jnp.bfloat16)
        input_grads = keep_slot(input_grads, low_grad, slot_id, in_range)
        incoming = passed_along(low_grad, "section", -1)
        return ((incoming, grad_sums, input_grads), None)

    grad_start = (
        jnp.zeros((D, 3 * D), jnp.float32),
        jnp.zeros((D, D), jnp.float32),
        jnp.zeros((D, FF), jnp.float32),
        jnp.zeros((FF, D), jnp.float32),
        jnp.zeros((3, D), jnp.float32),
        jnp.zeros((bias_count, D), jnp.float32),
        jnp.zeros((FF,), jnp.float32),
        jnp.zeros((2, FF), jnp.float32),
    )
    backward_start = (
        jnp.zeros((tok_rows, D), jnp.bfloat16),
        grad_start,
        jnp.zeros((micro_count, tok_rows, D), jnp.bfloat16),
    )
    backward_end, unused_back = lax.scan(backward_tick, backward_start, ticks)
    unused_grad, grad_sums, input_grads = backward_end
    shards = (
        lax.psum_scatter(grad_sums[0], "seq", scatter_dimension=0, tiled=True),
        lax.psum_scatter(grad_sums[1], "seq", scatter_dimension=0, tiled=True),
        lax.psum_scatter(grad_sums[2], "seq", scatter_dimension=0, tiled=True),
        lax.psum_scatter(grad_sums[3], "seq", scatter_dimension=0, tiled=True),
        lax.psum_scatter(grad_sums[4], "seq", scatter_dimension=1, tiled=True),
        lax.psum_scatter(grad_sums[5], "seq", scatter_dimension=1, tiled=True),
        lax.psum_scatter(grad_sums[6], "seq", scatter_dimension=0, tiled=True),
        lax.psum_scatter(grad_sums[7], "seq", scatter_dimension=1, tiled=True),
    )
    sources = (
        qkv_weight,
        out_weight,
        up_weight,
        down_weight,
        model_gains,
        model_biases,
        hidden_gains,
        hidden_biases,
    )
    placed = tuple(
        (
            lax.dynamic_update_index_in_dim(
                jnp.zeros(source.shape, jnp.float32), shard, layer_id, 0
            )
            for shard, source in zip(shards, sources)
        )
    )
    summed = (
        lax.psum(placed[0].astype(jnp.bfloat16), "section").astype(jnp.float32),
        lax.psum(placed[1].astype(jnp.bfloat16), "section").astype(jnp.float32),
        lax.psum(placed[2].astype(jnp.bfloat16), "section").astype(jnp.float32),
        lax.psum(placed[3].astype(jnp.bfloat16), "section").astype(jnp.float32),
        lax.psum(placed[4].astype(jnp.bfloat16), "section").astype(jnp.float32),
        lax.psum(placed[5].astype(jnp.bfloat16), "section").astype(jnp.float32),
        lax.psum(placed[6].astype(jnp.bfloat16), "section").astype(jnp.float32),
        lax.psum(placed[7].astype(jnp.bfloat16), "section").astype(jnp.float32),
    )
    layer_count = qkv_weight.shape[0]
    layer_terms = lax.dynamic_update_index_in_dim(
        jnp.zeros((layer_count, len(WIDTHS)), jnp.float32), log_sums, layer_id, 0
    )
    layer_picks = lax.dynamic_update_index_in_dim(
        jnp.zeros((layer_count, len(WIDTHS)), jnp.float32), pick_sums, layer_id, 0
    )
    log_totals, pick_totals = lax.psum((layer_terms, layer_picks), ("section", "seq"))
    pattern_means = log_totals / pick_totals
    return (
        outputs[None],
        input_grads[None],
        summed[0],
        summed[1],
        summed[2],
        summed[3],
        summed[4],
        summed[5],
        summed[6],
        summed[7],
        pattern_means,
    )


def solution(mesh):
    return jax.shard_map(
        body,
        mesh=mesh,
        in_specs=(
            P(None, "seq", None),
            P(),
            P(None, "seq", None),
            P(None, "seq", None),
            P(None, "seq", None),
            P(None, "seq", None),
            P(None, None, "seq"),
            P(None, None, "seq"),
            P(None, "seq"),
            P(None, None, "seq"),
            P(None, "seq", None),
        ),
        out_specs=(
            P("section", None, "seq", None),
            P("section", None, "seq", None),
            P(None, "seq", None),
            P(None, "seq", None),
            P(None, "seq", None),
            P(None, "seq", None),
            P(None, None, "seq"),
            P(None, None, "seq"),
            P(None, "seq"),
            P(None, None, "seq"),
            P(),
        ),
        check_vma=False,
    )
```

profile of v0, /device:TPU:14, one launch (start us, length us, event | category | flops | bytes accessed | tf_op | source)
XLA Modules:
  0.0 3542.2 jit_solution(15384873778998881099)
XLA Ops:
  78.3 52.4 %all-gather.17.cloned.1.call-done = bf16[1,768,3072]{2,1,0:T(8,128)(2,1)} async-done(((bf16[1,96,3072]{2,1,0:T(8,128)(2,1)}), bf16[1,768,3072]{2,1,0:T(8,128)(2,1)}) %all-gather.17.cloned.1.call-update) | async-done | bytes 4718608 | tf_op jit(solution)/shard_map/all_gather | solution.py:374
  130.7 52.6 %all-gather.19.cloned.1.call-done = bf16[1,3072,768]{2,1,0:T(8,128)(2,1)} async-done(((bf16[1,384,768]{2,1,0:T(8,128)(2,1)}), bf16[1,3072,768]{2,1,0:T(8,128)(2,1)}) %all-gather.19.cloned.1.call-update) | async-done | bytes 4718608 | tf_op jit(solution)/shard_map/all_gather | solution.py:375
  186.7 1063.9 %while.110 = (s32[]{:T(128)}, bf16[128,768]{1,0:T(8,128)(2,1)S(1)}, bf16[4,128,768]{2,1,0:T(8,128)(2,1)}, f32[4,128,768]{1,2,0:T(8,128)}, f32[4,12,128]{2,1,0:T(...) while((s32[]{:T(128)}, bf16[128,768]{1,0:T(8,128)(2,1)S(1)}, ...), condition=%wide.region_32.40_spmd.clone.clone, body=%wide.region_0.39_spmd.sunk.clone.clone.sunk | while | flops 1693779840 | bytes 100696176 | solution.py:451
  249.9 87.1 %collective-permute-done = bf16[128,768]{1,0:T(8,128)(2,1)S(1)} collective-permute-done((bf16[128,768]{1,0:T(8,128)(2,1)}, bf16[128,768]{1,0:T(8,128)(2,1)S(1)}, u32[]{:S(2)}, u32[]{:S(2)}) %collective-permute-start) | collective-permute-done | bytes 196640 | tf_op jit(solution)/shard_map/while/body/eval_jaxpr/ppermute | solution.py:20
  402.1 87.1 %collective-permute-done = bf16[128,768]{1,0:T(8,128)(2,1)S(1)} collective-permute-done((bf16[128,768]{1,0:T(8,128)(2,1)}, bf16[128,768]{1,0:T(8,128)(2,1)S(1)}, u32[]{:S(2)}, u32[]{:S(2)}) %collective-permute-start) | collective-permute-done | bytes 196640 | tf_op jit(solution)/shard_map/while/body/eval_jaxpr/ppermute | solution.py:20
  554.3 87.2 %collective-permute-done = bf16[128,768]{1,0:T(8,128)(2,1)S(1)} collective-permute-done((bf16[128,768]{1,0:T(8,128)(2,1)}, bf16[128,768]{1,0:T(8,128)(2,1)S(1)}, u32[]{:S(2)}, u32[]{:S(2)}) %collective-permute-start) | collective-permute-done | bytes 196640 | tf_op jit(solution)/shard_map/while/body/eval_jaxpr/ppermute | solution.py:20
  709.0 84.8 %collective-permute-done = bf16[128,768]{1,0:T(8,128)(2,1)S(1)} collective-permute-done((bf16[128,768]{1,0:T(8,128)(2,1)}, bf16[128,768]{1,0:T(8,128)(2,1)S(1)}, u32[]{:S(2)}, u32[]{:S(2)}) %collective-permute-start) | collective-permute-done | bytes 196640 | tf_op jit(solution)/shard_map/while/body/eval_jaxpr/ppermute | solution.py:20
  861.3 84.8 %collective-permute-done = bf16[128,768]{1,0:T(8,128)(2,1)S(1)} collective-permute-done((bf16[128,768]{1,0:T(8,128)(2,1)}, bf16[128,768]{1,0:T(8,128)(2,1)S(1)}, u32[]{:S(2)}, u32[]{:S(2)}) %collective-permute-start) | collective-permute-done | bytes 196640 | tf_op jit(solution)/shard_map/while/body/eval_jaxpr/ppermute | solution.py:20
  1013.6 84.8 %collective-permute-done = bf16[128,768]{1,0:T(8,128)(2,1)S(1)} collective-permute-done((bf16[128,768]{1,0:T(8,128)(2,1)}, bf16[128,768]{1,0:T(8,128)(2,1)S(1)}, u32[]{:S(2)}, u32[]{:S(2)}) %collective-permute-start) | collective-permute-done | bytes 196640 | tf_op jit(solution)/shard_map/while/body/eval_jaxpr/ppermute | solution.py:20
  1165.9 84.7 %collective-permute-done = bf16[128,768]{1,0:T(8,128)(2,1)S(1)} collective-permute-done((bf16[128,768]{1,0:T(8,128)(2,1)}, bf16[128,768]{1,0:T(8,128)(2,1)S(1)}, u32[]{:S(2)}, u32[]{:S(2)}) %collective-permute-start) | collective-permute-done | bytes 196640 | tf_op jit(solution)/shard_map/while/body/eval_jaxpr/ppermute | solution.py:20
  1269.2 1743.1 %while.109 = (s32[]{:T(128)}, bf16[128,768]{1,0:T(8,128)(2,1)}, f32[768,2304]{1,0:T(8,128)}, f32[768,768]{1,0:T(8,128)}, f32[768,3072]{1,0:T(8,128)}, /*index=5*...) while((s32[]{:T(128)}, bf16[128,768]{1,0:T(8,128)(2,1)}, ...), condition=%wide.region_79.87_spmd.clone, body=%wide.region_33.86_spmd.sunk.clone.sunk | while | flops 4359378944 | bytes 253367648 | solution.py:541
  1339.3 144.0 %reduce-scatter.29.cloned.1.call-done = f32[128,1536]{1,0:T(8,128)} async-done(((f32[1024,1536]{1,0:T(8,128)}), f32[128,1536]{1,0:T(8,128)}) %reduce-scatter.29.cloned.1.call-update) | async-done | bytes 786448 | tf_op jit(solution)/shard_map/while/body/eval_jaxpr/reduce_scatter | solution.py:508
  1483.3 42.9 %conditional.49 = (f32[768,2304]{1,0:T(8,128)}, f32[768,768]{1,0:T(8,128)}, f32[768,3072]{1,0:T(8,128)}, f32[3072,768]{1,0:T(8,128)}, f32[3,768]{1,0:T(4,128)}, ...) conditional(s32[]{:T(128)} %convert_element_type.472, ...), branch_computations={%region_55.76_spmd, %region_70.85_spmd} | conditional | flops 3072984576 | bytes 105913984
  1537.3 41.8 %all-gather.23.cloned.1.call-done = bf16[1024,1536]{0,1:T(8,128)(2,1)} async-done(((bf16[128,1536]{0,1:T(8,128)(2,1)}), bf16[1024,1536]{0,1:T(8,128)(2,1)}) %all-gather.23.cloned.1.call-update) | async-done | bytes 3145744 | tf_op jit(solution)/shard_map/while/body/eval_jaxpr/all_gather | solution.py:495
  1585.9 144.0 %reduce-scatter.29.cloned.1.call-done = f32[128,1536]{1,0:T(8,128)} async-done(((f32[1024,1536]{1,0:T(8,128)}), f32[128,1536]{1,0:T(8,128)}) %reduce-scatter.29.cloned.1.call-update) | async-done | bytes 786448 | tf_op jit(solution)/shard_map/while/body/eval_jaxpr/reduce_scatter | solution.py:508
  1729.9 42.9 %conditional.49 = (f32[768,2304]{1,0:T(8,128)}, f32[768,768]{1,0:T(8,128)}, f32[768,3072]{1,0:T(8,128)}, f32[3072,768]{1,0:T(8,128)}, f32[3,768]{1,0:T(4,128)}, ...) conditional(s32[]{:T(128)} %convert_element_type.472, ...), branch_computations={%region_55.76_spmd, %region_70.85_spmd} | conditional | flops 3072984576 | bytes 105913984
  1783.9 41.8 %all-gather.23.cloned.1.call-done = bf16[1024,1536]{0,1:T(8,128)(2,1)} async-done(((bf16[128,1536]{0,1:T(8,128)(2,1)}), bf16[1024,1536]{0,1:T(8,128)(2,1)}) %all-gather.23.cloned.1.call-update) | async-done | bytes 3145744 | tf_op jit(solution)/shard_map/while/body/eval_jaxpr/all_gather | solution.py:495
  1832.5 144.0 %reduce-scatter.29.cloned.1.call-done = f32[128,1536]{1,0:T(8,128)} async-done(((f32[1024,1536]{1,0:T(8,128)}), f32[128,1536]{1,0:T(8,128)}) %reduce-scatter.29.cloned.1.call-update) | async-done | bytes 786448 | tf_op jit(solution)/shard_map/while/body/eval_jaxpr/reduce_scatter | solution.py:508
  1976.5 42.9 %conditional.49 = (f32[768,2304]{1,0:T(8,128)}, f32[768,768]{1,0:T(8,128)}, f32[768,3072]{1,0:T(8,128)}, f32[3072,768]{1,0:T(8,128)}, f32[3,768]{1,0:T(4,128)}, ...) conditional(s32[]{:T(128)} %convert_element_type.472, ...), branch_computations={%region_55.76_spmd, %region_70.85_spmd} | conditional | flops 3072984576 | bytes 105913984
  2079.2 144.0 %reduce-scatter.29.cloned.1.call-done = f32[128,1536]{1,0:T(8,128)} async-done(((f32[1024,1536]{1,0:T(8,128)}), f32[128,1536]{1,0:T(8,128)}) %reduce-scatter.29.cloned.1.call-update) | async-done | bytes 786448 | tf_op jit(solution)/shard_map/while/body/eval_jaxpr/reduce_scatter | solution.py:508
  2223.2 42.9 %conditional.49 = (f32[768,2304]{1,0:T(8,128)}, f32[768,768]{1,0:T(8,128)}, f32[768,3072]{1,0:T(8,128)}, f32[3072,768]{1,0:T(8,128)}, f32[3,768]{1,0:T(4,128)}, ...) conditional(s32[]{:T(128)} %convert_element_type.472, ...), branch_computations={%region_55.76_spmd, %region_70.85_spmd} | conditional | flops 3072984576 | bytes 105913984
  2325.8 144.0 %reduce-scatter.29.cloned.1.call-done = f32[128,1536]{1,0:T(8,128)} async-done(((f32[1024,1536]{1,0:T(8,128)}), f32[128,1536]{1,0:T(8,128)}) %reduce-scatter.29.cloned.1.call-update) | async-done | bytes 786448 | tf_op jit(solution)/shard_map/while/body/eval_jaxpr/reduce_scatter | solution.py:508
  2469.8 42.9 %conditional.49 = (f32[768,2304]{1,0:T(8,128)}, f32[768,768]{1,0:T(8,128)}, f32[768,3072]{1,0:T(8,128)}, f32[3072,768]{1,0:T(8,128)}, f32[3,768]{1,0:T(4,128)}, ...) conditional(s32[]{:T(128)} %convert_element_type.472, ...), branch_computations={%region_55.76_spmd, %region_70.85_spmd} | conditional | flops 3072984576 | bytes 105913984
  2572.4 144.0 %reduce-scatter.29.cloned.1.call-done = f32[128,1536]{1,0:T(8,128)} async-done(((f32[1024,1536]{1,0:T(8,128)}), f32[128,1536]{1,0:T(8,128)}) %reduce-scatter.29.cloned.1.call-update) | async-done | bytes 786448 | tf_op jit(solution)/shard_map/while/body/eval_jaxpr/reduce_scatter | solution.py:508
  2716.4 42.9 %conditional.49 = (f32[768,2304]{1,0:T(8,128)}, f32[768,768]{1,0:T(8,128)}, f32[768,3072]{1,0:T(8,128)}, f32[3072,768]{1,0:T(8,128)}, f32[3,768]{1,0:T(4,128)}, ...) conditional(s32[]{:T(128)} %convert_element_type.472, ...), branch_computations={%region_55.76_spmd, %region_70.85_spmd} | conditional | flops 3072984576 | bytes 105913984
  2819.0 144.0 %reduce-scatter.29.cloned.1.call-done = f32[128,1536]{1,0:T(8,128)} async-done(((f32[1024,1536]{1,0:T(8,128)}), f32[128,1536]{1,0:T(8,128)}) %reduce-scatter.29.cloned.1.call-update) | async-done | bytes 786448 | tf_op jit(solution)/shard_map/while/body/eval_jaxpr/reduce_scatter | solution.py:508
  2963.0 42.9 %conditional.49 = (f32[768,2304]{1,0:T(8,128)}, f32[768,768]{1,0:T(8,128)}, f32[768,3072]{1,0:T(8,128)}, f32[3072,768]{1,0:T(8,128)}, f32[3,768]{1,0:T(4,128)}, ...) conditional(s32[]{:T(128)} %convert_element_type.472, ...), branch_computations={%region_55.76_spmd, %region_70.85_spmd} | conditional | flops 3072984576 | bytes 105913984
  3052.7 78.7 %reduce-scatter.15.cloned.1.call-done = f32[96,2304]{1,0:T(8,128)} async-done(((f32[768,2304]{1,0:T(8,128)}), f32[96,2304]{1,0:T(8,128)}) %reduce-scatter.15.cloned.1.call-update) | async-done | bytes 884752 | tf_op jit(solution)/shard_map/reduce_scatter | solution.py:544
  3132.7 98.9 %reduce-scatter.19.cloned.1.call-done = f32[96,3072]{1,0:T(8,128)} async-done(((f32[768,3072]{1,0:T(8,128)}), f32[96,3072]{1,0:T(8,128)}) %reduce-scatter.19.cloned.1.call-update) | async-done | bytes 1179664 | tf_op jit(solution)/shard_map/reduce_scatter | solution.py:546
  3232.9 98.8 %reduce-scatter.21.cloned.1.call-done = f32[384,768]{1,0:T(8,128)} async-done(((f32[3072,768]{1,0:T(8,128)}), f32[384,768]{1,0:T(8,128)}) %reduce-scatter.21.cloned.1.call-update) | async-done | bytes 1179664 | tf_op jit(solution)/shard_map/reduce_scatter | solution.py:547
  3335.5 42.0 %all-reduce.3 = (f32[2,5]{1,0:T(2,128)S(1)}, f32[2,5]{1,0:T(2,128)S(1)}) all-reduce(f32[2,5]{1,0:T(2,128)S(1)} %dynamic_update_slice.76, f32[2,5]{1,0:T(2,128)S(1)} %dynamic_update_slice.77), channel_id=1, replica_groups=mesh['section'=4,'seq'=8] {'section','seq'}, use_global_device_ids=true, to_apply=%region_96.104 | all-reduce | flops 20 | bytes 160 | tf_op jit(solution)/shard_map/psum | solution.py:588
  3440.7 87.6 %all-reduce.8.cloned.1.call-done = (bf16[2,96,2304]{2,1,0:T(8,128)(2,1)}, bf16[2,96,768]{2,1,0:T(8,128)(2,1)}, bf16[2,96,3072]{2,1,0:T(8,128)(2,1)}, bf16[2,384,768]{2,1,0:T(8,128)(2,1)}) async-done(((bf16[2,96,2304]{2,1,0:T(8,128)(2,1)}, bf16[2,96,768]{2,1,0:T(8,128)(2,1)}, bf16[2,96,3072]{2,1,0:T(8,128)(2,1)}, bf16[2,384,768]{2,1,0:T(8,128)(2,1)}), (bf16[2,96,2304]{2,1,0:T(8,128)(2,1)}, ...) | async-done | bytes 3538960 | tf_op jit(solution)/shard_map/psum | solution.py:572
  (1270 shorter events, 1413.9 us)
Async XLA Ops:
  7.2 63.8 %all-gather.21.cloned.1.call-start = ((), (), s32[]{:S(2)}) async-start(), calls=%async_computation.15 | async-start | bytes 1327104 | tf_op jit(solution)/shard_map/all_gather | solution.py:373
  9.0 69.3 %all-gather.15.cloned.1.call-start = ((), (), s32[]{:S(2)}) async-start(), calls=%async_computation.12 | async-start | bytes 3981312 | tf_op jit(solution)/shard_map/all_gather | solution.py:372
  10.9 119.7 %all-gather.17.cloned.1.call-start = ((), (), s32[]{:S(2)}) async-start(), calls=%async_computation.13 | async-start | bytes 5308416 | tf_op jit(solution)/shard_map/all_gather | solution.py:374
  11.9 171.4 %all-gather.19.cloned.1.call-start = ((), (), s32[]{:S(2)}) async-start(), calls=%async_computation.14 | async-start | bytes 5308416 | tf_op jit(solution)/shard_map/all_gather | solution.py:375
  247.9 89.1 %collective-permute-start = (bf16[128,768]{1,0:T(8,128)(2,1)}, bf16[128,768]{1,0:T(8,128)(2,1)S(1)}, u32[]{:S(2)}, u32[]{:S(2)}) collective-permute-start(bf16[128,768]{1,0:T(8,128)(2,1)} %get-tuple-element.2961), channel_id=1, source_target_pairs={{0,8},{8,16},{16,24},{1,9},{9,17},{17,25},{2,10},{10,18},{18,26},{... | collective-permute-start | bytes 589832 | tf_op jit(solution)/shard_map/while/body/eval_jaxpr/ppermute | solution.py:20
  337.0 48.2 %all-gather.25.cloned.1.call-start = ((), (), s32[]{:S(2)}) async-start(), calls=%async_computation.22 | async-start | bytes 3538944 | tf_op jit(solution)/shard_map/while/body/eval_jaxpr/all_gather | solution.py:415
  400.0 89.2 %collective-permute-start = (bf16[128,768]{1,0:T(8,128)(2,1)}, bf16[128,768]{1,0:T(8,128)(2,1)S(1)}, u32[]{:S(2)}, u32[]{:S(2)}) collective-permute-start(bf16[128,768]{1,0:T(8,128)(2,1)} %get-tuple-element.2961), channel_id=1, source_target_pairs={{0,8},{8,16},{16,24},{1,9},{9,17},{17,25},{2,10},{10,18},{18,26},{... | collective-permute-start | bytes 589832 | tf_op jit(solution)/shard_map/while/body/eval_jaxpr/ppermute | solution.py:20
  489.2 48.2 %all-gather.25.cloned.1.call-start = ((), (), s32[]{:S(2)}) async-start(), calls=%async_computation.22 | async-start | bytes 3538944 | tf_op jit(solution)/shard_map/while/body/eval_jaxpr/all_gather | solution.py:415
  552.2 89.3 %collective-permute-start = (bf16[128,768]{1,0:T(8,128)(2,1)}, bf16[128,768]{1,0:T(8,128)(2,1)S(1)}, u32[]{:S(2)}, u32[]{:S(2)}) collective-permute-start(bf16[128,768]{1,0:T(8,128)(2,1)} %get-tuple-element.2961), channel_id=1, source_target_pairs={{0,8},{8,16},{16,24},{1,9},{9,17},{17,25},{2,10},{10,18},{18,26},{... | collective-permute-start | bytes 589832 | tf_op jit(solution)/shard_map/while/body/eval_jaxpr/ppermute | solution.py:20
  641.5 48.2 %all-gather.25.cloned.1.call-start = ((), (), s32[]{:S(2)}) async-start(), calls=%async_computation.22 | async-start | bytes 3538944 | tf_op jit(solution)/shard_map/while/body/eval_jaxpr/all_gather | solution.py:415
  704.6 89.1 %collective-permute-start = (bf16[128,768]{1,0:T(8,128)(2,1)}, bf16[128,768]{1,0:T(8,128)(2,1)S(1)}, u32[]{:S(2)}, u32[]{:S(2)}) collective-permute-start(bf16[128,768]{1,0:T(8,128)(2,1)} %get-tuple-element.2961), channel_id=1, source_target_pairs={{0,8},{8,16},{16,24},{1,9},{9,17},{17,25},{2,10},{10,18},{18,26},{... | collective-permute-start | bytes 589832 | tf_op jit(solution)/shard_map/while/body/eval_jaxpr/ppermute | solution.py:20
  793.8 48.2 %all-gather.25.cloned.1.call-start = ((), (), s32[]{:S(2)}) async-start(), calls=%async_computation.22 | async-start | bytes 3538944 | tf_op jit(solution)/shard_map/while/body/eval_jaxpr/all_gather | solution.py:415
  857.0 89.1 %collective-permute-start = (bf16[128,768]{1,0:T(8,128)(2,1)}, bf16[128,768]{1,0:T(8,128)(2,1)S(1)}, u32[]{:S(2)}, u32[]{:S(2)}) collective-permute-start(bf16[128,768]{1,0:T(8,128)(2,1)} %get-tuple-element.2961), channel_id=1, source_target_pairs={{0,8},{8,16},{16,24},{1,9},{9,17},{17,25},{2,10},{10,18},{18,26},{... | collective-permute-start | bytes 589832 | tf_op jit(solution)/shard_map/while/body/eval_jaxpr/ppermute | solution.py:20
  946.1 48.2 %all-gather.25.cloned.1.call-start = ((), (), s32[]{:S(2)}) async-start(), calls=%async_computation.22 | async-start | bytes 3538944 | tf_op jit(solution)/shard_map/while/body/eval_jaxpr/all_gather | solution.py:415
  1009.3 89.1 %collective-permute-start = (bf16[128,768]{1,0:T(8,128)(2,1)}, bf16[128,768]{1,0:T(8,128)(2,1)S(1)}, u32[]{:S(2)}, u32[]{:S(2)}) collective-permute-start(bf16[128,768]{1,0:T(8,128)(2,1)} %get-tuple-element.2961), channel_id=1, source_target_pairs={{0,8},{8,16},{16,24},{1,9},{9,17},{17,25},{2,10},{10,18},{18,26},{... | collective-permute-start | bytes 589832 | tf_op jit(solution)/shard_map/while/body/eval_jaxpr/ppermute | solution.py:20
  1098.4 48.2 %all-gather.25.cloned.1.call-start = ((), (), s32[]{:S(2)}) async-start(), calls=%async_computation.22 | async-start | bytes 3538944 | tf_op jit(solution)/shard_map/while/body/eval_jaxpr/all_gather | solution.py:415
  1161.6 89.0 %collective-permute-start = (bf16[128,768]{1,0:T(8,128)(2,1)}, bf16[128,768]{1,0:T(8,128)(2,1)S(1)}, u32[]{:S(2)}, u32[]{:S(2)}) collective-permute-start(bf16[128,768]{1,0:T(8,128)(2,1)} %get-tuple-element.2961), channel_id=1, source_target_pairs={{0,8},{8,16},{16,24},{1,9},{9,17},{17,25},{2,10},{10,18},{18,26},{... | collective-permute-start | bytes 589832 | tf_op jit(solution)/shard_map/while/body/eval_jaxpr/ppermute | solution.py:20
  1289.8 193.5 %reduce-scatter.29.cloned.1.call-start = ((), (), s32[]{:S(2)}) async-start(), calls=%async_computation.21 | async-start | bytes 7077888 | tf_op jit(solution)/shard_map/while/body/eval_jaxpr/reduce_scatter | solution.py:508
  1532.4 46.7 %all-gather.23.cloned.1.call-start = ((), (), s32[]{:S(2)}) async-start(), calls=%async_computation.20 | async-start | bytes 3538944 | tf_op jit(solution)/shard_map/while/body/eval_jaxpr/all_gather | solution.py:495
  1536.3 193.7 %reduce-scatter.29.cloned.1.call-start = ((), (), s32[]{:S(2)}) async-start(), calls=%async_computation.21 | async-start | bytes 7077888 | tf_op jit(solution)/shard_map/while/body/eval_jaxpr/reduce_scatter | solution.py:508
  1782.9 193.6 %reduce-scatter.29.cloned.1.call-start = ((), (), s32[]{:S(2)}) async-start(), calls=%async_computation.21 | async-start | bytes 7077888 | tf_op jit(solution)/shard_map/while/body/eval_jaxpr/reduce_scatter | solution.py:508
  2029.5 193.6 %reduce-scatter.29.cloned.1.call-start = ((), (), s32[]{:S(2)}) async-start(), calls=%async_computation.21 | async-start | bytes 7077888 | tf_op jit(solution)/shard_map/while/body/eval_jaxpr/reduce_scatter | solution.py:508
  2276.1 193.6 %reduce-scatter.29.cloned.1.call-start = ((), (), s32[]{:S(2)}) async-start(), calls=%async_computation.21 | async-start | bytes 7077888 | tf_op jit(solution)/shard_map/while/body/eval_jaxpr/reduce_scatter | solution.py:508
  2522.7 193.6 %reduce-scatter.29.cloned.1.call-start = ((), (), s32[]{:S(2)}) async-start(), calls=%async_computation.21 | async-start | bytes 7077888 | tf_op jit(solution)/shard_map/while/body/eval_jaxpr/reduce_scatter | solution.py:508
  2769.4 193.6 %reduce-scatter.29.cloned.1.call-start = ((), (), s32[]{:S(2)}) async-start(), calls=%async_computation.21 | async-start | bytes 7077888 | tf_op jit(solution)/shard_map/while/body/eval_jaxpr/reduce_scatter | solution.py:508
  3012.9 118.5 %reduce-scatter.15.cloned.1.call-start = ((), (), s32[]{:S(2)}) async-start(), calls=%async_computation.8 | async-start | bytes 7962624 | tf_op jit(solution)/shard_map/reduce_scatter | solution.py:544
  3013.4 218.1 %reduce-scatter.19.cloned.1.call-start = ((), (), s32[]{:S(2)}) async-start(), calls=%async_computation.10 | async-start | bytes 10616832 | tf_op jit(solution)/shard_map/reduce_scatter | solution.py:546
  3014.2 317.6 %reduce-scatter.21.cloned.1.call-start = ((), (), s32[]{:S(2)}) async-start(), calls=%async_computation.11 | async-start | bytes 10616832 | tf_op jit(solution)/shard_map/reduce_scatter | solution.py:547
  3014.9 385.0 %reduce-scatter.23.cloned.1.call-start = ((), (), s32[]{:S(2)}) async-start(), calls=%async_computation.16 | async-start | bytes 442368
  3016.0 384.9 %reduce-scatter.25.cloned.1.call-start = ((), (), s32[]{:S(2)}) async-start(), calls=%async_computation.17 | async-start | bytes 442368
  3017.0 412.0 %reduce-scatter.27.cloned.1.call-start = ((), (), s32[]{:S(2)}) async-start(), calls=%async_computation.18 | async-start | bytes 1769472
  3018.8 509.5 %all-reduce.8.cloned.1.call-start = ((), (), s32[]{:S(2)}) async-start(), calls=%async_computation.19 | async-start | bytes 7077888 | tf_op jit(solution)/shard_map/psum | solution.py:572
  (270 other events, 4925.1 us)
Sparse Core Ops, SparseCore 0:
  37.7 40.5 all-gather.14
  80.5 50.1 all-gather.16
  132.7 50.5 all-gather.18
  192.7 40.3 all-gather.24
  342.8 42.4 all-gather.24
  494.9 42.4 all-gather.24
  647.2 42.4 all-gather.24
  799.6 42.4 all-gather.24
  951.9 42.4 all-gather.24
  1104.2 42.4 all-gather.24
  1290.0 42.4 all-gather.22
  1338.4 144.8 reduce-scatter.28
  1536.4 42.6 all-gather.22
  1585.0 144.8 reduce-scatter.28
  1783.0 42.6 all-gather.22
  1831.7 144.8 reduce-scatter.28
  2029.6 42.6 all-gather.22
  2078.3 144.8 reduce-scatter.28
  2276.2 42.6 all-gather.22
  2324.9 144.8 reduce-scatter.28
  2522.9 42.6 all-gather.22
  2571.5 144.8 reduce-scatter.28
  2769.5 42.6 all-gather.22
  2818.1 144.8 reduce-scatter.28
  3015.7 35.9 reduce-scatter.16
  3053.8 77.4 reduce-scatter.14
  3133.7 97.8 reduce-scatter.18
  3233.9 97.8 reduce-scatter.20
  3334.4 28.2 reduce-scatter.22
  3365.1 28.8 reduce-scatter.24
  3396.9 32.0 reduce-scatter.26
  3432.9 95.3 all-reduce.7
  (1 shorter events, 25.1 us)
where the time goes:
time: 3570 us; the launch traced here: 3540 us
  waiting for transfers between devices  2730 us (76%)
  local copies, waits for them, and re-layouts  251 us (7%)
  matrix products  250 us (7%)
  blocking collectives  127 us (4%)
  other arithmetic  112 us (3%)
    reduce_scatter x7, waiting for transfers between devices, backward_tick(): lax.psum_scatter(middle[3], 'seq', scatter_dimension=0, tiled=True)  1010 us
    ppermute x14, waiting for transfers between devices, passed_along(): lax.ppermute(value, axis, [(source, source + steps) for source in range(i...  625 us
    all_gather x7, waiting for transfers between devices, backward_tick(): all_keys = lax.all_gather(projected[:, D:], 'seq', axis=0, tiled=True)  292 us
    all_gather x7, waiting for transfers between devices, forward_tick(): whole_keys = lax.all_gather(projected[:, D:], 'seq', axis=0, tiled=True)  269 us
    reduce_scatter x1, waiting for transfers between devices, body(): lax.psum_scatter(grad_sums[2], 'seq', scatter_dimension=0, tiled=True)  98.9 us
    reduce_scatter x1, waiting for transfers between devices, body(): lax.psum_scatter(grad_sums[3], 'seq', scatter_dimension=0, tiled=True)  98.8 us
    psum x1, waiting for transfers between devices, body(): lax.psum(placed[0].astype(jnp.bfloat16), 'section').astype(jnp.float32)  87.6 us
    reduce_scatter x1, waiting for transfers between devices, body(): lax.psum_scatter(grad_sums[0], 'seq', scatter_dimension=0, tiled=True)  78.7 us
  transfers between devices with their start and end apart: 47, of which 44 were waited for; matrix products, arithmetic and copies ran while one was open for 2% of the time, Pallas kernels for 0%

commit v1 on v0

--- a/solution.py
+++ b/solution.py
@@ -1,6 +1,8 @@
 import jax
 import jax.numpy as jnp
 from jax import lax
+from jax.experimental import pallas as pl
+from jax.experimental.pallas import tpu as pltpu
 from jax.sharding import PartitionSpec as P
 
 D = 768
@@ -602,9 +604,966 @@
     )
 
 
+BF16 = jnp.bfloat16
+F32 = jnp.float32
+PAIRS = HEADS // 2
+OWNERS = (0, 2, 3, 4, 5, 6)
+TOKENS = 128
+PAIR_LANES = 128
+QUERY_STEP = 256
+MODEL_ROWS = 9
+VEC_ROWS = 16
+VMEM_BYTES = 60 * 1024 * 1024
+SCALE = HEAD_DIM ** (-0.5)
+
+
+def mul(left, right):
+    return lax.dot_general(left, right, (((1,), (0,)), ((), ())), preferred_element_type=F32)
+
+
+def mul_nt(left, right):
+    return lax.dot_general(left, right, (((1,), (1,)), ((), ())), preferred_element_type=F32)
+
+
+def mul_tn(left, right):
+    return lax.dot_general(left, right, (((0,), (0,)), ((), ())), preferred_element_type=F32)
+
+
+def standardize(values):
+    center = values - jnp.mean(values, -1, keepdims=True)
+    rstd = lax.rsqrt(jnp.mean(center * center, -1, keepdims=True) + EPSILON)
+    return (center * rstd, rstd)
+
+
+def norm_back(unit, rstd, unit_grad):
+    first = jnp.mean(unit_grad, -1, keepdims=True)
+    second = jnp.mean(unit_grad * unit, -1, keepdims=True)
+    return rstd * (unit_grad - first - unit * second)
+
+
+def remote(source, target, send_sem, recv_sem, axis, peer):
+    return pltpu.make_async_remote_copy(
+        src_ref=source,
+        dst_ref=target,
+        send_sem=send_sem,
+        recv_sem=recv_sem,
+        device_id={axis: peer},
+        device_id_type=pl.DeviceIdType.MESH,
+    )
+
+
+def greet(axis, peers):
+    barrier = pltpu.get_barrier_semaphore()
+    for peer in peers:
+        pl.semaphore_signal(
+            barrier, inc=1, device_id={axis: peer}, device_id_type=pl.DeviceIdType.MESH
+        )
+    pl.semaphore_wait(barrier, len(peers))
+
+
+def seq_peers(me, count):
+    return [lax.rem(me + step, count) for step in range(1, count)]
+
+
+def plane_peers(me):
+    return [
+        me,
+        me + 1 - 2 * lax.rem(me, 2),
+        lax.rem(me + 2, 4),
+        3 - me,
+    ]
+
+
+def rows_of(block, size=TOKENS):
+    return pl.ds(pl.multiple_of(block * size, size), size)
+
+
+def attention_forward_kernel(
+    x_ref,
+    w_ref,
+    vec_ref,
+    u_ref,
+    out_ref,
+    qkv_ref,
+    att_ref,
+    pair_att_ref,
+    pair_total_ref,
+    log_ref,
+    send,
+    att_send,
+    att_recv,
+    send_sem,
+    recv_sem,
+    att_send_sem,
+    att_recv_sem,
+):
+    me = lax.axis_index("seq")
+    count = 8
+    greet("seq", seq_peers(me, count))
+    inputs = x_ref[...].astype(F32)
+    unit, unused = standardize(inputs)
+    hidden = (unit * vec_ref[0:1, :] + vec_ref[3:4, :]).astype(BF16)
+    for block in range(3):
+        part = mul(hidden, w_ref[:, block * D : (block + 1) * D])
+        if block == 2:
+            part = part + vec_ref[6:7, :]
+        part = part.astype(BF16)
+        for pair in range(PAIRS):
+            send[pair, :, block * PAIR_LANES : (block + 1) * PAIR_LANES] = part[
+                :, pair * PAIR_LANES : (pair + 1) * PAIR_LANES
+            ]
+
+    def out_copy(pair):
+        return remote(
+            send.at[pair],
+            qkv_ref.at[rows_of(me)],
+            send_sem.at[pair],
+            recv_sem.at[me],
+            "seq",
+            OWNERS[pair],
+        )
+
+    for pair, owner in enumerate(OWNERS):
+
+        @pl.when(me != owner)
+        def _():
+            out_copy(pair).start()
+
+        @pl.when(me == owner)
+        def _():
+            qkv_ref[rows_of(me), :] = send[pair]
+
+    is_owner = (me != 1) & (me != 7)
+    my_pair = jnp.where(me == 0, 0, me - 1)
+    my_pair = jnp.where(my_pair > PAIRS - 1, PAIRS - 1, my_pair)
+    log_ref[...] = jnp.zeros_like(log_ref)
+
+    def back_copy(target):
+        return remote(
+            att_send.at[pl.ds(target * TOKENS, TOKENS)],
+            att_recv.at[my_pair],
+            att_send_sem.at[target],
+            att_recv_sem.at[my_pair],
+            "seq",
+            target,
+        )
+
+    @pl.when(is_owner)
+    def _():
+        lane = lax.broadcasted_iota(jnp.int32, (QUERY_STEP, PAIR_LANES), 1)
+        first_half = lane < HEAD_DIM
+        for step in range(count * TOKENS // QUERY_STEP):
+            for source in (2 * step, 2 * step + 1):
+
+                @pl.when(me != source)
+                def _():
+                    remote(
+                        send.at[0],
+                        qkv_ref.at[pl.ds(source * TOKENS, TOKENS)],
+                        send_sem.at[0],
+                        recv_sem.at[source],
+                        "seq",
+                        source,
+                    ).wait_recv()
+
+            start = step * QUERY_STEP
+            keys_end = start + QUERY_STEP
+            rows = slice(start, keys_end)
+            query = qkv_ref[rows, 0:PAIR_LANES] * jnp.asarray(SCALE, BF16)
+            keys = qkv_ref[0:keys_end, PAIR_LANES : 2 * PAIR_LANES]
+            values = qkv_ref[0:keys_end, 2 * PAIR_LANES : 3 * PAIR_LANES]
+            causal = lax.broadcasted_iota(jnp.int32, (QUERY_STEP, keys_end), 1) <= (
+                start + lax.broadcasted_iota(jnp.int32, (QUERY_STEP, keys_end), 0)
+            )
+            sums = []
+            totals = []
+            logs = jnp.zeros((1, PAIR_LANES), F32)
+            for head in range(2):
+                mine = first_half if head == 0 else ~first_half
+                own_query = jnp.where(mine, query, jnp.zeros_like(query))
+                scores = mul_nt(own_query, keys)
+                raised = jnp.where(causal, jnp.exp(scores), 0.0)
+                pick_query = u_ref[head, rows, :]
+                pick_keys = u_ref[head, 0:keys_end, :]
+                counts = mul_nt(pick_query, pick_keys)
+                weighted = (raised * counts).astype(BF16)
+                sums.append(mul(weighted, values))
+                pattern = mul(raised.astype(BF16), pick_keys)
+                picked = pick_query.astype(F32)
+                totals.append(jnp.sum(pattern * picked, -1, keepdims=True))
+                chosen = picked > 0.5
+                logs = logs + jnp.sum(
+                    jnp.where(chosen, jnp.log(jnp.where(chosen, pattern, 1.0)), 0.0),
+                    0,
+                    keepdims=True,
+                )
+            log_ref[0:1, :] += logs
+            total = jnp.where(first_half, totals[0], totals[1])
+            attended = jnp.where(first_half, sums[0], sums[1]) / total
+            pair_att_ref[rows, :] = attended
+            pair_total_ref[rows, :] = total
+            att_send[rows, :] = attended.astype(BF16)
+            for target in (2 * step, 2 * step + 1):
+
+                @pl.when(me != target)
+                def _():
+                    back_copy(target).start()
+
+                @pl.when(me == target)
+                def _():
+                    att_recv[my_pair] = att_send[target * TOKENS : (target + 1) * TOKENS, :]
+
+    for pair, owner in enumerate(OWNERS):
+
+        @pl.when(me != owner)
+        def _():
+            remote(
+                att_send.at[pl.ds(0, TOKENS)],
+                att_recv.at[pair],
+                att_send_sem.at[0],
+                att_recv_sem.at[pair],
+                "seq",
+                owner,
+            ).wait_recv()
+
+        att_ref[:, pair * PAIR_LANES : (pair + 1) * PAIR_LANES] = att_recv[pair]
+    inner_unit, unused = standardize(att_ref[...].astype(F32))
+    inner = (inner_unit * vec_ref[1:2, :] + vec_ref[4:5, :]).astype(BF16)
+    branch = mul(inner, w_ref[:, 3 * D : 4 * D]) + vec_ref[7:8, :]
+    out_ref[...] = (inputs + branch).astype(BF16)
+    for pair, owner in enumerate(OWNERS):
+
+        @pl.when(me != owner)
+        def _():
+            out_copy(pair).wait_send()
+
+    @pl.when(is_owner)
+    def _():
+        for target in range(count):
+
+            @pl.when(me != target)
+            def _():
+                back_copy(target).wait_send()
+
+
+def attention_backward_kernel(
+    g_ref,
+    x_ref,
+    att_ref,
+    w_ref,
+    vec_ref,
+    u_ref,
+    qkv_ref,
+    pair_att_ref,
+    pair_total_ref,
+    gx_ref,
+    grad_ref,
+    do_send,
+    do_recv,
+    key_sum,
+    value_sum,
+    d_send,
+    d_recv,
+    d_proj,
+    vec_rows,
+    send_sem,
+    recv_sem,
+    back_send_sem,
+    back_recv_sem,
+):
+    me = lax.axis_index("seq")
+    count = 8
+    greet("seq", seq_peers(me, count))
+    grad = g_ref[...]
+    inner_unit, inner_rstd = standardize(att_ref[...].astype(F32))
+    inner_grad = mul_nt(grad, w_ref[:, 3 * D : 4 * D])
+    att_grad = norm_back(inner_unit, inner_rstd, inner_grad * vec_ref[1:2, :]).astype(BF16)
+    for pair in range(PAIRS):
+        do_send[pair] = att_grad[:, pair * PAIR_LANES : (pair + 1) * PAIR_LANES]
+
+    def out_copy(pair):
+        return remote(
+            do_send.at[pair],
+            do_recv.at[rows_of(me)],
+            send_sem.at[pair],
+            recv_sem.at[me],
+            "seq",
+            OWNERS[pair],
+        )
+
+    for pair, owner in enumerate(OWNERS):
+
+        @pl.when(me != owner)
+        def _():
+            out_copy(pair).start()
+
+        @pl.when(me == owner)
+        def _():
+            do_recv[rows_of(me), :] = do_send[pair]
+
+    vec_rows[...] = jnp.zeros_like(vec_rows)
+    vec_rows[1:2, :] = jnp.sum(inner_grad * inner_unit, 0, keepdims=True)
+    vec_rows[4:5, :] = jnp.sum(inner_grad, 0, keepdims=True)
+    vec_rows[7:8, :] = jnp.sum(grad.astype(F32), 0, keepdims=True)
+    inner = (inner_unit * vec_ref[1:2, :] + vec_ref[4:5, :]).astype(BF16)
+    grad_ref[:, 3 * D : 4 * D] = mul_tn(inner, grad).astype(BF16)
+
+    is_owner = (me != 1) & (me != 7)
+    my_pair = jnp.where(me == 0, 0, me - 1)
+    my_pair = jnp.where(my_pair > PAIRS - 1, PAIRS - 1, my_pair)
+
+    def back_copy(target):
+        return remote(
+            d_send.at[pl.ds(target * TOKENS, TOKENS)],
+            d_recv.at[my_pair],
+            back_send_sem.at[target],
+            back_recv_sem.at[my_pair],
+            "seq",
+            target,
+        )
+
+    @pl.when(is_owner)
+    def _():
+        for source in range(count):
+
+            @pl.when(me != source)
+            def _():
+                remote(
+                    do_send.at[0],
+                    do_recv.at[pl.ds(source * TOKENS, TOKENS)],
+                    send_sem.at[0],
+                    recv_sem.at[source],
+                    "seq",
+                    source,
+                ).wait_recv()
+
+        key_sum[...] = jnp.zeros_like(key_sum)
+        value_sum[...] = jnp.zeros_like(value_sum)
+        lane = lax.broadcasted_iota(jnp.int32, (QUERY_STEP, PAIR_LANES), 1)
+        first_half = lane < HEAD_DIM
+        for step in reversed(range(count * TOKENS // QUERY_STEP)):
+            start = step * QUERY_STEP
+            keys_end = start + QUERY_STEP
+            rows = slice(start, keys_end)
+            plain_query = qkv_ref[rows, 0:PAIR_LANES]
+            query = plain_query * jnp.asarray(SCALE, BF16)
+            keys = qkv_ref[0:keys_end, PAIR_LANES : 2 * PAIR_LANES]
+            values = qkv_ref[0:keys_end, 2 * PAIR_LANES : 3 * PAIR_LANES]
+            causal = lax.broadcasted_iota(jnp.int32, (QUERY_STEP, keys_end), 1) <= (
+                start + lax.broadcasted_iota(jnp.int32, (QUERY_STEP, keys_end), 0)
+            )
+            head_grad = do_recv[rows, :]
+            inverse = 1.0 / pair_total_ref[rows, :]
+            head_float = head_grad.astype(F32)
+            products = head_float * pair_att_ref[rows, :]
+            scaled = (head_float * inverse).astype(BF16)
+            key_lanes = lax.broadcasted_iota(jnp.int32, (keys_end, PAIR_LANES), 1) < HEAD_DIM
+            query_parts = []
+            key_parts = []
+            value_parts = []
+            for head in range(2):
+                mine = first_half if head == 0 else ~first_half
+                own_query = jnp.where(mine, query, jnp.zeros_like(query))
+                own_grad = jnp.where(mine, head_grad, jnp.zeros_like(head_grad))
+                delta = jnp.sum(jnp.where(mine, products, 0.0), -1, keepdims=True)
+                own_inverse = jnp.max(jnp.where(mine, inverse, 0.0), -1, keepdims=True)
+                counts = mul_nt(u_ref[head, rows, :], u_ref[head, 0:keys_end, :])
+                scores = mul_nt(own_query, keys)
+                weighted = jnp.where(causal, jnp.exp(scores) * counts, 0.0)
+                prob_grad = mul_nt(own_grad, values)
+                score_grad = (weighted * own_inverse * (prob_grad - delta)).astype(BF16)
+                query_parts.append(mul(score_grad, keys))
+                key_parts.append(mul_tn(score_grad, plain_query))
+                value_parts.append(mul_tn(weighted.astype(BF16), scaled))
+            key_sum[0:keys_end, :] += jnp.where(key_lanes, key_parts[0], key_parts[1])
+            value_sum[0:keys_end, :] += jnp.where(key_lanes, value_parts[0], value_parts[1])
+            query_grad = jnp.where(first_half, query_parts[0], query_parts[1]) * SCALE
+            d_send[rows, 0:PAIR_LANES] = query_grad.astype(BF16)
+            d_send[rows, PAIR_LANES : 2 * PAIR_LANES] = (key_sum[rows, :] * SCALE).astype(BF16)
+            d_send[rows, 2 * PAIR_LANES : 3 * PAIR_LANES] = value_sum[rows, :].astype(BF16)
+            for target in (2 * step, 2 * step + 1):
+
+                @pl.when(me != target)
+                def _():
+                    back_copy(target).start()
+
+                @pl.when(me == target)
+                def _():
+                    d_recv[my_pair] = d_send[target * TOKENS : (target + 1) * TOKENS, :]
+
+    unit, rstd = standardize(x_ref[...].astype(F32))
+    hidden = (unit * vec_ref[0:1, :] + vec_ref[3:4, :]).astype(BF16)
+    for pair, owner in enumerate(OWNERS):
+
+        @pl.when(me != owner)
+        def _():
+            remote(
+                d_send.at[pl.ds(0, TOKENS)],
+                d_recv.at[pair],
+                back_send_sem.at[0],
+                back_recv_sem.at[pair],
+                "seq",
+                owner,
+            ).wait_recv()
+
+        for block in range(3):
+            d_proj[:, block * D + pair * PAIR_LANES : block * D + (pair + 1) * PAIR_LANES] = d_recv[
+                pair, :, block * PAIR_LANES : (block + 1) * PAIR_LANES
+            ]
+    hidden_grad = mul_nt(d_proj[...], w_ref[:, 0 : 3 * D])
+    input_grad = norm_back(unit, rstd, hidden_grad * vec_ref[0:1, :])
+    gx_ref[...] = (grad.astype(F32) + input_grad).astype(BF16)
+    vec_rows[0:1, :] = jnp.sum(hidden_grad * unit, 0, keepdims=True)
+    vec_rows[3:4, :] = jnp.sum(hidden_grad, 0, keepdims=True)
+    vec_rows[6:7, :] = jnp.sum(d_proj[:, 2 * D : 3 * D].astype(F32), 0, keepdims=True)
+    for block in range(3):
+        grad_ref[:, block * D : (block + 1) * D] = mul_tn(
+            hidden, d_proj[:, block * D : (block + 1) * D]
+        ).astype(BF16)
+    grad_ref[:, 4 * D : 4 * D + PAIR_LANES] = vec_rows[...].T.astype(BF16)
+    for pair, owner in enumerate(OWNERS):
+
+        @pl.when(me != owner)
+        def _():
+            out_copy(pair).wait_send()
+
+    @pl.when(is_owner)
+    def _():
+        for target in range(count):
+
+            @pl.when(me != target)
+            def _():
+                back_copy(target).wait_send()
+
+
+def gelu_parts(values):
+    below = 0.5 * (1.0 + lax.erf(values * (0.5**0.5)))
+    return (values * below, below)
+
+
+def share_stats(columns, send, recv, send_sem, recv_sem, peers):
+    send[...] = columns.T[0:8, :]
+    recv[0] = send[...]
+    copies = [
+        remote(send, recv.at[k], send_sem.at[k], recv_sem.at[k], "section", peers[k])
+        for k in range(1, 4)
+    ]
+    for copy in copies:
+        copy.start()
+    return copies
+
+
+def two_columns(first, second):
+    lane = lax.broadcasted_iota(jnp.int32, (first.shape[0], PAIR_LANES), 1)
+    return jnp.where(lane == 0, first, jnp.where(lane == 1, second, 0.0))
+
+
+def slot_rows(k):
+    return slice(k * TOKENS, (k + 1) * TOKENS)
+
+
+def feed_forward_kernel(
+    x_ref,
+    w_ref,
+    vec_ref,
+    out_ref,
+    hid_ref,
+    up_ref,
+    stat_ref,
+    active,
+    columns,
+    stat_rows,
+    part_send,
+    part_recv,
+    stat_send,
+    stat_recv,
+    hid_send_sem,
+    hid_recv_sem,
+    stat_send_sem,
+    stat_recv_sem,
+    part_send_sem,
+    part_recv_sem,
+):
+    me = lax.axis_index("section")
+    peers = plane_peers(me)
+    greet("section", peers[1:])
+    inputs = x_ref[...].astype(F32)
+    unit, unused = standardize(inputs)
+    hid_ref[slot_rows(0), :] = (unit * vec_ref[2:3, :] + vec_ref[5:6, :]).astype(BF16)
+    hidden_copies = [
+        remote(
+            hid_ref.at[pl.ds(0, TOKENS)],
+            hid_ref.at[pl.ds(k * TOKENS, TOKENS)],
+            hid_send_sem.at[k],
+            hid_recv_sem.at[k],
+            "section",
+            peers[k],
+        )
+        for k in range(1, 4)
+    ]
+    for copy in hidden_copies:
+        copy.start()
+    for k in range(4):
+        if k > 0:
+            hidden_copies[k - 1].wait_recv()
+        upward = mul(hid_ref[slot_rows(k), :], w_ref[:, 0:D]) + vec_ref[10:11, :]
+        up_ref[slot_rows(k), :] = upward
+        values, unused = gelu_parts(upward)
+        active[slot_rows(k), :] = values
+        mean = jnp.mean(values, -1, keepdims=True)
+        center = values - mean
+        columns[slot_rows(k), :] = two_columns(mean, jnp.sum(center * center, -1, keepdims=True))
+    stat_copies = share_stats(
+        columns[...], stat_send, stat_recv, stat_send_sem, stat_recv_sem, peers
+    )
+    for copy in stat_copies:
+        copy.wait_recv()
+    stat_rows[...] = jnp.zeros_like(stat_rows)
+    for k in range(4):
+        means = [stat_recv[source, 0:1, slot_rows(k ^ source)] for source in range(4)]
+        squares = [stat_recv[source, 1:2, slot_rows(k ^ source)] for source in range(4)]
+        mean = (means[0] + means[1] + means[2] + means[3]) * 0.25
+        spread = squares[0] + squares[1] + squares[2] + squares[3]
+        for each in means:
+            spread = spread + D * (each - mean) * (each - mean)
+        stat_rows[0:1, slot_rows(k)] = mean
+        stat_rows[1:2, slot_rows(k)] = lax.rsqrt(spread * (1.0 / FF) + EPSILON)
+    stat_ref[...] = stat_rows[...].T
+    branch = None
+    part_copies = []
+    for k in (1, 2, 3, 0):
+        both = stat_ref[slot_rows(k), :]
+        inner = (
+            (active[slot_rows(k), :] - both[:, 0:1]) * both[:, 1:2] * vec_ref[9:10, :]
+            + vec_ref[11:12, :]
+        ).astype(BF16)
+        part = mul(inner, w_ref[:, D : 2 * D])
+        if k == 0:
+            branch = part
+        else:
+            part_send[k] = part.astype(BF16)
+            part_copies.append(
+                remote(
+                    part_send.at[k],
+                    part_recv.at[k],
+                    part_send_sem.at[k],
+                    part_recv_sem.at[k],
+                    "section",
+                    peers[k],
+                )
+            )
+            part_copies[-1].start()
+    for k in range(1, 4):
+        part_copies[k - 1].wait_recv()
+        branch = branch + part_recv[k].astype(F32)
+    out_ref[...] = (inputs + branch + vec_ref[8:9, :]).astype(BF16)
+    for copy in hidden_copies + stat_copies + part_copies:
+        copy.wait_send()
+
+
+def feed_backward_kernel(
+    g_ref,
+    x_ref,
+    hid_ref,
+    up_ref,
+    stat_ref,
+    w_ref,
+    vec_ref,
+    gx_ref,
+    grad_ref,
+    grads,
+    units,
+    slopes,
+    unit_grads,
+    inners,
+    lows,
+    columns,
+    stat_rows,
+    part_send,
+    part_recv,
+    stat_send,
+    stat_recv,
+    vec_rows,
+    g_send_sem,
+    g_recv_sem,
+    stat_send_sem,
+    stat_recv_sem,
+    part_send_sem,
+    part_recv_sem,
+):
+    me = lax.axis_index("section")
+    peers = plane_peers(me)
+    greet("section", peers[1:])
+    grads[slot_rows(0), :] = g_ref[...]
+    grad_copies = [
+        remote(
+            grads.at[pl.ds(0, TOKENS)],
+            grads.at[pl.ds(k * TOKENS, TOKENS)],
+            g_send_sem.at[k],
+            g_recv_sem.at[k],
+            "section",
+            peers[k],
+        )
+        for k in range(1, 4)
+    ]
+    for copy in grad_copies:
+        copy.start()
+    gain_sum = jnp.zeros((1, D), F32)
+    bias_sum = jnp.zeros((1, D), F32)
+    for k in range(4):
+        both = stat_ref[slot_rows(k), :]
+        upward = up_ref[slot_rows(k), :]
+        values, below = gelu_parts(upward)
+        slopes[slot_rows(k), :] = below + upward * (
+            jnp.exp(-0.5 * upward * upward) * (0.5 / 3.141592653589793) ** 0.5
+        )
+        unit = (values - both[:, 0:1]) * both[:, 1:2]
+        units[slot_rows(k), :] = unit
+        inners[slot_rows(k), :] = (unit * vec_ref[9:10, :] + vec_ref[11:12, :]).astype(BF16)
+        if k > 0:
+            grad_copies[k - 1].wait_recv()
+        inner_grad = mul_nt(grads[slot_rows(k), :], w_ref[:, D : 2 * D])
+        gain_sum = gain_sum + jnp.sum(inner_grad * unit, 0, keepdims=True)
+        bias_sum = bias_sum + jnp.sum(inner_grad, 0, keepdims=True)
+        unit_grad = inner_grad * vec_ref[9:10, :]
+        unit_grads[slot_rows(k), :] = unit_grad
+        columns[slot_rows(k), :] = two_columns(
+            jnp.sum(unit_grad, -1, keepdims=True), jnp.sum(unit_grad * unit, -1, keepdims=True)
+        )
+    stat_copies = share_stats(
+        columns[...], stat_send, stat_recv, stat_send_sem, stat_recv_sem, peers
+    )
+    vec_rows[...] = jnp.zeros_like(vec_rows)
+    vec_rows[9:10, :] = gain_sum
+    vec_rows[11:12, :] = bias_sum
+    grad_ref[:, D : 2 * D] = mul_tn(inners[...], grads[...]).astype(BF16)
+    for copy in stat_copies:
+        copy.wait_recv()
+    stat_rows[...] = jnp.zeros_like(stat_rows)
+    for k in range(4):
+        for line in range(2):
+            parts = [stat_recv[source, line : line + 1, slot_rows(k ^ source)] for source in range(4)]
+            stat_rows[line : line + 1, slot_rows(k)] = (
+                parts[0] + parts[1] + parts[2] + parts[3]
+            ) * (1.0 / FF)
+    columns[...] = stat_rows[...].T
+    hidden_grad = None
+    low_sum = jnp.zeros((1, D), F32)
+    part_copies = []
+    for k in (1, 2, 3, 0):
+        rstd = stat_ref[slot_rows(k), :][:, 1:2]
+        both = columns[slot_rows(k), :]
+        low = (
+            rstd
+            * (unit_grads[slot_rows(k), :] - both[:, 0:1] - units[slot_rows(k), :] * both[:, 1:2])
+            * slopes[slot_rows(k), :]
+        ).astype(BF16)
+        lows[slot_rows(k), :] = low
+        low_sum = low_sum + jnp.sum(low.astype(F32), 0, keepdims=True)
+        part = mul_nt(low, w_ref[:, 0:D])
+        if k == 0:
+            hidden_grad = part
+        else:
+            part_send[k] = part.astype(BF16)
+            part_copies.append(
+                remote(
+                    part_send.at[k],
+                    part_recv.at[k],
+                    part_send_sem.at[k],
+                    part_recv_sem.at[k],
+                    "section",
+                    peers[k],
+                )
+            )
+            part_copies[-1].start()
+    vec_rows[10:11, :] = low_sum
+    grad_ref[:, 0:D] = mul_tn(hid_ref[...], lows[...]).astype(BF16)
+    unit, rstd = standardize(x_ref[...].astype(F32))
+    for k in range(1, 4):
+        part_copies[k - 1].wait_recv()
+        hidden_grad = hidden_grad + part_recv[k].astype(F32)
+    grad = g_ref[...].astype(F32)
+    gx_ref[...] = (grad + norm_back(unit, rstd, hidden_grad * vec_ref[2:3, :])).astype(BF16)
+    vec_rows[2:3, :] = jnp.sum(hidden_grad * unit, 0, keepdims=True)
+    vec_rows[5:6, :] = jnp.sum(hidden_grad, 0, keepdims=True)
+    vec_rows[8:9, :] = jnp.sum(grad, 0, keepdims=True)
+    grad_ref[:, 2 * D : 2 * D + PAIR_LANES] = vec_rows[...].T.astype(BF16)
+    for copy in grad_copies + stat_copies + part_copies:
+        copy.wait_send()
+
+
+def shaped(shape, kind):
+    return jax.ShapeDtypeStruct(shape, kind)
+
+
+def call_kernel(kernel, name, number, outs, scratch, args, flops):
+    vmem = pl.BlockSpec(memory_space=pltpu.VMEM)
+    return pl.pallas_call(
+        kernel,
+        name=name,
+        out_shape=outs,
+        in_specs=[vmem] * len(args),
+        out_specs=[vmem] * len(outs),
+        scratch_shapes=scratch,
+        compiler_params=pltpu.CompilerParams(
+            collective_id=number, has_side_effects=True, vmem_limit_bytes=VMEM_BYTES
+        ),
+        cost_estimate=pl.CostEstimate(flops=flops, bytes_accessed=60_000_000, transcendentals=0),
+    )(*args)
+
+
+def run_attention(number, x, w, vec, picks):
+    dma = pltpu.SemaphoreType.DMA
+    group = 8 * TOKENS
+    return call_kernel(
+        attention_forward_kernel,
+        "attention_forward",
+        number,
+        [
+            shaped((TOKENS, D), BF16),
+            shaped((group, 3 * PAIR_LANES), BF16),
+            shaped((TOKENS, D), BF16),
+            shaped((group, PAIR_LANES), F32),
+            shaped((group, PAIR_LANES), F32),
+            shaped((8, PAIR_LANES), F32),
+        ],
+        [
+            pltpu.VMEM((PAIRS, TOKENS, 3 * PAIR_LANES), BF16),
+            pltpu.VMEM((group, PAIR_LANES), BF16),
+            pltpu.VMEM((PAIRS, TOKENS, PAIR_LANES), BF16),
+            dma((PAIRS,)),
+            dma((8,)),
+            dma((8,)),
+            dma((PAIRS,)),
+        ],
+        (x, w, vec, picks),
+        10**9,
+    )
+
+
+def run_attention_back(number, grad, x, att, w, vec, picks, qkv, pair_att, pair_total):
+    dma = pltpu.SemaphoreType.DMA
+    group = 8 * TOKENS
+    return call_kernel(
+        attention_backward_kernel,
+        "attention_backward",
+        number,
+        [shaped((TOKENS, D), BF16), shaped((D, 4 * D + PAIR_LANES), BF16)],
+        [
+            pltpu.VMEM((PAIRS, TOKENS, PAIR_LANES), BF16),
+            pltpu.VMEM((group, PAIR_LANES), BF16),
+            pltpu.VMEM((group, PAIR_LANES), F32),
+            pltpu.VMEM((group, PAIR_LANES), F32),
+            pltpu.VMEM((group, 3 * PAIR_LANES), BF16),
+            pltpu.VMEM((PAIRS, TOKENS, 3 * PAIR_LANES), BF16),
+            pltpu.VMEM((TOKENS, 3 * D), BF16),
+            pltpu.VMEM((PAIR_LANES, D), F32),
+            dma((PAIRS,)),
+            dma((8,)),
+            dma((8,)),
+            dma((PAIRS,)),
+        ],
+        (grad, x, att, w, vec, picks, qkv, pair_att, pair_total),
+        2 * 10**9,
+    )
+
+
+def run_feed(number, x, w, vec):
+    dma = pltpu.SemaphoreType.DMA
+    wide = 4 * TOKENS
+    return call_kernel(
+        feed_forward_kernel,
+        "feed_forward",
+        number,
+        [
+            shaped((TOKENS, D), BF16),
+            shaped((wide, D), BF16),
+            shaped((wide, D), F32),
+            shaped((wide, PAIR_LANES), F32),
+        ],
+        [
+            pltpu.VMEM((wide, D), F32),
+            pltpu.VMEM((wide, PAIR_LANES), F32),
+            pltpu.VMEM((PAIR_LANES, wide), F32),
+            pltpu.VMEM((4, TOKENS, D), BF16),
+            pltpu.VMEM((4, TOKENS, D), BF16),
+            pltpu.VMEM((8, wide), F32),
+            pltpu.VMEM((4, 8, wide), F32),
+        ]
+        + [dma((4,))] * 6,
+        (x, w, vec),
+        10**9,
+    )
+
+
+def run_feed_back(number, grad, x, hid, upward, stat, w, vec):
+    dma = pltpu.SemaphoreType.DMA
+    wide = 4 * TOKENS
+    return call_kernel(
+        feed_backward_kernel,
+        "feed_backward",
+        number,
+        [shaped((TOKENS, D), BF16), shaped((D, 2 * D + PAIR_LANES), BF16)],
+        [
+            pltpu.VMEM((wide, D), BF16),
+            pltpu.VMEM((wide, D), F32),
+            pltpu.VMEM((wide, D), F32),
+            pltpu.VMEM((wide, D), F32),
+            pltpu.VMEM((wide, D), BF16),
+            pltpu.VMEM((wide, D), BF16),
+            pltpu.VMEM((wide, PAIR_LANES), F32),
+            pltpu.VMEM((PAIR_LANES, wide), F32),
+            pltpu.VMEM((4, TOKENS, D), BF16),
+            pltpu.VMEM((4, TOKENS, D), BF16),
+            pltpu.VMEM((8, wide), F32),
+            pltpu.VMEM((4, 8, wide), F32),
+            pltpu.VMEM((PAIR_LANES, D), F32),
+        ]
+        + [dma((4,))] * 6,
+        (grad, x, hid, upward, stat, w, vec),
+        2 * 10**9,
+    )
+
+
+def pattern_picks(lengths, my_pair):
+    tokens = jnp.arange(8 * TOKENS, dtype=jnp.int32)
+    row_ids, pos = place_rows(lengths, tokens)
+    lane = jnp.arange(PAIR_LANES, dtype=jnp.int32)
+    number, row = (lane // 4, lane % 4)
+    ratio = jnp.where(number < 5, jnp.array(RATIOS + (1, 1, 1), jnp.int32)[jnp.minimum(number, 7)], 1)
+    heads = 2 * my_pair + jnp.arange(2, dtype=jnp.int32)
+    same = (row_ids[:, None] == row[None, :]) & (number < 5)[None, :]
+    fits = (pos[:, None] % ratio[None, :])[None] == (heads[:, None] % ratio[None, :])[:, None, :]
+    return (same[None] & fits).astype(BF16)
+
+
+def quick_body(
+    embeds,
+    row_lengths,
+    qkv_weight,
+    out_weight,
+    up_weight,
+    down_weight,
+    model_gains,
+    model_biases,
+    hidden_gains,
+    hidden_biases,
+    cotangent,
+):
+    section = lax.axis_index("section")
+    seq = lax.axis_index("seq")
+    layers = qkv_weight.shape[0]
+    depth = qkv_weight.shape[1]
+    piece = FF // 4 // 8
+
+    def of_section(stacked, axis):
+        return lax.dynamic_index_in_dim(stacked, section, axis, False)
+
+    hidden_vecs = jnp.concatenate([hidden_gains[:, None], hidden_biases], 1)
+    hidden_vecs = of_section(hidden_vecs.reshape(layers, 3, 4, piece), 2)
+    small = jnp.concatenate(
+        [model_gains, model_biases, hidden_vecs, jnp.zeros((layers, 4, depth), BF16)], 1
+    )
+    small = lax.all_gather(small, "seq", axis=0, tiled=False)
+    vecs = jnp.transpose(small, (1, 2, 0, 3)).reshape(layers, VEC_ROWS, D).astype(F32)
+    attention_weights = []
+    feed_weights = []
+    for layer in range(layers):
+        rows = jnp.concatenate([qkv_weight[layer], out_weight[layer]], 1)
+        rows = of_section(rows.reshape(4, depth // 4, 4 * D), 0)
+        attention_weights.append(lax.all_gather(rows, ("seq", "section"), axis=0, tiled=True))
+        up_rows = of_section(up_weight[layer].reshape(depth, 8, 4, piece), 2).reshape(depth, D)
+        down_rows = of_section(down_weight[layer].reshape(4, piece, D), 0)
+        rows = jnp.concatenate([up_rows, down_rows], 1)
+        feed_weights.append(lax.all_gather(rows, "seq", axis=0, tiled=True))
+    is_owner = (seq != 1) & (seq != 7)
+    my_pair = jnp.clip(jnp.where(seq == 0, 0, seq - 1), 0, PAIRS - 1)
+    picks = pattern_picks(lax.dynamic_index_in_dim(row_lengths, section, 0, False), my_pair)
+    stream = lax.dynamic_index_in_dim(embeds, section, 0, False)
+    grad = lax.dynamic_index_in_dim(cotangent, section, 0, False)
+    outputs = []
+    kept = []
+    log_rows = []
+    for layer in range(layers):
+        vec = vecs[layer]
+        into_attention = stream
+        stream, qkv, att, pair_att, pair_total, logs = run_attention(
+            10 + layer, stream, attention_weights[layer], vec, picks
+        )
+        outputs.append(stream)
+        log_rows.append(logs[0])
+        into_feed = stream
+        stream, hid, upward, stat = run_feed(20 + layer, stream, feed_weights[layer], vec)
+        outputs.append(stream)
+        kept.append((into_attention, att, qkv, pair_att, pair_total, into_feed, hid, upward, stat))
+    sublayer_outputs = lax.all_to_all(jnp.stack(outputs), "section", 0, 0, tiled=True)
+    pick_rows = jnp.where(is_owner, jnp.sum(picks.astype(F32), (0, 1)), 0.0)
+    lines = jnp.stack(log_rows + [pick_rows])[:, :20].reshape(layers + 1, 5, 4).sum(-1)
+    lines = lax.psum(lines, ("section", "seq"))
+    pattern_means = lines[:layers] / lines[layers:]
+    grads = [None] * (2 * layers)
+    attention_shards = [None] * layers
+    feed_shards = [None] * layers
+    for layer in reversed(range(layers)):
+        vec = vecs[layer]
+        into_attention, att, qkv, pair_att, pair_total, into_feed, hid, upward, stat = kept[layer]
+        grad, step = run_feed_back(
+            30 + layer, grad, into_feed, hid, upward, stat, feed_weights[layer], vec
+        )
+        grads[2 * layer + 1] = grad
+        shard = lax.psum_scatter(step, "seq", scatter_dimension=0, tiled=True)
+        feed_shards[layer] = lax.all_gather(shard, "section", axis=0, tiled=False)
+        grad, step = run_attention_back(
+            40 + layer,
+            grad,
+            into_attention,
+            att,
+            attention_weights[layer],
+            vec,
+            picks,
+            qkv,
+            pair_att,
+            pair_total,
+        )
+        grads[2 * layer] = grad
+        shard = lax.psum_scatter(step, ("seq", "section"), scatter_dimension=0, tiled=True)
+        attention_shards[layer] = lax.all_gather(shard, "section", axis=0, tiled=True)
+    sublayer_grads = lax.all_to_all(jnp.stack(grads), "section", 0, 0, tiled=True)
+    attention_all = jnp.stack(attention_shards).astype(F32)
+    feed_all = jnp.stack(feed_shards).astype(F32)
+    qkv_grad = attention_all[:, :, : 3 * D]
+    out_grad = attention_all[:, :, 3 * D : 4 * D]
+    model_vecs = attention_all[:, :, 4 * D : 4 * D + MODEL_ROWS] + jnp.sum(
+        feed_all[:, :, :, 2 * D : 2 * D + MODEL_ROWS], 1
+    )
+    model_vecs = jnp.transpose(model_vecs, (0, 2, 1))
+    up_grad = feed_all[:, :, :, :D].reshape(layers, 4, depth, 8, piece)
+    up_grad = jnp.transpose(up_grad, (0, 2, 3, 1, 4)).reshape(layers, depth, FF)
+    down_grad = feed_all[:, :, :, D : 2 * D].reshape(layers, 4 * piece, D)
+    hidden_rows = feed_all[:, :, :, 2 * D + MODEL_ROWS : 2 * D + MODEL_ROWS + 3]
+    hidden_rows = jnp.transpose(hidden_rows, (0, 3, 1, 2)).reshape(layers, 3, 4 * piece)
+    return (
+        sublayer_outputs[None],
+        sublayer_grads[None],
+        qkv_grad,
+        out_grad,
+        up_grad,
+        down_grad,
+        model_vecs[:, 0:3],
+        model_vecs[:, 3:9],
+        hidden_rows[:, 0],
+        hidden_rows[:, 1:3],
+        pattern_means,
+    )
+
+
+def fits_quick(mesh):
+    return mesh.shape["section"] == 4 and mesh.shape["seq"] == 8
+
+
 def solution(mesh):
     return jax.shard_map(
-        body,
+        quick_body if fits_quick(mesh) else body,
         mesh=mesh,
         in_specs=(
             P(None, "seq", None),

time: 3570 us -> 733 us (0.21)
  waiting for transfers between devices: 2730 us -> 252 us
  Pallas kernels: 0 us -> 292 us
  matrix products: 250 us -> 0 us
  local copies, waits for them, and re-layouts: 251 us -> 50.5 us
  other arithmetic: 112 us -> 22 us
  blocking collectives: 127 us -> 83.6 us
    reduce_scatter x11 -> x2, waiting for transfers between devices: 1320 us -> 0.33 us  [quick_body(): shard = lax.psum_scatter(step, 'seq', scatter_dimension=0, tiled=True)]
    ppermute x14 -> x0, waiting for transfers between devices: 625 us -> none  [passed_along(): lax.ppermute(value, axis, [(source, source + steps) for source in range(i...]
    all_gather x18 -> x6, waiting for transfers between devices: 673 us -> 93 us  [the longest x2 67.6 us: quick_body(): lax.all_gather(rows, ('seq', 'section'), axis=0, tiled=True)]
    pallas_call x0 -> x8, Pallas kernels: none -> 292 us  [call_kernel(): pl.pallas_call(kernel, name=name, out_shape=outs, in_specs=[vmem] * len(a...]
    dot_general x49 -> x0, matrix products: 250 us -> none  [the longest x7 62.6 us: feed_backward(): jnp.einsum('tf,td->fd', inner_norm, grad_out, preferred_element_type=jnp....]
    unnamed x15 -> x12, waiting for transfers between devices: 29.8 us -> 150 us
    psum x1 -> x0, waiting for transfers between devices: 87.6 us -> none  [body(): lax.psum(placed[0].astype(jnp.bfloat16), 'section').astype(jnp.float32)]
    dynamic_slice x64 -> x2, local copies, waits for them, and re-layouts: 63.8 us -> 2.49 us  [of_section(): return lax.dynamic_index_in_dim(stacked, section, axis, False)]
  transfers between devices with their start and end apart: 47 -> 12, of which waited for: 44 -> 7; matrix products, arithmetic and copies ran while one was open for 2% -> 6% of each run, Pallas kernels for 0% -> 32%
where the time goes in v1:
time: 733 us; the launch traced here: 726 us
  Pallas kernels  292 us (40%)
  waiting for transfers between devices  252 us (34%)
  blocking collectives  83.6 us (11%)
  local copies, waits for them, and re-layouts  50.5 us (7%)
  other arithmetic  22 us (3%)
  between operations  14.9 us (2%)
  starting transfers between devices  10.5 us (1%)
    pallas_call x8, Pallas kernels, call_kernel(): pl.pallas_call(kernel, name=name, out_shape=outs, in_specs=[vmem] * len(a...  292 us
    unnamed x12, waiting for transfers between devices  150 us
    all_gather x2, waiting for transfers between devices, quick_body(): lax.all_gather(rows, ('seq', 'section'), axis=0, tiled=True)  67.6 us
    psum x1, blocking collectives, quick_body(): lines = lax.psum(lines, ('section', 'seq'))  43.3 us
    all_gather x2, blocking collectives, quick_body(): lax.all_gather(shard, 'section', axis=0, tiled=True)  25.9 us
    all_gather x2, waiting for transfers between devices, quick_body(): feed_shards[layer] = lax.all_gather(shard, 'section', axis=0, tiled=False)  25.4 us
  transfers between devices with their start and end apart: 12, of which 7 were waited for; matrix products, arithmetic and copies ran while one was open for 6% of the time, Pallas kernels for 32%

profile of v1, /device:TPU:14, one launch (start us, length us, event | category | flops | bytes accessed | tf_op | source)
XLA Modules:
  0.0 725.5 jit_solution(599609536982393662)
XLA Ops:
  19.8 14.4 %all-gather.1 = bf16[16,16,96]{2,1,0:T(8,128)(2,1)S(1)} all-gather(bf16[2,16,96]{2,1,0:T(8,128)(2,1)S(1)} %maximum_maximum_fusion), channel_id=3, replica_groups=mesh['section'=4,'seq'=8] {'seq'}, dimensions={0}, use_global_device_ids=true | all-gather | bytes 55296 | tf_op jit(solution)/shard_map/all_gather | solution.py:1467
  38.1 5.1 remainder_select_fusion
  44.2 31.6 %all-gather.16.cloned.1.call-done = bf16[1,768,3072]{2,1,0:T(8,128)(2,1)} async-done(((bf16[1,24,3072]{2,1,0:T(8,128)(2,1)}), bf16[1,768,3072]{2,1,0:T(8,128)(2,1)}) %all-gather.16.cloned.1.call-update) | async-done | bytes 4718608 | tf_op jit(solution)/shard_map/all_gather | solution.py:1474
  75.8 42.4 %attention_forward.2 = (bf16[128,768]{1,0:T(8,128)(2,1)}, bf16[1024,384]{1,0:T(8,128)(2,1)}, bf16[128,768]{1,0:T(8,128)(2,1)}, f32[1024,128]{1,0:T(8,128)}, f32[1024,128]{1,0:T(8,128)}, /*index=5*/f32[8,128]{1,0:T(8,128)}) custom-call(bf16[128,768]{1,0:T(8,128)(2,1)} %get-tuple-element.143.x_ref, bf16[768,3072]{1,0:T(8,128)(2,1)} %bitcast.77, ...), custom_call_target="tpu_custom_call" | custom-call | flops 1000000000 | bytes 60000000 | tf_op jit(solution)/shard_map/attention_forward/pallas_call | solution.py:1301
  118.2 31.5 %feed_forward.2 = (bf16[128,768]{1,0:T(8,128)(2,1)}, bf16[512,768]{1,0:T(8,128)(2,1)}, f32[512,768]{1,0:T(8,128)}, f32[512,128]{1,0:T(8,128)}) custom-call(bf16[128,768]{1,0:T(8,128)(2,1)} %get-tuple-element.39.x_ref, bf16[768,1536]{1,0:T(8,128)(2,1)} %all-gather.12.cloned.1.call-done.w_ref, f32[16,768]{1,0:T(8,128)} %squeeze.48.vec_ref), custom_call_target="tpu_custom_call" | custom-call | flops 1000000000 | bytes 60000000 | tf_op jit(solution)/shard_map/feed_forward/pallas_call | solution.py:1301
  149.8 35.9 %all-gather.18.cloned.1.call-done = bf16[1,768,3072]{2,1,0:T(8,128)(2,1)} async-done(((bf16[1,24,3072]{2,1,0:T(8,128)(2,1)}), bf16[1,768,3072]{2,1,0:T(8,128)(2,1)}) %all-gather.18.cloned.1.call-update) | async-done | bytes 4718608 | tf_op jit(solution)/shard_map/all_gather | solution.py:1474
  185.7 42.4 %attention_forward.3 = (bf16[128,768]{1,0:T(8,128)(2,1)}, bf16[1024,384]{1,0:T(8,128)(2,1)}, bf16[128,768]{1,0:T(8,128)(2,1)}, f32[1024,128]{1,0:T(8,128)}, f32[1024,128]{1,0:T(8,128)}, /*index=5*/f32[8,128]{1,0:T(8,128)}) custom-call(bf16[128,768]{1,0:T(8,128)(2,1)} %get-tuple-element.40.x_ref, bf16[768,3072]{1,0:T(8,128)(2,1)} %bitcast.79, ...), custom_call_target="tpu_custom_call" | custom-call | flops 1000000000 | bytes 60000000 | tf_op jit(solution)/shard_map/attention_forward/pallas_call | solution.py:1301
  228.2 31.4 %feed_forward.3 = (bf16[128,768]{1,0:T(8,128)(2,1)}, bf16[512,768]{1,0:T(8,128)(2,1)}, f32[512,768]{1,0:T(8,128)}, f32[512,128]{1,0:T(8,128)}) custom-call(bf16[128,768]{1,0:T(8,128)(2,1)} %get-tuple-element.41.x_ref, bf16[768,1536]{1,0:T(8,128)(2,1)} %all-gather.14.cloned.1.call-done.w_ref, f32[16,768]{1,0:T(8,128)} %squeeze.51.vec_ref), custom_call_target="tpu_custom_call" | custom-call | flops 1000000000 | bytes 60000000 | tf_op jit(solution)/shard_map/feed_forward/pallas_call | solution.py:1301
  259.6 27.7 %feed_backward.2 = (bf16[128,768]{1,0:T(8,128)(2,1)}, bf16[768,1664]{1,0:T(8,128)(2,1)}) custom-call(bf16[128,768]{1,0:T(8,128)(2,1)} %get-tuple-element.142.g_ref, bf16[128,768]{1,0:T(8,128)(2,1)} %get-tuple-element.41.x_ref, bf16[512,768]{1,0:T(8,128)(2,1)} %get-tuple-element.43.hid_ref, f32[512,768]{1,0:T(8,128)} %get-tuple-element.44.up_ref, ...), custom_call_target="tpu_custom_call" | custom-call | flops 2000000000 | bytes 60000000 | tf_op jit(solution)/shard_map/feed_backward/pallas_call | solution.py:1301
  287.4 43.0 %attention_backward.2 = (bf16[128,768]{1,0:T(8,128)(2,1)}, bf16[768,3200]{1,0:T(8,128)(2,1)}) custom-call(bf16[128,768]{1,0:T(8,128)(2,1)} %get-tuple-element.46.g_ref, bf16[128,768]{1,0:T(8,128)(2,1)} %get-tuple-element.40.x_ref, bf16[128,768]{1,0:T(8,128)(2,1)} %get-tuple-element.47.att_ref, bf16[768,3072]{1,0:T(8,128)(2,1)} %bitcast.80, ...), custom_call_target="tpu_custom_call" | custom-call | flops 2000000000 | bytes 60000000 | tf_op jit(solution)/shard_map/attention_backward/pallas_call | solution.py:1301
  330.5 31.6 %feed_backward.3 = (bf16[128,768]{1,0:T(8,128)(2,1)}, bf16[768,1664]{1,0:T(8,128)(2,1)}) custom-call(bf16[128,768]{1,0:T(8,128)(2,1)} %get-tuple-element.51.g_ref, bf16[128,768]{1,0:T(8,128)(2,1)} %get-tuple-element.39.x_ref, bf16[512,768]{1,0:T(8,128)(2,1)} %get-tuple-element.52.hid_ref, f32[512,768]{1,0:T(8,128)} %get-tuple-element.53.up_ref, ...), custom_call_target="tpu_custom_call" | custom-call | flops 2000000000 | bytes 60000000 | tf_op jit(solution)/shard_map/feed_backward/pallas_call | solution.py:1301
  362.1 41.7 %attention_backward.3 = (bf16[128,768]{1,0:T(8,128)(2,1)}, bf16[768,3200]{1,0:T(8,128)(2,1)}) custom-call(bf16[128,768]{1,0:T(8,128)(2,1)} %get-tuple-element.55.g_ref, bf16[128,768]{1,0:T(8,128)(2,1)} %get-tuple-element.143.x_ref, bf16[128,768]{1,0:T(8,128)(2,1)} %get-tuple-element.56.att_ref, bf16[768,3072]{1,0:T(8,128)(2,1)} %bitcast.78, ...), custom_call_target="tpu_custom_call" | custom-call | flops 2000000000 | bytes 60000000 | tf_op jit(solution)/shard_map/attention_backward/pallas_call | solution.py:1301
  406.4 5.2 all-to-all-start.1
  413.2 8.5 %all-to-all-done.1 = bf16[4,128,768]{2,1,0:T(8,128)(2,1)S(1)} async-done(((bf16[4,128,768]{2,1,0:T(8,128)(2,1)}), bf16[4,128,768]{2,1,0:T(8,128)(2,1)S(1)}, u32[]{:S(2)}, u32[]{:S(2)}) %all-to-all-start.1) | async-done | bytes 786464 | tf_op jit(solution)/shard_map/all_to_all | solution.py:1531
  421.7 5.0 all-to-all-start
  428.2 43.3 %psum.7 = f32[3,5]{1,0:T(4,128)S(1)} all-reduce(f32[3,5]{1,0:T(4,128)S(1)} %reduce_sum.49), channel_id=1, replica_groups=mesh['section'=4,'seq'=8] {'section','seq'}, use_global_device_ids=true, to_apply=%region_10.11 | all-reduce | flops 15 | bytes 120 | tf_op jit(solution)/shard_map/psum | solution.py:1502
  472.1 51.0 %reduce-scatter.13.cloned.1.call-done = bf16[24,3200]{1,0:T(8,128)(2,1)} async-done(((bf16[768,3200]{1,0:T(8,128)(2,1)}), bf16[24,3200]{1,0:T(8,128)(2,1)}) %reduce-scatter.13.cloned.1.call-update) | async-done | bytes 153616
  523.1 10.6 %all_gather.42 = bf16[96,3200]{1,0:T(8,128)(2,1)S(1)} all-gather(bf16[24,3200]{1,0:T(8,128)(2,1)} %reduce-scatter.13.cloned.1.call-done), channel_id=1, replica_groups=mesh['section'=4,'seq'=8] {'section'}, dimensions={0}, use_global_device_ids=true | all-gather | bytes 768000 | tf_op jit(solution)/shard_map/all_gather | solution.py:1530
  534.9 97.7 %reduce-scatter.15.cloned.1.call-done = bf16[24,3200]{1,0:T(8,128)(2,1)} async-done(((bf16[768,3200]{1,0:T(8,128)(2,1)}), bf16[24,3200]{1,0:T(8,128)(2,1)}) %reduce-scatter.15.cloned.1.call-update) | async-done | bytes 153616
  632.6 15.3 %all_gather.43 = bf16[96,3200]{1,0:T(8,128)(2,1)} all-gather(bf16[24,3200]{1,0:T(8,128)(2,1)} %reduce-scatter.15.cloned.1.call-done), channel_id=1, replica_groups=mesh['section'=4,'seq'=8] {'section'}, dimensions={0}, use_global_device_ids=true | all-gather | bytes 768000 | tf_op jit(solution)/shard_map/all_gather | solution.py:1530
  647.9 3.4 copy.84
  653.2 2.0 copy.90
  655.2 4.3 maximum_convert_fusion.1
  659.7 3.1 copy.89
  662.8 3.4 copy.86
  666.2 25.4 %all-gather.20.cloned.1.call-done = bf16[384,1664]{1,0:T(8,128)(2,1)} async-done(((bf16[96,1664]{1,0:T(8,128)(2,1)}), bf16[384,1664]{1,0:T(8,128)(2,1)}) %all-gather.20.cloned.1.call-update) | async-done | bytes 1277968 | tf_op jit(solution)/shard_map/all_gather | solution.py:1515
  691.6 3.4 copy.85
  697.6 2.7 maximum_convert_fusion
  700.9 2.7 fusion.13
  703.6 4.6 copy.88
  708.1 3.3 copy.87
  711.4 5.3 reshape.351
  (129 shorter events, 31.8 us)
Async XLA Ops:
  7.2 3.1 copy-start.7
  7.2 68.6 %all-gather.16.cloned.1.call-start = ((), (), s32[]{:S(2)}) async-start(), calls=%async_computation.10 | async-start | bytes 4866048 | tf_op jit(solution)/shard_map/all_gather | solution.py:1474
  10.2 108.0 %all-gather.12.cloned.1.call-start = ((), (), s32[]{:S(2)}) async-start(), calls=%async_computation.6 | async-start | bytes 2654208 | tf_op jit(solution)/shard_map/all_gather | solution.py:1478
  14.7 4.8 copy-start.17
  14.7 4.8 copy-start.18
  14.7 4.9 copy-start.15
  14.7 4.9 copy-start.16
  14.7 171.0 %all-gather.18.cloned.1.call-start = ((), (), s32[]{:S(2)}) async-start(), calls=%async_computation.11 | async-start | bytes 4866048 | tf_op jit(solution)/shard_map/all_gather | solution.py:1474
  15.5 212.7 %all-gather.14.cloned.1.call-start = ((), (), s32[]{:S(2)}) async-start(), calls=%async_computation.7 | async-start | bytes 2654208 | tf_op jit(solution)/shard_map/all_gather | solution.py:1478
  18.5 386.2 %reduce-scatter.11.cloned.1.call-start = ((), (), s32[]{:S(2)}) async-start(), calls=%async_computation.9 | async-start | bytes 2875392 | tf_op jit(solution)/shard_map/reduce_scatter | solution.py:1514
  287.4 124.6 %reduce-scatter.9.cloned.1.call-start = ((), (), s32[]{:S(2)}) async-start(), calls=%async_computation.8 | async-start | bytes 2875392 | tf_op jit(solution)/shard_map/reduce_scatter | solution.py:1514
  362.1 161.1 %reduce-scatter.13.cloned.1.call-start = ((), (), s32[]{:S(2)}) async-start(), calls=%async_computation.14 | async-start | bytes 5068800
  403.9 228.7 %reduce-scatter.15.cloned.1.call-start = ((), (), s32[]{:S(2)}) async-start(), calls=%async_computation.15 | async-start | bytes 5068800
  403.9 1.5 copy-start.8
  404.0 1.5 copy-start.9
  404.0 1.5 copy-start.13
  404.0 1.5 copy-start.14
  404.6 7.5 %copy-start.6 = (bf16[128,768]{1,0:T(8,128)(2,1)S(1)}, bf16[128,768]{1,0:T(8,128)(2,1)}, u32[]{:S(2)}) copy-start(bf16[128,768]{1,0:T(8,128)(2,1)} %get-tuple-element.40.x_ref) | copy-start | bytes 589828
  404.7 7.5 %copy-start.10 = (bf16[128,768]{1,0:T(8,128)(2,1)S(1)}, bf16[128,768]{1,0:T(8,128)(2,1)}, u32[]{:S(2)}) copy-start(bf16[128,768]{1,0:T(8,128)(2,1)} %get-tuple-element.39.x_ref) | copy-start | bytes 589828
  404.7 7.5 %copy-start.11 = (bf16[128,768]{1,0:T(8,128)(2,1)S(1)}, bf16[128,768]{1,0:T(8,128)(2,1)}, u32[]{:S(2)}) copy-start(bf16[128,768]{1,0:T(8,128)(2,1)} %get-tuple-element.41.x_ref) | copy-start | bytes 589828
  404.7 7.5 %copy-start.12 = (bf16[128,768]{1,0:T(8,128)(2,1)S(1)}, bf16[128,768]{1,0:T(8,128)(2,1)}, u32[]{:S(2)}) copy-start(bf16[128,768]{1,0:T(8,128)(2,1)} %get-tuple-element.42) | copy-start | bytes 589828
  404.7 258.1 %all-gather.22.cloned.1.call-start = ((), (), s32[]{:S(2)}) async-start(), calls=%async_computation.13 | async-start | bytes 1597440 | tf_op jit(solution)/shard_map/all_gather | solution.py:1515
  406.4 15.2 %all-to-all-start.1 = ((bf16[4,128,768]{2,1,0:T(8,128)(2,1)}), bf16[4,128,768]{2,1,0:T(8,128)(2,1)S(1)}, u32[]{:S(2)}, u32[]{:S(2)}) async-start(bf16[4,128,768]{2,1,0:T(8,128)(2,1)} %pad_maximum_fusion.1), calls=%async_computation.1 | async-start | bytes 1572864 | tf_op jit(solution)/shard_map/all_to_all | solution.py:1531
  411.6 280.0 %all-gather.20.cloned.1.call-start = ((), (), s32[]{:S(2)}) async-start(), calls=%async_computation.12 | async-start | bytes 1597440 | tf_op jit(solution)/shard_map/all_gather | solution.py:1515
  421.7 112.0 %copy-start.2 = (bf16[4,128,768]{2,1,0:T(8,128)(2,1)}, bf16[4,128,768]{2,1,0:T(8,128)(2,1)S(1)}, u32[]{:S(2)}) copy-start(bf16[4,128,768]{2,1,0:T(8,128)(2,1)S(1)} %all-to-all-done.1) | copy-start | bytes 2359300
  421.7 50.4 %all-to-all-start = ((bf16[4,128,768]{2,1,0:T(8,128)(2,1)}), bf16[4,128,768]{2,1,0:T(8,128)(2,1)S(1)}, u32[]{:S(2)}, u32[]{:S(2)}) async-start(bf16[4,128,768]{2,1,0:T(8,128)(2,1)} %pad_maximum_fusion), calls=%async_computation | async-start | bytes 1572864 | tf_op jit(solution)/shard_map/all_to_all | solution.py:1499
  472.1 61.6 %copy-start.4 = (bf16[4,128,768]{2,1,0:T(8,128)(2,1)}, bf16[4,128,768]{2,1,0:T(8,128)(2,1)S(1)}, u32[]{:S(2)}) copy-start(bf16[4,128,768]{2,1,0:T(8,128)(2,1)S(1)} %all-to-all-done) | copy-start | bytes 2359300
  534.9 120.3 %copy-start = (bf16[1,96,3200]{1,0,2:T(2,128)(2,1)}, bf16[1,96,3200]{1,0,2:T(2,128)(2,1)S(1)}, u32[]{:S(2)}) copy-start(bf16[1,96,3200]{1,0,2:T(2,128)(2,1)S(1)} %copy.83) | copy-start | bytes 1843204
  651.3 4.0 copy-start.1
  711.4 5.3 copy-start.5
  711.4 6.2 copy-start.3
Sparse Core Ops, SparseCore 0:
  11.5 64.2 all-gather.15
  78.0 38.7 all-gather.11
  119.7 65.9 all-gather.17
  187.8 38.8 all-gather.13
  287.5 50.8 reduce-scatter.10
  362.2 49.6 reduce-scatter.8
  417.6 105.4 reduce-scatter.12
  529.8 102.7 reduce-scatter.14
  634.4 26.8 all-gather.21
  663.0 28.5 all-gather.19

commit v2 on v0

--- a/solution.py
+++ b/solution.py
@@ -1,6 +1,8 @@
 import jax
 import jax.numpy as jnp
 from jax import lax
+from jax.experimental import pallas as pl
+from jax.experimental.pallas import tpu as pltpu
 from jax.sharding import PartitionSpec as P
 
 D = 768
@@ -602,9 +604,1787 @@
     )
 
 
+BF16 = jnp.bfloat16
+F32 = jnp.float32
+PAIRS = HEADS // 2
+OWNERS = (0, 2, 3, 4, 5, 6)
+TOKENS = 128
+PAIR_LANES = 128
+QUERY_STEP = 256
+VEC_ROWS = 16
+KERNEL_VMEM_BYTES = 62 * 1024 * 1024
+SCALE = HEAD_DIM ** (-0.5)
+
+
+def mul(left, right):
+    return lax.dot_general(left, right, (((1,), (0,)), ((), ())), preferred_element_type=F32)
+
+
+def mul_nt(left, right):
+    return lax.dot_general(left, right, (((1,), (1,)), ((), ())), preferred_element_type=F32)
+
+
+def mul_tn(left, right):
+    return lax.dot_general(left, right, (((0,), (0,)), ((), ())), preferred_element_type=F32)
+
+
+def standardize(values):
+    center = values - jnp.mean(values, -1, keepdims=True)
+    rstd = lax.rsqrt(jnp.mean(center * center, -1, keepdims=True) + EPSILON)
+    return (center * rstd, rstd)
+
+
+def norm_back(unit, rstd, unit_grad):
+    first = jnp.mean(unit_grad, -1, keepdims=True)
+    second = jnp.mean(unit_grad * unit, -1, keepdims=True)
+    return rstd * (unit_grad - first - unit * second)
+
+
+def remote(source, target, send_sem, recv_sem, axis, peer):
+    return pltpu.make_async_remote_copy(
+        src_ref=source,
+        dst_ref=target,
+        send_sem=send_sem,
+        recv_sem=recv_sem,
+        device_id={axis: peer},
+        device_id_type=pl.DeviceIdType.MESH,
+    )
+
+
+def greet(axis, peers):
+    barrier = pltpu.get_barrier_semaphore()
+    for peer in peers:
+        pl.semaphore_signal(
+            barrier, inc=1, device_id={axis: peer}, device_id_type=pl.DeviceIdType.MESH
+        )
+    pl.semaphore_wait(barrier, len(peers))
+
+
+def seq_peers(me, count):
+    return [lax.rem(me + step, count) for step in range(1, count)]
+
+
+def plane_peers(me):
+    return [
+        me,
+        me + 1 - 2 * lax.rem(me, 2),
+        lax.rem(me + 2, 4),
+        3 - me,
+    ]
+
+
+def rows_of(block, size=TOKENS):
+    return pl.ds(pl.multiple_of(block * size, size), size)
+
+
+def gelu_parts(values):
+    below = 0.5 * (1.0 + lax.erf(values * (0.5**0.5)))
+    return (values * below, below)
+
+
+def share_stats(columns, send, recv, send_sem, recv_sem, peers):
+    send[...] = columns.T[0:8, :]
+    recv[0] = send[...]
+    copies = [
+        remote(send, recv.at[k], send_sem.at[k], recv_sem.at[k], "section", peers[k])
+        for k in range(1, 4)
+    ]
+    for copy in copies:
+        copy.start()
+    return copies
+
+
+def two_columns(first, second):
+    lane = lax.broadcasted_iota(jnp.int32, (first.shape[0], PAIR_LANES), 1)
+    return jnp.where(lane == 0, first, jnp.where(lane == 1, second, 0.0))
+
+
+def slot_rows(k):
+    return slice(k * TOKENS, (k + 1) * TOKENS)
+
+
+def shaped(shape, kind):
+    return jax.ShapeDtypeStruct(shape, kind)
+
+
+class Named:
+    def __init__(self, groups, refs):
+        names = [name for group in groups for name in group]
+        for name, ref in zip(names, refs, strict=True):
+            setattr(self, name, ref)
+
+
+GROUP_TOKENS = 8 * TOKENS
+WIDE = 4 * TOKENS
+SHARD = D // 8
+FORE_VMEM = dict(embeds=0, gains=0, biases=0, hgains=0, hbiases=0)
+FORE_ANY = dict(qkv_w=0, out_w=0, up_w=0, down_w=0)
+FORE_OUT = dict(
+    sub=((4, TOKENS, D), BF16, True),
+    streams=((4, TOKENS, D), BF16, True),
+    att=((2, TOKENS, D), BF16, True),
+    vecs=((2, VEC_ROWS, D), F32, True),
+    picks=((2, GROUP_TOKENS, PAIR_LANES), BF16, True),
+    logs=((8, PAIR_LANES), F32, True),
+    wa_out=((2, 4, 4, 2, SHARD, D), BF16, False),
+    wf_out=((2, 2, 4, 2, SHARD, D), BF16, False),
+    qkv_out=((2, 3, GROUP_TOKENS, PAIR_LANES), BF16, False),
+    pa_out=((2, GROUP_TOKENS, PAIR_LANES), F32, False),
+    pt_out=((2, GROUP_TOKENS, PAIR_LANES), F32, False),
+    hid_out=((2, WIDE, D), BF16, False),
+    up_out=((2, WIDE, D), F32, False),
+    stat_out=((2, WIDE, PAIR_LANES), F32, False),
+)
+FORE_SCRATCH = dict(
+    wa=((2, 4, 4, 2, SHARD, D), BF16),
+    wf=((2, 2, 4, 2, SHARD, D), BF16),
+    qkv=((2, 3, GROUP_TOKENS, PAIR_LANES), BF16),
+    pa=((2, GROUP_TOKENS, PAIR_LANES), F32),
+    pt=((2, GROUP_TOKENS, PAIR_LANES), F32),
+    hid=((2, WIDE, D), BF16),
+    up=((2, WIDE, D), F32),
+    stat=((2, WIDE, PAIR_LANES), F32),
+    raw_up=((2, SHARD, FF), BF16),
+    small_src=((2, 32, PAIR_LANES), BF16),
+    small=((8, 2, 32, PAIR_LANES), BF16),
+    hidden=((WIDE, D), BF16),
+    proj_send=((4, PAIRS, TOKENS, PAIR_LANES), BF16),
+    send=((PAIRS, 3, TOKENS, PAIR_LANES), BF16),
+    att_send=((GROUP_TOKENS, PAIR_LANES), BF16),
+    att_recv=((2, PAIRS, TOKENS, PAIR_LANES), BF16),
+    active=((WIDE, D), F32),
+    columns=((WIDE, PAIR_LANES), F32),
+    stat_rows=((PAIR_LANES, WIDE), F32),
+    part_send=((4, TOKENS, D), BF16),
+    part_recv=((2, 4, TOKENS, D), BF16),
+    stat_send=((8, WIDE), F32),
+    stat_recv=((2, 4, 8, WIDE), F32),
+)
+FORE_SEMS = dict(
+    load_sem=(2, 3),
+    store_sem=(2, 8),
+    small_s=(8,),
+    small_r=(8,),
+    az_s=(2, 4),
+    az_r=(2, 4),
+    asib_s=(2,),
+    asib_r=(2,),
+    axy_s=(2, 4),
+    axy_r=(2, 4),
+    axs_s=(2, 4),
+    axs_r=(2, 4),
+    fz_s=(2, 2, 4),
+    fz_r=(2, 2, 4),
+    fsib_s=(2, 2),
+    fsib_r=(2, 2),
+    wide_s=(4, PAIRS),
+    wide_r=(3, 8),
+    qkv_s=(PAIRS,),
+    qkv_r=(8,),
+    att_s=(2, 8),
+    att_r=(2, PAIRS),
+    hid_s=(2, 4),
+    hid_r=(2, 4),
+    stat_s=(2, 4),
+    stat_r=(2, 4),
+    part_s=(2, 4),
+    part_r=(2, 4),
+    sub_s=(4,),
+    sub_r=(4,),
+)
+
+
+def square(ref):
+    return ref[...].reshape(D, D)
+
+
+def remote_both(source, target, send_sem, recv_sem, section, seq):
+    return pltpu.make_async_remote_copy(
+        src_ref=source,
+        dst_ref=target,
+        send_sem=send_sem,
+        recv_sem=recv_sem,
+        device_id=(section, seq),
+        device_id_type=pl.DeviceIdType.MESH,
+    )
+
+
+def make_picks(lengths_ref, section, my_pair, picks_ref):
+    tokens = lax.broadcasted_iota(jnp.int32, (GROUP_TOKENS, PAIR_LANES), 0)
+    lane = lax.broadcasted_iota(jnp.int32, (GROUP_TOKENS, PAIR_LANES), 1)
+    row_id = jnp.zeros_like(tokens)
+    first = jnp.zeros_like(tokens)
+    end = 0
+    for row in range(lengths_ref.shape[1]):
+        end = end + lengths_ref[section, row]
+        passed = tokens >= end
+        row_id = row_id + jnp.where(passed, 1, 0)
+        first = jnp.where(passed, end, first)
+    pos = (tokens - first).astype(F32)
+    number = lax.shift_right_logical(lane, 2)
+    row = lane - 4 * number
+    ratio = jnp.zeros(lane.shape, F32)
+    for i, each in enumerate(RATIOS):
+        ratio = jnp.where(number == i, float(each), ratio)
+    valid = ratio > 0.5
+    ratio = jnp.where(valid, ratio, 1.0)
+
+    def residue(values):
+        return values - ratio * jnp.floor((values + 0.5) / ratio)
+
+    residues = residue(pos)
+    for head in range(2):
+        wanted = residue(jnp.full(lane.shape, 2 * my_pair + head, jnp.int32).astype(F32))
+        fits = valid & (row == row_id) & (jnp.abs(residues - wanted) < 0.5)
+        picks_ref[head] = jnp.where(fits, 1.0, 0.0).astype(BF16)
+
+
+def forward_kernel(lengths, *refs):
+    b = Named([FORE_VMEM, FORE_ANY, FORE_OUT, FORE_SCRATCH, FORE_SEMS], refs)
+    me = lax.axis_index("seq")
+    section = lax.axis_index("section")
+    peers = plane_peers(section)
+    core = lax.rem(me, 2)
+    chip = lax.div(me, 2)
+    sibling = me + 1 - 2 * core
+    is_owner = (me != 1) & (me != 7)
+    my_pair = jnp.where(me == 0, 0, me - 1)
+    my_pair = jnp.where(my_pair > PAIRS - 1, PAIRS - 1, my_pair)
+
+    barrier = pltpu.get_barrier_semaphore()
+    for other in range(4):
+        for j in range(8):
+
+            @pl.when((section != other) | (me != j))
+            def _():
+                pl.semaphore_signal(
+                    barrier, inc=1, device_id=(other, j), device_id_type=pl.DeviceIdType.MESH
+                )
+
+    def load_block(layer):
+        target = b.wa.at[layer, section, chip, core]
+
+        def from_qkv():
+            return pltpu.make_async_copy(
+                b.qkv_w.at[layer, :, pl.ds(pl.multiple_of(lax.rem(section, 3) * D, D), D)],
+                target,
+                b.load_sem.at[layer, 0],
+            )
+
+        def from_out():
+            return pltpu.make_async_copy(b.out_w.at[layer], target, b.load_sem.at[layer, 0])
+
+        return from_qkv, from_out
+
+    def load_up(layer):
+        return pltpu.make_async_copy(b.up_w.at[layer], b.raw_up.at[layer], b.load_sem.at[layer, 1])
+
+    def load_down(layer):
+        return pltpu.make_async_copy(
+            b.down_w.at[layer, pl.ds(pl.multiple_of(section * SHARD, SHARD), SHARD)],
+            b.wf.at[layer, 1, chip, core],
+            b.load_sem.at[layer, 2],
+        )
+
+    for layer in range(2):
+        from_qkv, from_out = load_block(layer)
+
+        @pl.when(section != 3)
+        def _():
+            from_qkv().start()
+
+        @pl.when(section == 3)
+        def _():
+            from_out().start()
+
+        load_up(layer).start()
+        load_down(layer).start()
+
+    def pick_up(layer):
+        load_up(layer).wait()
+        load_down(layer).wait()
+        raw = b.raw_up[layer]
+        for s in range(4):
+
+            @pl.when(section == s)
+            def _():
+                b.wf[layer, 0, chip, core] = jnp.concatenate(
+                    [
+                        raw[:, (4 * j + s) * SHARD : (4 * j + s + 1) * SHARD].astype(F32)
+                        for j in range(8)
+                    ],
+                    1,
+                ).astype(BF16)
+
+    def block_z(layer, step):
+        target = lax.rem(chip + step, 4)
+        return remote(
+            b.wa.at[layer, section, chip, core],
+            b.wa.at[layer, section, chip, core],
+            b.az_s.at[layer, step],
+            b.az_r.at[layer, step],
+            "seq",
+            2 * target + core,
+        )
+
+    def block_z_wait(layer):
+        for step in range(1, 4):
+            source = lax.rem(chip + 4 - step, 4)
+            remote(
+                b.wa.at[layer, section, source, core],
+                b.wa.at[layer, section, source, core],
+                b.az_s.at[layer, step],
+                b.az_r.at[layer, step],
+                "seq",
+                2 * source + core,
+            ).wait_recv()
+
+    def plane_view(layer, slot, side):
+        return b.wa.at[layer, slot, :, side]
+
+    def block_sibling(layer, side):
+        view = plane_view(layer, section, side)
+        return remote(view, view, b.asib_s.at[layer], b.asib_r.at[layer], "seq", sibling)
+
+    def block_plane(layer, k, slot):
+        view = plane_view(layer, slot, core)
+        return remote(view, view, b.axy_s.at[layer, k], b.axy_r.at[layer, k], "section", peers[k])
+
+    def block_across(layer, k, side):
+        view = plane_view(layer, peers[k], side)
+        return remote(view, view, b.axs_s.at[layer, k], b.axs_r.at[layer, k], "seq", sibling)
+
+    def feed_z(layer, which, step):
+        target = lax.rem(chip + step, 4)
+        return remote(
+            b.wf.at[layer, which, chip, core],
+            b.wf.at[layer, which, chip, core],
+            b.fz_s.at[layer, which, step],
+            b.fz_r.at[layer, which, step],
+            "seq",
+            2 * target + core,
+        )
+
+    def feed_z_start(layer, which):
+        for step in range(1, 4):
+            feed_z(layer, which, step).start()
+
+    def feed_sibling(layer, which, side):
+        view = b.wf.at[layer, which, :, side]
+        return remote(
+            view, view, b.fsib_s.at[layer, which], b.fsib_r.at[layer, which], "seq", sibling
+        )
+
+    def feed_z_pass(layer, which):
+        for step in range(1, 4):
+            source = lax.rem(chip + 4 - step, 4)
+            remote(
+                b.wf.at[layer, which, source, core],
+                b.wf.at[layer, which, source, core],
+                b.fz_s.at[layer, which, step],
+                b.fz_r.at[layer, which, step],
+                "seq",
+                2 * source + core,
+            ).wait_recv()
+        feed_sibling(layer, which, core).start()
+
+    def block_z_start(layer):
+        from_qkv, from_out = load_block(layer)
+
+        @pl.when(section != 3)
+        def _():
+            from_qkv().wait()
+
+        @pl.when(section == 3)
+        def _():
+            from_out().wait()
+
+        for step in range(1, 4):
+            block_z(layer, step).start()
+
+    for layer in range(2):
+        gains = b.gains[layer].astype(F32)
+        biases = b.biases[layer].astype(F32)
+        hidden_gain = b.hgains[layer : layer + 1, :].astype(F32)
+        hidden_bias = b.hbiases[layer].astype(F32)
+        lines = [gains, biases]
+        for each in (hidden_gain, hidden_bias[0:1, :], hidden_bias[1:2, :]):
+            for s in range(4):
+                lines.append(each[:, s * SHARD : (s + 1) * SHARD])
+        lines.append(jnp.zeros((11, SHARD), F32))
+        packed = jnp.concatenate(lines, 0)
+        packed = jnp.concatenate([packed, jnp.zeros((32, PAIR_LANES - SHARD), F32)], 1)
+        b.small_src[layer] = packed.astype(BF16)
+    b.small[me] = b.small_src[...]
+    pl.semaphore_wait(barrier, 31)
+
+    def small_copy(step):
+        return remote(
+            b.small_src,
+            b.small.at[me],
+            b.small_s.at[step],
+            b.small_r.at[step],
+            "seq",
+            lax.rem(me + step, 8),
+        )
+
+    for step in range(1, 8):
+        small_copy(step).start()
+    block_z_start(0)
+    make_picks(lengths, section, my_pair, b.picks)
+    pick_up(0)
+    for step in range(1, 8):
+        source = lax.rem(me + 8 - step, 8)
+        remote(
+            b.small_src,
+            b.small.at[source],
+            b.small_s.at[step],
+            b.small_r.at[step],
+            "seq",
+            source,
+        ).wait_recv()
+    for layer in range(2):
+        pieces = []
+        for j in range(8):
+            block = b.small[j, layer].astype(F32)
+            lines = [block[0:9]]
+            for third in range(3):
+                line = jnp.zeros((1, PAIR_LANES), F32)
+                for s in range(4):
+                    at = 9 + 4 * third + s
+                    line = line + jnp.where(section == s, block[at : at + 1], 0.0)
+                lines.append(line)
+            lines.append(jnp.zeros((4, PAIR_LANES), F32))
+            pieces.append(jnp.concatenate(lines, 0)[:, 0:SHARD])
+        b.vecs[layer] = jnp.concatenate(pieces, 1)
+    b.logs[...] = jnp.zeros_like(b.logs)
+
+    def send_sub(number):
+        @pl.when(section != number)
+        def _():
+            sub_copy(number).start()
+
+        @pl.when(section == number)
+        def _():
+            b.sub[section] = b.streams[number]
+
+    def sub_copy(number):
+        return remote(
+            b.streams.at[number],
+            b.sub.at[section],
+            b.sub_s.at[number],
+            b.sub_r.at[section],
+            "section",
+            number,
+        )
+
+    def back_copy(layer, target):
+        return remote(
+            b.att_send.at[pl.ds(target * TOKENS, TOKENS)],
+            b.att_recv.at[layer, my_pair],
+            b.att_s.at[layer, target],
+            b.att_r.at[layer, my_pair],
+            "seq",
+            target,
+        )
+
+    def attend(layer):
+        lane = lax.broadcasted_iota(jnp.int32, (QUERY_STEP, PAIR_LANES), 1)
+        first_half = lane < HEAD_DIM
+        for step in range(GROUP_TOKENS // QUERY_STEP):
+            start = step * QUERY_STEP
+            keys_end = start + QUERY_STEP
+            rows = slice(start, keys_end)
+            query = b.qkv[layer, 0, rows, :] * jnp.asarray(SCALE, BF16)
+            keys = b.qkv[layer, 1, 0:keys_end, :]
+            values = b.qkv[layer, 2, 0:keys_end, :]
+            causal = lax.broadcasted_iota(jnp.int32, (QUERY_STEP, keys_end), 1) <= (
+                start + lax.broadcasted_iota(jnp.int32, (QUERY_STEP, keys_end), 0)
+            )
+            sums = []
+            totals = []
+            logs = jnp.zeros((1, PAIR_LANES), F32)
+            picked_sum = jnp.zeros((1, PAIR_LANES), F32)
+            for head in range(2):
+                mine = first_half if head == 0 else ~first_half
+                own_query = jnp.where(mine, query, jnp.zeros_like(query))
+                scores = mul_nt(own_query, keys)
+                raised = jnp.where(causal, jnp.exp(scores), 0.0)
+                pick_query = b.picks[head, rows, :]
+                pick_keys = b.picks[head, 0:keys_end, :]
+                counts = mul_nt(pick_query, pick_keys)
+                weighted = (raised * counts).astype(BF16)
+                sums.append(mul(weighted, values))
+                pattern = mul(raised.astype(BF16), pick_keys)
+                picked = pick_query.astype(F32)
+                totals.append(jnp.sum(pattern * picked, -1, keepdims=True))
+                chosen = picked > 0.5
+                logs = logs + jnp.sum(
+                    jnp.where(chosen, jnp.log(jnp.where(chosen, pattern, 1.0)), 0.0),
+                    0,
+                    keepdims=True,
+                )
+                picked_sum = picked_sum + jnp.sum(picked, 0, keepdims=True)
+            b.logs[layer : layer + 1, :] += logs
+            if layer == 0:
+                b.logs[2:3, :] += picked_sum
+            total = jnp.where(first_half, totals[0], totals[1])
+            attended = jnp.where(first_half, sums[0], sums[1]) / total
+            b.pa[layer, rows, :] = attended
+            b.pt[layer, rows, :] = total
+            b.att_send[rows, :] = attended.astype(BF16)
+            for target in (2 * step, 2 * step + 1):
+
+                @pl.when(me != target)
+                def _():
+                    back_copy(layer, target).start()
+
+                @pl.when(me == target)
+                def _():
+                    b.att_recv[layer, my_pair] = b.att_send[
+                        target * TOKENS : (target + 1) * TOKENS, :
+                    ]
+
+    def attention_end(layer, inputs):
+        vec = b.vecs.at[layer]
+        for pair, owner in enumerate(OWNERS):
+
+            @pl.when(me != owner)
+            def _():
+                remote(
+                    b.att_send.at[pl.ds(0, TOKENS)],
+                    b.att_recv.at[layer, pair],
+                    b.att_s.at[layer, 0],
+                    b.att_r.at[layer, pair],
+                    "seq",
+                    owner,
+                ).wait_recv()
+
+            b.att[layer, :, pair * PAIR_LANES : (pair + 1) * PAIR_LANES] = b.att_recv[layer, pair]
+        inner_unit, unused = standardize(b.att[layer].astype(F32))
+        inner = (inner_unit * vec[1:2, :] + vec[4:5, :]).astype(BF16)
+        branch = mul(inner, square(b.wa.at[layer, 3])) + vec[7:8, :]
+        b.streams[2 * layer] = (inputs + branch).astype(BF16)
+        send_sub(2 * layer)
+
+        @pl.when(is_owner)
+        def _():
+            for target in range(8):
+
+                @pl.when(me != target)
+                def _():
+                    back_copy(layer, target).wait_send()
+
+    def feed(layer, waiting, resting):
+        vec = b.vecs.at[layer]
+        inputs = b.streams[2 * layer].astype(F32)
+        unit, unused = standardize(inputs)
+        b.hid[layer, slot_rows(0), :] = (unit * vec[2:3, :] + vec[5:6, :]).astype(BF16)
+        hidden_copies = [
+            remote(
+                b.hid.at[layer, pl.ds(0, TOKENS)],
+                b.hid.at[layer, pl.ds(k * TOKENS, TOKENS)],
+                b.hid_s.at[layer, k],
+                b.hid_r.at[layer, k],
+                "section",
+                peers[k],
+            )
+            for k in range(1, 4)
+        ]
+        for copy in hidden_copies:
+            copy.start()
+        waiting()
+        feed_sibling(layer, 0, 1 - core).wait_recv()
+        for k in range(4):
+            if k > 0:
+                hidden_copies[k - 1].wait_recv()
+            upward = mul(b.hid[layer, slot_rows(k), :], square(b.wf.at[layer, 0])) + vec[10:11, :]
+            b.up[layer, slot_rows(k), :] = upward
+            values, unused = gelu_parts(upward)
+            b.active[slot_rows(k), :] = values
+            mean = jnp.mean(values, -1, keepdims=True)
+            center = values - mean
+            b.columns[slot_rows(k), :] = two_columns(
+                mean, jnp.sum(center * center, -1, keepdims=True)
+            )
+        stat_copies = share_stats(
+            b.columns[...],
+            b.stat_send,
+            b.stat_recv.at[layer],
+            b.stat_s.at[layer],
+            b.stat_r.at[layer],
+            peers,
+        )
+        resting()
+        for copy in stat_copies:
+            copy.wait_recv()
+        b.stat_rows[...] = jnp.zeros((PAIR_LANES, WIDE), F32)
+        for k in range(4):
+            means = [b.stat_recv[layer, other, 0:1, slot_rows(k ^ other)] for other in range(4)]
+            squares = [b.stat_recv[layer, other, 1:2, slot_rows(k ^ other)] for other in range(4)]
+            mean = (means[0] + means[1] + means[2] + means[3]) * 0.25
+            spread = squares[0] + squares[1] + squares[2] + squares[3]
+            for each in means:
+                spread = spread + D * (each - mean) * (each - mean)
+            b.stat_rows[0:1, slot_rows(k)] = mean
+            b.stat_rows[1:2, slot_rows(k)] = lax.rsqrt(spread * (1.0 / FF) + EPSILON)
+        b.stat[layer] = b.stat_rows[...].T
+        feed_sibling(layer, 1, 1 - core).wait_recv()
+        branch = None
+        part_copies = []
+        for k in (1, 2, 3, 0):
+            both = b.stat[layer, slot_rows(k), :]
+            inner = (
+                (b.active[slot_rows(k), :] - both[:, 0:1]) * both[:, 1:2] * vec[9:10, :]
+                + vec[11:12, :]
+            ).astype(BF16)
+            part = mul(inner, square(b.wf.at[layer, 1]))
+            if k == 0:
+                branch = part
+            else:
+                b.part_send[k] = part.astype(BF16)
+                part_copies.append(
+                    remote(
+                        b.part_send.at[k],
+                        b.part_recv.at[layer, k],
+                        b.part_s.at[layer, k],
+                        b.part_r.at[layer, k],
+                        "section",
+                        peers[k],
+                    )
+                )
+                part_copies[-1].start()
+        for k in range(1, 4):
+            part_copies[k - 1].wait_recv()
+            branch = branch + b.part_recv[layer, k].astype(F32)
+        b.streams[2 * layer + 1] = (inputs + branch + vec[8:9, :]).astype(BF16)
+        send_sub(2 * layer + 1)
+        for copy in hidden_copies + stat_copies + part_copies:
+            copy.wait_send()
+
+    def stores(layer, chosen):
+        pairs = (
+            (b.wa, b.wa_out),
+            (b.wf, b.wf_out),
+            (b.qkv, b.qkv_out),
+            (b.pa, b.pa_out),
+            (b.pt, b.pt_out),
+            (b.hid, b.hid_out),
+            (b.up, b.up_out),
+            (b.stat, b.stat_out),
+        )
+        return [
+            pltpu.make_async_copy(source.at[layer], target.at[layer], b.store_sem.at[layer, i])
+            for i, (source, target) in enumerate(pairs)
+            if i in chosen
+        ]
+
+    first = b.vecs.at[0]
+    for micro in range(4):
+        unit, unused = standardize(b.embeds[micro].astype(F32))
+        b.hidden[slot_rows(micro), :] = (unit * first[0:1, :] + first[3:4, :]).astype(BF16)
+    block_z_wait(0)
+    block_sibling(0, core).start()
+
+    @pl.when(section == 3)
+    def _():
+        for k in range(1, 4):
+            block_plane(0, k, section).start()
+
+    feed_z_start(0, 0)
+    block_sibling(0, 1 - core).wait_recv()
+
+    def wide_copy(micro, pair):
+        return remote_both(
+            b.proj_send.at[micro, pair],
+            b.qkv.at[0, lax.rem(section, 3), rows_of(me)],
+            b.wide_s.at[micro, pair],
+            b.wide_r.at[lax.rem(section, 3), me],
+            micro,
+            OWNERS[pair],
+        )
+
+    @pl.when(section != 3)
+    def _():
+        bias = jnp.where(section == 2, first[6:7, :], 0.0)
+        for micro in range(4):
+            part = mul(b.hidden[slot_rows(micro), :], square(b.wa.at[0, section])) + bias
+            part = part.astype(BF16)
+            for pair, owner in enumerate(OWNERS):
+                b.proj_send[micro, pair] = part[:, pair * PAIR_LANES : (pair + 1) * PAIR_LANES]
+                local = (section == micro) & (me == owner)
+
+                @pl.when(~local)
+                def _():
+                    wide_copy(micro, pair).start()
+
+                @pl.when(local)
+                def _():
+                    b.qkv[0, section, rows_of(me), :] = b.proj_send[micro, pair]
+
+    @pl.when(is_owner)
+    def _():
+        for block in range(3):
+            for source in range(8):
+
+                @pl.when((section != block) | (me != source))
+                def _():
+                    remote_both(
+                        b.proj_send.at[0, 0],
+                        b.qkv.at[0, block, pl.ds(source * TOKENS, TOKENS)],
+                        b.wide_s.at[0, 0],
+                        b.wide_r.at[block, source],
+                        block,
+                        source,
+                    ).wait_recv()
+
+    feed_z_start(0, 1)
+
+    @pl.when(is_owner)
+    def _():
+        attend(0)
+
+    feed_z_pass(0, 0)
+    for k in range(1, 4):
+
+        @pl.when(peers[k] == 3)
+        def _():
+            block_plane(0, k, peers[k]).wait_recv()
+            block_across(0, k, core).start()
+
+    block_z_start(1)
+    for k in range(1, 4):
+
+        @pl.when(peers[k] == 3)
+        def _():
+            block_across(0, k, 1 - core).wait_recv()
+
+    attention_end(0, b.embeds[section].astype(F32))
+
+    @pl.when(section != 3)
+    def _():
+        for micro in range(4):
+            for pair, owner in enumerate(OWNERS):
+
+                @pl.when((section != micro) | (me != owner))
+                def _():
+                    wide_copy(micro, pair).wait_send()
+
+    def waiting():
+        feed_z_pass(0, 1)
+        pick_up(1)
+
+    def resting():
+        block_z_wait(1)
+        block_sibling(1, core).start()
+        for k in range(1, 4):
+            block_plane(1, k, section).start()
+        feed_z_start(1, 0)
+
+    feed(0, waiting, resting)
+    for copy in stores(0, range(2, 8)):
+        copy.start()
+
+    second = b.vecs.at[1]
+    inputs = b.streams[1].astype(F32)
+    unit, unused = standardize(inputs)
+    own_hidden = (unit * second[0:1, :] + second[3:4, :]).astype(BF16)
+    block_sibling(1, 1 - core).wait_recv()
+    for k in range(1, 4):
+        block_plane(1, k, peers[k]).wait_recv()
+        block_across(1, k, core).start()
+    for k in range(1, 4):
+        block_across(1, k, 1 - core).wait_recv()
+    for block in range(3):
+        part = mul(own_hidden, square(b.wa.at[1, block]))
+        if block == 2:
+            part = part + second[6:7, :]
+        part = part.astype(BF16)
+        for pair in range(PAIRS):
+            b.send[pair, block] = part[:, pair * PAIR_LANES : (pair + 1) * PAIR_LANES]
+
+    def out_copy(pair):
+        return remote(
+            b.send.at[pair],
+            b.qkv.at[1, :, rows_of(me)],
+            b.qkv_s.at[pair],
+            b.qkv_r.at[me],
+            "seq",
+            OWNERS[pair],
+        )
+
+    for pair, owner in enumerate(OWNERS):
+
+        @pl.when(me != owner)
+        def _():
+            out_copy(pair).start()
+
+        @pl.when(me == owner)
+        def _():
+            b.qkv[1, :, rows_of(me), :] = b.send[pair]
+
+    @pl.when(is_owner)
+    def _():
+        for source in range(8):
+
+            @pl.when(me != source)
+            def _():
+                remote(
+                    b.send.at[0],
+                    b.qkv.at[1, :, pl.ds(source * TOKENS, TOKENS)],
+                    b.qkv_s.at[0],
+                    b.qkv_r.at[source],
+                    "seq",
+                    source,
+                ).wait_recv()
+
+    feed_z_start(1, 1)
+
+    @pl.when(section != 3)
+    def _():
+        for k in range(1, 4):
+            block_plane(0, k, section).start()
+
+    @pl.when(is_owner)
+    def _():
+        attend(1)
+
+    feed_z_pass(1, 0)
+    attention_end(1, inputs)
+    for pair, owner in enumerate(OWNERS):
+
+        @pl.when(me != owner)
+        def _():
+            out_copy(pair).wait_send()
+
+    def waiting_last():
+        feed_z_pass(1, 1)
+        for k in range(1, 4):
+
+            @pl.when(peers[k] != 3)
+            def _():
+                block_plane(0, k, peers[k]).wait_recv()
+                block_across(0, k, core).start()
+
+    def resting_last():
+        for copy in stores(1, (0, 2, 3, 4)):
+            copy.start()
+        for k in range(1, 4):
+
+            @pl.when(peers[k] != 3)
+            def _():
+                block_across(0, k, 1 - core).wait_recv()
+
+        for copy in stores(0, (0, 1)):
+            copy.start()
+
+    feed(1, waiting_last, resting_last)
+    for copy in stores(1, (1, 5, 6, 7)):
+        copy.start()
+    for source in range(4):
+
+        @pl.when(section != source)
+        def _():
+            remote(
+                b.streams.at[0],
+                b.sub.at[source],
+                b.sub_s.at[0],
+                b.sub_r.at[source],
+                "section",
+                source,
+            ).wait_recv()
+
+    for number in range(4):
+
+        @pl.when(section != number)
+        def _():
+            sub_copy(number).wait_send()
+
+    for step in range(1, 8):
+        small_copy(step).wait_send()
+    for layer in range(2):
+        block_sibling(layer, core).wait_send()
+        for step in range(1, 4):
+            block_z(layer, step).wait_send()
+            for which in range(2):
+                feed_z(layer, which, step).wait_send()
+        for which in range(2):
+            feed_sibling(layer, which, core).wait_send()
+        for k in range(1, 4):
+            block_plane(layer, k, section).wait_send()
+            block_across(layer, k, core).wait_send()
+        for copy in stores(layer, range(8)):
+            copy.wait()
+
+
+def run_forward(number, lengths, near, far):
+    vmem = pl.BlockSpec(memory_space=pltpu.VMEM)
+    anywhere = pl.BlockSpec(memory_space=pl.ANY)
+    return pl.pallas_call(
+        forward_kernel,
+        name="forward",
+        out_shape=[shaped(out[0], out[1]) for out in FORE_OUT.values()],
+        in_specs=[pl.BlockSpec(memory_space=pltpu.SMEM)]
+        + [vmem] * len(FORE_VMEM)
+        + [anywhere] * len(FORE_ANY),
+        out_specs=[vmem if out[2] else anywhere for out in FORE_OUT.values()],
+        scratch_shapes=[pltpu.VMEM(item[0], item[1]) for item in FORE_SCRATCH.values()]
+        + [pltpu.SemaphoreType.DMA(item) for item in FORE_SEMS.values()],
+        compiler_params=pltpu.CompilerParams(
+            collective_id=number, has_side_effects=True, vmem_limit_bytes=KERNEL_VMEM_BYTES
+        ),
+        cost_estimate=pl.CostEstimate(
+            flops=10**10, bytes_accessed=100_000_000, transcendentals=0
+        ),
+    )(lengths, *near, *far)
+
+
+BACK_VMEM = dict(cotangent=0, embeds=0, x_in=0, att=0, vecs=0, picks=0, logs=0)
+BACK_ANY = dict(
+    wa_in=0, wf_in=0, qkv_in=0, pa_in=0, pt_in=0, hid_in=0, up_in=0, stat_in=0
+)
+BACK_OUT = dict(
+    sub=((4, TOKENS, D), BF16, True),
+    qkv_out=((2, SHARD, 3 * D), F32, False),
+    out_out=((2, SHARD, D), F32, False),
+    up_out=((2, SHARD, FF), F32, False),
+    down_out=((2, 4 * SHARD, D), F32, False),
+    gain_out=((2, 3, SHARD), F32, True),
+    bias_out=((2, 6, SHARD), F32, True),
+    hidden_out=((2, 3, 4 * SHARD), F32, True),
+    means_out=((2, 5), F32, True),
+)
+BACK_SCRATCH = dict(
+    wa=((4, 4, 2, SHARD, D), BF16),
+    wf=((2, 4, 2, SHARD, D), BF16),
+    qkv=((3, GROUP_TOKENS, PAIR_LANES), BF16),
+    pa=((GROUP_TOKENS, PAIR_LANES), F32),
+    pt=((GROUP_TOKENS, PAIR_LANES), F32),
+    hid=((WIDE, D), BF16),
+    up=((WIDE, D), F32),
+    stat=((WIDE, PAIR_LANES), F32),
+    streams=((4, TOKENS, D), BF16),
+    grads=((WIDE, D), BF16),
+    units=((WIDE, D), F32),
+    unit_grads=((WIDE, D), F32),
+    inners=((WIDE, D), BF16),
+    lows=((WIDE, D), BF16),
+    columns=((WIDE, PAIR_LANES), F32),
+    stat_rows=((PAIR_LANES, WIDE), F32),
+    part_send=((4, TOKENS, D), BF16),
+    part_recv=((4, TOKENS, D), BF16),
+    stat_send=((8, WIDE), F32),
+    stat_recv=((4, 8, WIDE), F32),
+    do_send=((PAIRS, TOKENS, PAIR_LANES), BF16),
+    do_recv=((GROUP_TOKENS, PAIR_LANES), BF16),
+    key_sum=((GROUP_TOKENS, PAIR_LANES), F32),
+    value_sum=((GROUP_TOKENS, PAIR_LANES), F32),
+    d_send=((GROUP_TOKENS, 3 * PAIR_LANES), BF16),
+    d_recv=((PAIRS, TOKENS, 3 * PAIR_LANES), BF16),
+    left_src=((2, TOKENS, D), BF16),
+    right_src=((4, TOKENS, D), BF16),
+    left=((WIDE, D), BF16),
+    right=((WIDE, D), BF16),
+    vec_rows=((2, PAIR_LANES, D), F32),
+    prod_f=((4, 2, 4, SHARD, D), BF16),
+    prod_a=((2, 2, 4, SHARD, D + PAIR_LANES), BF16),
+    pair_f=((4, 4, SHARD, D), BF16),
+    pair_a=((2, 4, SHARD, D + PAIR_LANES), BF16),
+    line_f=((4, 3, SHARD, D), BF16),
+    line_a=((2, 3, SHARD, D + PAIR_LANES), BF16),
+    all_f=((4, 4, SHARD, D), BF16),
+    all_a=((2, 4, SHARD, D + PAIR_LANES), BF16),
+    stage_a=((SHARD, 4 * D), F32),
+    stage_u=((SHARD, FF), F32),
+    stage_d=((4 * SHARD, D), F32),
+    log_line=((8, 8, PAIR_LANES), F32),
+    log_plane=((4, 8, PAIR_LANES), F32),
+)
+BACK_SEMS = dict(
+    load_sem=(16,),
+    store_sem=(4,),
+    g_s=(2, 4),
+    g_r=(2, 4),
+    stat_s=(2, 4),
+    stat_r=(2, 4),
+    part_s=(2, 4),
+    part_r=(2, 4),
+    do_s=(2, PAIRS),
+    do_r=(2, 8),
+    d_s=(2, 8),
+    d_r=(2, PAIRS),
+    left_s=(2, 4),
+    left_r=(2, 4),
+    right_s=(2, 4),
+    right_r=(2, 4),
+    sub_s=(4,),
+    sub_r=(4,),
+    pair_s=(6,),
+    pair_r=(6,),
+    line_s=(6, 3),
+    line_r=(6, 3),
+    all_s=(6, 4),
+    all_r=(6, 4),
+    log_s=(8,),
+    log_r=(8,),
+    log_plane_s=(4,),
+    log_plane_r=(4,),
+)
+
+
+def backward_kernel(*refs):
+    b = Named([BACK_VMEM, BACK_ANY, BACK_OUT, BACK_SCRATCH, BACK_SEMS], refs)
+    me = lax.axis_index("seq")
+    section = lax.axis_index("section")
+    peers = plane_peers(section)
+    core = lax.rem(me, 2)
+    chip = lax.div(me, 2)
+    sibling = me + 1 - 2 * core
+    is_owner = (me != 1) & (me != 7)
+    my_pair = jnp.where(me == 0, 0, me - 1)
+    my_pair = jnp.where(my_pair > PAIRS - 1, PAIRS - 1, my_pair)
+
+    barrier = pltpu.get_barrier_semaphore()
+    for peer in seq_peers(me, 8):
+        pl.semaphore_signal(
+            barrier, inc=1, device_id={"seq": peer}, device_id_type=pl.DeviceIdType.MESH
+        )
+    for peer in peers[1:]:
+        pl.semaphore_signal(
+            barrier, inc=1, device_id={"section": peer}, device_id_type=pl.DeviceIdType.MESH
+        )
+
+    def loads(layer, first, pairs):
+        return [
+            pltpu.make_async_copy(
+                source.at[layer], target, b.load_sem.at[8 * layer + first + number]
+            )
+            for number, (source, target) in enumerate(pairs)
+        ]
+
+    def feed_loads(layer):
+        pairs = ((b.wf_in, b.wf), (b.hid_in, b.hid), (b.up_in, b.up), (b.stat_in, b.stat))
+        return loads(layer, 0, pairs)
+
+    def attention_loads(layer):
+        pairs = ((b.wa_in, b.wa), (b.qkv_in, b.qkv), (b.pa_in, b.pa), (b.pt_in, b.pt))
+        return loads(layer, 4, pairs)
+
+    for copy in feed_loads(1) + attention_loads(1):
+        copy.start()
+    b.log_line[me] = b.logs[...]
+    pl.semaphore_wait(barrier, 10)
+
+    def log_copy(step):
+        return remote(
+            b.logs,
+            b.log_line.at[me],
+            b.log_s.at[step],
+            b.log_r.at[step],
+            "seq",
+            lax.rem(me + step, 8),
+        )
+
+    def log_plane_copy(k, slot):
+        return remote(
+            b.log_plane.at[slot],
+            b.log_plane.at[slot],
+            b.log_plane_s.at[k],
+            b.log_plane_r.at[k],
+            "section",
+            peers[k],
+        )
+
+    def sum_logs():
+        for step in range(1, 8):
+            source = lax.rem(me + 8 - step, 8)
+            remote(
+                b.logs,
+                b.log_line.at[source],
+                b.log_s.at[step],
+                b.log_r.at[step],
+                "seq",
+                source,
+            ).wait_recv()
+        total = b.log_line[0]
+        for j in range(1, 8):
+            total = total + b.log_line[j]
+        b.log_plane[section] = total
+        for k in range(1, 4):
+            log_plane_copy(k, section).start()
+
+    def finish_logs():
+        for k in range(1, 4):
+            log_plane_copy(k, peers[k]).wait_recv()
+        total = b.log_plane[0]
+        for other in range(1, 4):
+            total = total + b.log_plane[other]
+        lane = lax.broadcasted_iota(jnp.int32, (8, PAIR_LANES), 1)
+        number = lax.shift_right_logical(lane, 2)
+        lines = jnp.zeros((8, PAIR_LANES), F32)
+        for i in range(5):
+            part = jnp.sum(jnp.where(number == i, total, 0.0), -1, keepdims=True)
+            lines = lines + jnp.where(lane == i, part, 0.0)
+        means = lines[0:2, :] / jnp.where(lane[0:2, :] < 5, lines[2:3, :], 1.0)
+        b.means_out[...] = means[:, 0:5]
+        for step in range(1, 8):
+            log_copy(step).wait_send()
+        for k in range(1, 4):
+            log_plane_copy(k, section).wait_send()
+
+    for step in range(1, 8):
+        log_copy(step).start()
+
+    def matrix(number):
+        layer, which = divmod(number, 3)
+        if which == 2:
+            return (b.prod_a, b.pair_a, b.line_a, b.all_a, layer, D + PAIR_LANES)
+        return (b.prod_f, b.pair_f, b.line_f, b.all_f, 2 * layer + which, D)
+
+    def store_product(number, value):
+        prod, unused_pair, unused_line, unused_all, i, unused_width = matrix(number)
+        for j in range(8):
+            prod[i, j % 2, j // 2, :, 0:D] = value[j * SHARD : (j + 1) * SHARD, :].astype(BF16)
+
+    def pair_copy(number):
+        prod, pair, unused_line, unused_all, i, unused_width = matrix(number)
+        return remote(
+            prod.at[i, 1 - core],
+            pair.at[i],
+            b.pair_s.at[number],
+            b.pair_r.at[number],
+            "seq",
+            sibling,
+        )
+
+    def line_copy(number, step):
+        prod, unused_pair, line, unused_all, i, unused_width = matrix(number)
+        target = lax.rem(chip + step, 4)
+        return remote(
+            prod.at[i, core, target],
+            line.at[i, step - 1],
+            b.line_s.at[number, step - 1],
+            b.line_r.at[number, step - 1],
+            "seq",
+            2 * target + core,
+        )
+
+    def all_copy(number, k, slot):
+        unused_prod, unused_pair, unused_line, whole, i, unused_width = matrix(number)
+        return remote(
+            whole.at[i, slot],
+            whole.at[i, slot],
+            b.all_s.at[number, k],
+            b.all_r.at[number, k],
+            "section",
+            peers[k],
+        )
+
+    def sum_pair(number):
+        prod, pair, unused_line, unused_all, i, unused_width = matrix(number)
+        pair_copy(number).wait_recv()
+        for block in range(4):
+            prod[i, core, block] = (
+                prod[i, core, block].astype(F32) + pair[i, block].astype(F32)
+            ).astype(BF16)
+        for step in range(1, 4):
+            line_copy(number, step).start()
+
+    def sum_line(number):
+        prod, unused_pair, line, whole, i, unused_width = matrix(number)
+        total = prod[i, core, chip].astype(F32)
+        for step in range(1, 4):
+            line_copy(number, step).wait_recv()
+            total = total + line[i, step - 1].astype(F32)
+        whole[i, section] = total.astype(BF16)
+        for k in range(1, 4):
+            all_copy(number, k, section).start()
+
+    def store_copies(number):
+        layer, which = divmod(number, 3)
+        if which == 2:
+            return [
+                pltpu.make_async_copy(
+                    b.stage_a.at[:, pl.ds(0, 3 * D)], b.qkv_out.at[1 - layer], b.store_sem.at[0]
+                ),
+                pltpu.make_async_copy(
+                    b.stage_a.at[:, pl.ds(3 * D, D)], b.out_out.at[1 - layer], b.store_sem.at[1]
+                ),
+            ]
+        if which == 0:
+            return [pltpu.make_async_copy(b.stage_u, b.up_out.at[1 - layer], b.store_sem.at[2])]
+        return [pltpu.make_async_copy(b.stage_d, b.down_out.at[1 - layer], b.store_sem.at[3])]
+
+    def finish(number):
+        unused_prod, unused_pair, unused_line, whole, i, unused_width = matrix(number)
+        layer, which = divmod(number, 3)
+        for k in range(1, 4):
+            all_copy(number, k, peers[k]).wait_recv()
+        if layer == 1:
+            for copy in store_copies(number - 3):
+                copy.wait()
+        if which == 1:
+            for source in range(4):
+                b.stage_d[source * SHARD : (source + 1) * SHARD, :] = whole[i, source].astype(F32)
+        elif which == 0:
+            for j in range(8):
+                b.stage_u[:, j * 4 * SHARD : (j + 1) * 4 * SHARD] = jnp.concatenate(
+                    [
+                        whole[i, source, :, j * SHARD : (j + 1) * SHARD].astype(F32)
+                        for source in range(4)
+                    ],
+                    1,
+                )
+        else:
+            for source in range(4):
+                b.stage_a[:, source * D : (source + 1) * D] = whole[i, source, :, 0:D].astype(F32)
+            lines = []
+            for source in range(4):
+                tail = whole[i, source, :, D : D + PAIR_LANES].astype(F32)
+                tail = jnp.concatenate([tail, jnp.zeros((PAIR_LANES - SHARD, PAIR_LANES), F32)], 0)
+                lines.append(tail.T)
+            model = lines[0] + lines[1] + lines[2] + lines[3]
+            b.gain_out[1 - layer] = model[0:3, 0:SHARD]
+            b.bias_out[1 - layer] = model[3:9, 0:SHARD]
+            b.hidden_out[1 - layer] = jnp.concatenate([each[9:12, 0:SHARD] for each in lines], 1)
+        for copy in store_copies(number):
+            copy.start()
+
+    def sub_copy(number):
+        return remote(
+            b.streams.at[number],
+            b.sub.at[section],
+            b.sub_s.at[number],
+            b.sub_r.at[section],
+            "section",
+            number,
+        )
+
+    def send_sub(number):
+        @pl.when(section != number)
+        def _():
+            sub_copy(number).start()
+
+        @pl.when(section == number)
+        def _():
+            b.sub[section] = b.streams[number]
+
+    def feed_phase(layer, grad_ref, x_ref, early, middle, late):
+        phase = 1 - layer
+        vec = b.vecs.at[layer]
+        rows = b.vec_rows.at[layer]
+        up_number = 3 * phase
+        down_number = 3 * phase + 1
+        b.grads[slot_rows(0), :] = grad_ref[...]
+        grad_copies = [
+            remote(
+                b.grads.at[pl.ds(0, TOKENS)],
+                b.grads.at[pl.ds(k * TOKENS, TOKENS)],
+                b.g_s.at[phase, k],
+                b.g_r.at[phase, k],
+                "section",
+                peers[k],
+            )
+            for k in range(1, 4)
+        ]
+        for copy in grad_copies:
+            copy.start()
+        rows[...] = jnp.zeros((PAIR_LANES, D), F32)
+        early()
+        for copy in feed_loads(layer):
+            copy.wait()
+        gain_sum = jnp.zeros((1, D), F32)
+        bias_sum = jnp.zeros((1, D), F32)
+        for k in range(4):
+            both = b.stat[slot_rows(k), :]
+            upward = b.up[slot_rows(k), :]
+            values, below = gelu_parts(upward)
+            b.up[slot_rows(k), :] = below + upward * (
+                jnp.exp(-0.5 * upward * upward) * (0.5 / 3.141592653589793) ** 0.5
+            )
+            unit = (values - both[:, 0:1]) * both[:, 1:2]
+            b.units[slot_rows(k), :] = unit
+            b.inners[slot_rows(k), :] = (unit * vec[9:10, :] + vec[11:12, :]).astype(BF16)
+            if k > 0:
+                grad_copies[k - 1].wait_recv()
+            inner_grad = mul_nt(b.grads[slot_rows(k), :], square(b.wf.at[1]))
+            gain_sum = gain_sum + jnp.sum(inner_grad * unit, 0, keepdims=True)
+            bias_sum = bias_sum + jnp.sum(inner_grad, 0, keepdims=True)
+            unit_grad = inner_grad * vec[9:10, :]
+            b.unit_grads[slot_rows(k), :] = unit_grad
+            b.columns[slot_rows(k), :] = two_columns(
+                jnp.sum(unit_grad, -1, keepdims=True), jnp.sum(unit_grad * unit, -1, keepdims=True)
+            )
+        stat_copies = share_stats(
+            b.columns[...],
+            b.stat_send,
+            b.stat_recv,
+            b.stat_s.at[phase],
+            b.stat_r.at[phase],
+            peers,
+        )
+        rows[9:10, :] = gain_sum
+        rows[11:12, :] = bias_sum
+        store_product(down_number, mul_tn(b.inners[...], b.grads[...]))
+        pair_copy(down_number).start()
+        middle()
+        for copy in stat_copies:
+            copy.wait_recv()
+        b.stat_rows[...] = jnp.zeros((PAIR_LANES, WIDE), F32)
+        for k in range(4):
+            for line in range(2):
+                parts = [
+                    b.stat_recv[source, line : line + 1, slot_rows(k ^ source)]
+                    for source in range(4)
+                ]
+                b.stat_rows[line : line + 1, slot_rows(k)] = (
+                    parts[0] + parts[1] + parts[2] + parts[3]
+                ) * (1.0 / FF)
+        b.columns[...] = b.stat_rows[...].T
+        hidden_grad = None
+        low_sum = jnp.zeros((1, D), F32)
+        part_copies = []
+        for k in (1, 2, 3, 0):
+            rstd = b.stat[slot_rows(k), :][:, 1:2]
+            both = b.columns[slot_rows(k), :]
+            low = (
+                rstd
+                * (
+                    b.unit_grads[slot_rows(k), :]
+                    - both[:, 0:1]
+                    - b.units[slot_rows(k), :] * both[:, 1:2]
+                )
+                * b.up[slot_rows(k), :]
+            ).astype(BF16)
+            b.lows[slot_rows(k), :] = low
+            low_sum = low_sum + jnp.sum(low.astype(F32), 0, keepdims=True)
+            part = mul_nt(low, square(b.wf.at[0]))
+            if k == 0:
+                hidden_grad = part
+            else:
+                b.part_send[k] = part.astype(BF16)
+                part_copies.append(
+                    remote(
+                        b.part_send.at[k],
+                        b.part_recv.at[k],
+                        b.part_s.at[phase, k],
+                        b.part_r.at[phase, k],
+                        "section",
+                        peers[k],
+                    )
+                )
+                part_copies[-1].start()
+        rows[10:11, :] = low_sum
+        store_product(up_number, mul_tn(b.hid[...], b.lows[...]))
+        pair_copy(up_number).start()
+        unit, rstd = standardize(x_ref[...].astype(F32))
+        for k in range(1, 4):
+            part_copies[k - 1].wait_recv()
+            hidden_grad = hidden_grad + b.part_recv[k].astype(F32)
+        grad = grad_ref[...].astype(F32)
+        number = 2 * layer + 1
+        b.streams[number] = (
+            grad + norm_back(unit, rstd, hidden_grad * vec[2:3, :])
+        ).astype(BF16)
+        rows[2:3, :] = jnp.sum(hidden_grad * unit, 0, keepdims=True)
+        rows[5:6, :] = jnp.sum(hidden_grad, 0, keepdims=True)
+        rows[8:9, :] = jnp.sum(grad, 0, keepdims=True)
+        for copy in grad_copies + stat_copies + part_copies:
+            copy.wait_send()
+        late()
+
+    def attention_phase(layer, grad_ref, x_ref, att_ref, before, inside, after):
+        phase = 1 - layer
+        vec = b.vecs.at[layer]
+        rows = b.vec_rows.at[layer]
+        grad = grad_ref[...]
+        inner_unit, inner_rstd = standardize(att_ref[...].astype(F32))
+        attention_ready = attention_loads(layer)
+        attention_ready[0].wait()
+        inner_grad = mul_nt(grad, square(b.wa.at[3]))
+        att_grad = norm_back(inner_unit, inner_rstd, inner_grad * vec[1:2, :]).astype(BF16)
+        for pair in range(PAIRS):
+            b.do_send[pair] = att_grad[:, pair * PAIR_LANES : (pair + 1) * PAIR_LANES]
+
+        def out_copy(pair):
+            return remote(
+                b.do_send.at[pair],
+                b.do_recv.at[rows_of(me)],
+                b.do_s.at[phase, pair],
+                b.do_r.at[phase, me],
+                "seq",
+                OWNERS[pair],
+            )
+
+        for pair, owner in enumerate(OWNERS):
+
+            @pl.when(me != owner)
+            def _():
+                out_copy(pair).start()
+
+            @pl.when(me == owner)
+            def _():
+                b.do_recv[rows_of(me), :] = b.do_send[pair]
+
+        def left_copy(k):
+            return remote(
+                b.left_src.at[lax.div(peers[k], 3)],
+                b.left.at[pl.ds(k * TOKENS, TOKENS)],
+                b.left_s.at[phase, k],
+                b.left_r.at[phase, k],
+                "section",
+                peers[k],
+            )
+
+        def right_copy(k):
+            return remote(
+                b.right_src.at[peers[k]],
+                b.right.at[pl.ds(k * TOKENS, TOKENS)],
+                b.right_s.at[phase, k],
+                b.right_r.at[phase, k],
+                "section",
+                peers[k],
+            )
+
+        unit, rstd = standardize(x_ref[...].astype(F32))
+        b.left_src[0] = (unit * vec[0:1, :] + vec[3:4, :]).astype(BF16)
+        b.left_src[1] = (inner_unit * vec[1:2, :] + vec[4:5, :]).astype(BF16)
+        b.right_src[3] = grad
+        for k in range(1, 4):
+            left_copy(k).start()
+
+            @pl.when(peers[k] == 3)
+            def _():
+                right_copy(k).start()
+
+        b.left[slot_rows(0), :] = b.left_src[lax.div(section, 3)]
+        rows[1:2, :] = jnp.sum(inner_grad * inner_unit, 0, keepdims=True)
+        rows[4:5, :] = jnp.sum(inner_grad, 0, keepdims=True)
+        rows[7:8, :] = jnp.sum(grad.astype(F32), 0, keepdims=True)
+        for copy in attention_ready[1:]:
+            copy.wait()
+
+        def back_copy(target):
+            return remote(
+                b.d_send.at[pl.ds(target * TOKENS, TOKENS)],
+                b.d_recv.at[my_pair],
+                b.d_s.at[phase, target],
+                b.d_r.at[phase, my_pair],
+                "seq",
+                target,
+            )
+
+        @pl.when(is_owner)
+        def _():
+            for source in range(8):
+
+                @pl.when(me != source)
+                def _():
+                    remote(
+                        b.do_send.at[0],
+                        b.do_recv.at[pl.ds(source * TOKENS, TOKENS)],
+                        b.do_s.at[phase, 0],
+                        b.do_r.at[phase, source],
+                        "seq",
+                        source,
+                    ).wait_recv()
+
+        before()
+
+        @pl.when(is_owner)
+        def _():
+            b.key_sum[...] = jnp.zeros((GROUP_TOKENS, PAIR_LANES), F32)
+            b.value_sum[...] = jnp.zeros((GROUP_TOKENS, PAIR_LANES), F32)
+            lane = lax.broadcasted_iota(jnp.int32, (QUERY_STEP, PAIR_LANES), 1)
+            first_half = lane < HEAD_DIM
+            for step in reversed(range(GROUP_TOKENS // QUERY_STEP)):
+                start = step * QUERY_STEP
+                keys_end = start + QUERY_STEP
+                block = slice(start, keys_end)
+                plain_query = b.qkv[0, block, :]
+                query = plain_query * jnp.asarray(SCALE, BF16)
+                keys = b.qkv[1, 0:keys_end, :]
+                values = b.qkv[2, 0:keys_end, :]
+                causal = lax.broadcasted_iota(jnp.int32, (QUERY_STEP, keys_end), 1) <= (
+                    start + lax.broadcasted_iota(jnp.int32, (QUERY_STEP, keys_end), 0)
+                )
+                head_grad = b.do_recv[block, :]
+                inverse = 1.0 / b.pt[block, :]
+                head_float = head_grad.astype(F32)
+                products = head_float * b.pa[block, :]
+                scaled = (head_float * inverse).astype(BF16)
+                key_lanes = lax.broadcasted_iota(jnp.int32, (keys_end, PAIR_LANES), 1) < HEAD_DIM
+                query_parts = []
+                key_parts = []
+                value_parts = []
+                for head in range(2):
+                    mine = first_half if head == 0 else ~first_half
+                    own_query = jnp.where(mine, query, jnp.zeros_like(query))
+                    own_grad = jnp.where(mine, head_grad, jnp.zeros_like(head_grad))
+                    delta = jnp.sum(jnp.where(mine, products, 0.0), -1, keepdims=True)
+                    own_inverse = jnp.max(jnp.where(mine, inverse, 0.0), -1, keepdims=True)
+                    counts = mul_nt(b.picks[head, block, :], b.picks[head, 0:keys_end, :])
+                    scores = mul_nt(own_query, keys)
+                    weighted = jnp.where(causal, jnp.exp(scores) * counts, 0.0)
+                    prob_grad = mul_nt(own_grad, values)
+                    score_grad = (weighted * own_inverse * (prob_grad - delta)).astype(BF16)
+                    query_parts.append(mul(score_grad, keys))
+                    key_parts.append(mul_tn(score_grad, plain_query))
+                    value_parts.append(mul_tn(weighted.astype(BF16), scaled))
+                b.key_sum[0:keys_end, :] += jnp.where(key_lanes, key_parts[0], key_parts[1])
+                b.value_sum[0:keys_end, :] += jnp.where(key_lanes, value_parts[0], value_parts[1])
+                query_grad = jnp.where(first_half, query_parts[0], query_parts[1]) * SCALE
+                b.d_send[block, 0:PAIR_LANES] = query_grad.astype(BF16)
+                b.d_send[block, PAIR_LANES : 2 * PAIR_LANES] = (
+                    b.key_sum[block, :] * SCALE
+                ).astype(BF16)
+                b.d_send[block, 2 * PAIR_LANES : 3 * PAIR_LANES] = b.value_sum[block, :].astype(
+                    BF16
+                )
+                for target in (2 * step, 2 * step + 1):
+
+                    @pl.when(me != target)
+                    def _():
+                        back_copy(target).start()
+
+                    @pl.when(me == target)
+                    def _():
+                        b.d_recv[my_pair] = b.d_send[target * TOKENS : (target + 1) * TOKENS, :]
+
+        inside()
+        for pair, owner in enumerate(OWNERS):
+
+            @pl.when(me != owner)
+            def _():
+                remote(
+                    b.d_send.at[pl.ds(0, TOKENS)],
+                    b.d_recv.at[pair],
+                    b.d_s.at[phase, 0],
+                    b.d_r.at[phase, pair],
+                    "seq",
+                    owner,
+                ).wait_recv()
+
+            for third in range(3):
+                b.right_src[third, :, pair * PAIR_LANES : (pair + 1) * PAIR_LANES] = b.d_recv[
+                    pair, :, third * PAIR_LANES : (third + 1) * PAIR_LANES
+                ]
+        for k in range(1, 4):
+
+            @pl.when(peers[k] != 3)
+            def _():
+                right_copy(k).start()
+
+        b.right[slot_rows(0), :] = b.right_src[section]
+        hidden_grad = mul_nt(b.right_src[0], square(b.wa.at[0]))
+        for third in range(1, 3):
+            hidden_grad = hidden_grad + mul_nt(b.right_src[third], square(b.wa.at[third]))
+        b.streams[2 * layer] = (
+            grad.astype(F32) + norm_back(unit, rstd, hidden_grad * vec[0:1, :])
+        ).astype(BF16)
+        rows[0:1, :] = jnp.sum(hidden_grad * unit, 0, keepdims=True)
+        rows[3:4, :] = jnp.sum(hidden_grad, 0, keepdims=True)
+        rows[6:7, :] = jnp.sum(b.right_src[2].astype(F32), 0, keepdims=True)
+        for k in range(1, 4):
+            left_copy(k).wait_recv()
+        after()
+
+        def weights_part():
+            for k in range(1, 4):
+                right_copy(k).wait_recv()
+            number = 3 * phase + 2
+            store_product(number, mul_tn(b.left[...], b.right[...]))
+            tail = rows[...].T.astype(BF16)
+            for j in range(8):
+                b.prod_a[phase, j % 2, j // 2, :, D : D + PAIR_LANES] = tail[
+                    j * SHARD : (j + 1) * SHARD, :
+                ]
+            pair_copy(number).start()
+            for k in range(1, 4):
+                left_copy(k).wait_send()
+                right_copy(k).wait_send()
+            for pair, owner in enumerate(OWNERS):
+
+                @pl.when(me != owner)
+                def _():
+                    out_copy(pair).wait_send()
+
+            @pl.when(is_owner)
+            def _():
+                for target in range(8):
+
+                    @pl.when(me != target)
+                    def _():
+                        back_copy(target).wait_send()
+
+        return weights_part
+
+    def nothing():
+        pass
+
+    UP1, DOWN1, ATT1, UP0, DOWN0, ATT0 = range(6)
+
+    def next_feed():
+        for copy in feed_loads(0):
+            copy.start()
+
+    feed_phase(1, b.cotangent.at[section], b.x_in.at[2], nothing, nothing, next_feed)
+    send_sub(3)
+    deferred = attention_phase(
+        1,
+        b.streams.at[3],
+        b.x_in.at[1],
+        b.att.at[1],
+        lambda: sum_pair(DOWN1),
+        lambda: sum_pair(UP1),
+        lambda: [copy.start() for copy in attention_loads(0)],
+    )
+    send_sub(2)
+
+    def early():
+        deferred()
+        sum_line(DOWN1)
+        sum_logs()
+
+    def late():
+        sum_line(UP1)
+        finish(DOWN1)
+
+    feed_phase(0, b.streams.at[2], b.x_in.at[0], early, lambda: sum_pair(ATT1), late)
+    send_sub(1)
+
+    def before():
+        sum_pair(DOWN0)
+        sum_line(ATT1)
+
+    def inside():
+        sum_pair(UP0)
+        finish(UP1)
+        finish_logs()
+
+    deferred = attention_phase(
+        0, b.streams.at[1], b.embeds.at[section], b.att.at[0], before, inside, nothing)
+    send_sub(0)
+    deferred()
+    sum_line(DOWN0)
+    sum_pair(ATT0)
+    sum_line(UP0)
+    finish(ATT1)
+    finish(DOWN0)
+    finish(UP0)
+    sum_line(ATT0)
+    finish(ATT0)
+    for source in range(4):
+
+        @pl.when(section != source)
+        def _():
+            remote(
+                b.streams.at[0],
+                b.sub.at[source],
+                b.sub_s.at[0],
+                b.sub_r.at[source],
+                "section",
+                source,
+            ).wait_recv()
+
+    for number in range(4):
+
+        @pl.when(section != number)
+        def _():
+            sub_copy(number).wait_send()
+
+    for number in range(6):
+        pair_copy(number).wait_send()
+        for step in range(1, 4):
+            line_copy(number, step).wait_send()
+        for k in range(1, 4):
+            all_copy(number, k, section).wait_send()
+    for number in (UP0, DOWN0, ATT0):
+        for copy in store_copies(number):
+            copy.wait()
+
+
+def run_backward(number, near, far):
+    vmem = pl.BlockSpec(memory_space=pltpu.VMEM)
+    anywhere = pl.BlockSpec(memory_space=pl.ANY)
+    return pl.pallas_call(
+        backward_kernel,
+        name="backward",
+        out_shape=[shaped(out[0], out[1]) for out in BACK_OUT.values()],
+        in_specs=[vmem] * len(BACK_VMEM) + [anywhere] * len(BACK_ANY),
+        out_specs=[vmem if out[2] else anywhere for out in BACK_OUT.values()],
+        scratch_shapes=[pltpu.VMEM(item[0], item[1]) for item in BACK_SCRATCH.values()]
+        + [pltpu.SemaphoreType.DMA(item) for item in BACK_SEMS.values()],
+        compiler_params=pltpu.CompilerParams(
+            collective_id=number, has_side_effects=True, vmem_limit_bytes=KERNEL_VMEM_BYTES
+        ),
+        cost_estimate=pl.CostEstimate(
+            flops=10**10, bytes_accessed=100_000_000, transcendentals=0
+        ),
+    )(*near, *far)
+
+
+def quick_body(
+    embeds,
+    row_lengths,
+    qkv_weight,
+    out_weight,
+    up_weight,
+    down_weight,
+    model_gains,
+    model_biases,
+    hidden_gains,
+    hidden_biases,
+    cotangent,
+):
+    fore = Named(
+        [FORE_OUT],
+        run_forward(
+            10,
+            row_lengths,
+            (embeds, model_gains, model_biases, hidden_gains, hidden_biases),
+            (qkv_weight, out_weight, up_weight, down_weight),
+        ),
+    )
+    back = Named(
+        [BACK_OUT],
+        run_backward(
+            20,
+            (cotangent, embeds, fore.streams, fore.att, fore.vecs, fore.picks, fore.logs),
+            (
+                fore.wa_out,
+                fore.wf_out,
+                fore.qkv_out,
+                fore.pa_out,
+                fore.pt_out,
+                fore.hid_out,
+                fore.up_out,
+                fore.stat_out,
+            ),
+        ),
+    )
+    return (
+        fore.sub[None],
+        back.sub[None],
+        back.qkv_out,
+        back.out_out,
+        back.up_out,
+        back.down_out,
+        back.gain_out,
+        back.bias_out,
+        back.hidden_out[:, 0],
+        back.hidden_out[:, 1:3],
+        back.means_out,
+    )
+
+
+def fits_quick(mesh):
+    return mesh.shape["section"] == 4 and mesh.shape["seq"] == 8
+
+
 def solution(mesh):
     return jax.shard_map(
-        body,
+        quick_body if fits_quick(mesh) else body,
         mesh=mesh,
         in_specs=(
             P(None, "seq", None),

time: 3570 us -> 449 us (0.13)
  waiting for transfers between devices: 2730 us -> 0 us
  Pallas kernels: 0 us -> 422 us
  matrix products: 250 us -> 0 us
  local copies, waits for them, and re-layouts: 251 us -> 17.8 us
  blocking collectives: 127 us -> 0 us
  other arithmetic: 112 us -> 0 us
    reduce_scatter x11 -> x0, waiting for transfers between devices: 1320 us -> none  [the longest x7 1010 us: backward_tick(): lax.psum_scatter(middle[3], 'seq', scatter_dimension=0, tiled=True)]
    all_gather x18 -> x0, waiting for transfers between devices: 673 us -> none  [the longest x7 292 us: backward_tick(): all_keys = lax.all_gather(projected[:, D:], 'seq', axis=0, tiled=True)]
    ppermute x14 -> x0, waiting for transfers between devices: 625 us -> none  [passed_along(): lax.ppermute(value, axis, [(source, source + steps) for source in range(i...]
    pallas_call x0 -> x2, Pallas kernels: none -> 422 us  [the longest x1 221 us: run_forward(): pl.pallas_call(forward_kernel, name='forward', out_shape=[shaped(out[0],...]
    dot_general x49 -> x0, matrix products: 250 us -> none  [the longest x7 62.6 us: feed_backward(): jnp.einsum('tf,td->fd', inner_norm, grad_out, preferred_element_type=jnp....]
    psum x1 -> x0, waiting for transfers between devices: 87.6 us -> none  [body(): lax.psum(placed[0].astype(jnp.bfloat16), 'section').astype(jnp.float32)]
    dynamic_slice x64 -> x0, local copies, waits for them, and re-layouts: 63.8 us -> none  [the longest x42 41.1 us: keep_slot(): previous = lax.dynamic_index_in_dim(store, slot_id, 0, False)]
    all_gather x4 -> x0, blocking collectives: 54.8 us -> none  [the longest x1 15.2 us: body(): lax.all_gather(pick_layer(model_biases), 'seq', axis=1, tiled=True)]
  transfers between devices with their start and end apart: 47 -> 0, of which waited for: 44 -> 0; matrix products, arithmetic and copies ran while one was open for 2% -> 0% of each run, Pallas kernels for 0% -> 0%
where the time goes in v2:
time: 449 us; the launch traced here: 441 us
  Pallas kernels  422 us (94%)
  local copies, waits for them, and re-layouts  17.8 us (4%)
    pallas_call x1, Pallas kernels, run_forward(): pl.pallas_call(forward_kernel, name='forward', out_shape=[shaped(out[0],...  221 us
    pallas_call x1, Pallas kernels, run_backward(): pl.pallas_call(backward_kernel, name='backward', out_shape=[shaped(out[0]...  201 us
    unnamed x24, local copies, waits for them, and re-layouts  15.8 us

profile of v2, /device:TPU:14, one launch (start us, length us, event | category | flops | bytes accessed | tf_op | source)
XLA Modules:
  0.0 440.9 jit_solution(11516665495544213841)
XLA Ops:
  0.6 1.3 copy.22.refs_1_
  1.9 1.3 copy.23.refs_2_
  3.2 221.3 %forward.1 = (bf16[4,128,768]{2,1,0:T(8,128)(2,1)}, bf16[4,128,768]{2,1,0:T(8,128)(2,1)}, bf16[2,128,768]{2,1,0:T(8,128)(2,1)}, f32[2,16,768]{2,1,0:T(8,128)}, b...) custom-call(s32[4,4]{1,0:T(4,128)} %lengths.1, ...), custom_call_target="tpu_custom_call" | custom-call | flops 10000000000 | bytes 100000000 | tf_op jit(solution)/shard_map/forward/pallas_call | solution.py:1523
  224.5 0.0 copy-start.3
  224.5 200.5 %backward.1 = (bf16[4,128,768]{2,1,0:T(8,128)(2,1)}, f32[2,96,2304]{2,1,0:T(8,128)}, f32[2,96,768]{2,1,0:T(8,128)}, f32[2,96,3072]{2,1,0:T(8,128)}, f32[2,384,76...) custom-call(bf16[4,128,768]{2,1,0:T(8,128)(2,1)} %refs_0_.3, ...), custom_call_target="tpu_custom_call" | custom-call | flops 10000000000 | bytes 100000000 | tf_op jit(solution)/shard_map/backward/pallas_call | solution.py:2310
  425.1 0.0 copy-start.2
  425.1 1.4 copy.24
  426.5 0.7 slice.6
  427.2 1.3 slice.7
  428.5 0.6 copy.28
  429.1 1.3 copy.25
  430.4 0.0 copy-done.3
  430.4 0.9 copy.36
  431.2 0.0 copy-start.4
  431.2 2.1 copy.37
  433.4 0.0 copy-done.2
  433.4 0.0 copy-start.1
  433.4 1.2 copy.38
  434.6 0.0 copy-done.4
  434.6 0.8 copy.39
  435.4 0.5 copy-done.1
  435.9 0.0 copy-start
  435.9 1.4 copy.40
  437.3 1.1 copy-done
  438.4 0.0 copy-start.5
  438.4 1.4 copy.41
  439.8 0.0 copy-done.5
  439.8 0.6 copy.42
Async XLA Ops:
  224.5 205.8 %copy-start.3 = (bf16[4,128,768]{2,1,0:T(8,128)(2,1)S(1)}, bf16[4,128,768]{2,1,0:T(8,128)(2,1)}, u32[]{:S(2)}) copy-start(bf16[4,128,768]{2,1,0:T(8,128)(2,1)} %get-tuple-element.34) | copy-start | bytes 2359300
  425.1 8.3 %copy-start.2 = (f32[2,96,2304]{2,1,0:T(8,128)S(1)}, f32[2,96,2304]{2,1,0:T(8,128)}, u32[]{:S(2)}) copy-start(f32[2,96,2304]{2,1,0:T(8,128)} %get-tuple-element.81) | copy-start | bytes 5308420
  431.2 3.3 copy-start.4
  433.4 2.5 copy-start.1
  435.9 2.5 copy-start
  438.4 1.4 copy-start.5

commit v3 on v0

--- a/solution.py
+++ b/solution.py
@@ -1,6 +1,8 @@
 import jax
 import jax.numpy as jnp
 from jax import lax
+from jax.experimental import pallas as pl
+from jax.experimental.pallas import tpu as pltpu
 from jax.sharding import PartitionSpec as P
 
 D = 768
@@ -602,9 +604,2078 @@
     )
 
 
+BF16 = jnp.bfloat16
+F32 = jnp.float32
+PAIRS = HEADS // 2
+OWNERS = (0, 2, 3, 4, 5, 6)
+TOKENS = 128
+PAIR_LANES = 128
+QUERY_STEP = 256
+VEC_ROWS = 16
+KERNEL_VMEM_BYTES = 62 * 1024 * 1024
+SCALE = HEAD_DIM ** (-0.5)
+
+
+def mul(left, right):
+    return lax.dot_general(left, right, (((1,), (0,)), ((), ())), preferred_element_type=F32)
+
+
+def mul_nt(left, right):
+    return lax.dot_general(left, right, (((1,), (1,)), ((), ())), preferred_element_type=F32)
+
+
+def mul_tn(left, right):
+    return lax.dot_general(left, right, (((0,), (0,)), ((), ())), preferred_element_type=F32)
+
+
+def standardize(values):
+    center = values - jnp.mean(values, -1, keepdims=True)
+    rstd = lax.rsqrt(jnp.mean(center * center, -1, keepdims=True) + EPSILON)
+    return (center * rstd, rstd)
+
+
+def norm_back(unit, rstd, unit_grad):
+    first = jnp.mean(unit_grad, -1, keepdims=True)
+    second = jnp.mean(unit_grad * unit, -1, keepdims=True)
+    return rstd * (unit_grad - first - unit * second)
+
+
+def remote(source, target, send_sem, recv_sem, axis, peer):
+    return pltpu.make_async_remote_copy(
+        src_ref=source,
+        dst_ref=target,
+        send_sem=send_sem,
+        recv_sem=recv_sem,
+        device_id={axis: peer},
+        device_id_type=pl.DeviceIdType.MESH,
+    )
+
+
+def greet(axis, peers):
+    barrier = pltpu.get_barrier_semaphore()
+    for peer in peers:
+        pl.semaphore_signal(
+            barrier, inc=1, device_id={axis: peer}, device_id_type=pl.DeviceIdType.MESH
+        )
+    pl.semaphore_wait(barrier, len(peers))
+
+
+def seq_peers(me, count):
+    return [lax.rem(me + step, count) for step in range(1, count)]
+
+
+def plane_peers(me):
+    return [
+        me,
+        me + 1 - 2 * lax.rem(me, 2),
+        lax.rem(me + 2, 4),
+        3 - me,
+    ]
+
+
+def rows_of(block, size=TOKENS):
+    return pl.ds(pl.multiple_of(block * size, size), size)
+
+
+def gelu_parts(values):
+    below = 0.5 * (1.0 + lax.erf(values * (0.5**0.5)))
+    return (values * below, below)
+
+
+def share_stats(columns, send, recv, send_sem, recv_sem, peers):
+    send[...] = columns.T[0:8, :]
+    recv[0] = send[...]
+    copies = [
+        remote(send, recv.at[k], send_sem.at[k], recv_sem.at[k], "section", peers[k])
+        for k in range(1, 4)
+    ]
+    for copy in copies:
+        copy.start()
+    return copies
+
+
+def two_columns(first, second):
+    lane = lax.broadcasted_iota(jnp.int32, (first.shape[0], PAIR_LANES), 1)
+    return jnp.where(lane == 0, first, jnp.where(lane == 1, second, 0.0))
+
+
+def slot_rows(k):
+    return slice(k * TOKENS, (k + 1) * TOKENS)
+
+
+def shaped(shape, kind):
+    return jax.ShapeDtypeStruct(shape, kind)
+
+
+class Named:
+    def __init__(self, groups, refs):
+        names = [name for group in groups for name in group]
+        for name, ref in zip(names, refs, strict=True):
+            setattr(self, name, ref)
+
+
+GROUP_TOKENS = 8 * TOKENS
+WIDE = 4 * TOKENS
+SHARD = D // 8
+
+
+def square(ref):
+    return ref[...].reshape(D, D)
+
+
+def remote_both(source, target, send_sem, recv_sem, section, seq):
+    return pltpu.make_async_remote_copy(
+        src_ref=source,
+        dst_ref=target,
+        send_sem=send_sem,
+        recv_sem=recv_sem,
+        device_id=(section, seq),
+        device_id_type=pl.DeviceIdType.MESH,
+    )
+
+
+def greet_all(barrier, section, me):
+    for other in range(4):
+        for j in range(8):
+
+            @pl.when((section != other) | (me != j))
+            def _():
+                pl.semaphore_signal(
+                    barrier, inc=1, device_id=(other, j), device_id_type=pl.DeviceIdType.MESH
+                )
+
+
+class Place:
+    def __init__(self):
+        self.me = lax.axis_index("seq")
+        self.section = lax.axis_index("section")
+        self.peers = plane_peers(self.section)
+        self.core = lax.rem(self.me, 2)
+        self.chip = lax.div(self.me, 2)
+        self.high = lax.div(self.chip, 2)
+        self.low = lax.rem(self.chip, 2)
+        self.sibling = self.me + 1 - 2 * self.core
+        self.across = 2 * (2 * (1 - self.high) + self.low) + self.core
+        self.next = 2 * (2 * self.high + 1 - self.low) + self.core
+        self.is_owner = (self.me != 1) & (self.me != 7)
+        pair = jnp.where(self.me == 0, 0, self.me - 1)
+        self.my_pair = jnp.where(pair > PAIRS - 1, PAIRS - 1, pair)
+
+
+class LineGather:
+    def __init__(self, place, base, far_sems, near_sems, core_sems):
+        self.place = place
+        self.base = base
+        self.far_sems = far_sems
+        self.near_sems = near_sems
+        self.core_sems = core_sems
+
+    def far(self, high):
+        p = self.place
+        view = self.base.at[high, p.low, p.core]
+        return remote(view, view, self.far_sems[0], self.far_sems[1], "seq", p.across)
+
+    def near(self, low):
+        p = self.place
+        view = self.base.at[:, low, p.core]
+        return remote(view, view, self.near_sems[0], self.near_sems[1], "seq", p.next)
+
+    def cores(self, core):
+        p = self.place
+        view = self.base.at[:, :, core]
+        return remote(view, view, self.core_sems[0], self.core_sems[1], "seq", p.sibling)
+
+    def start(self):
+        self.far(self.place.high).start()
+
+    def pass_line(self):
+        self.far(1 - self.place.high).wait_recv()
+        self.near(self.place.low).start()
+
+    def pass_core(self):
+        self.near(1 - self.place.low).wait_recv()
+        self.cores(self.place.core).start()
+
+    def ready(self):
+        self.cores(1 - self.place.core).wait_recv()
+
+    def drain(self):
+        self.far(self.place.high).wait_send()
+        self.near(self.place.low).wait_send()
+        self.cores(self.place.core).wait_send()
+
+
+FORE_VMEM = dict(gains=0, biases=0, hgains=0, hbiases=0)
+FORE_ANY = dict(embeds_in=0, qkv_w=0, out_w=0, up_w=0, down_w=0)
+FORE_OUT = dict(
+    sub=((4, TOKENS, D), BF16, True),
+    streams_out=((4, TOKENS, D), BF16, False),
+    att_out=((2, TOKENS, D), BF16, False),
+    vecs=((2, VEC_ROWS, D), F32, True),
+    picks_out=((2, GROUP_TOKENS, PAIR_LANES), BF16, False),
+    logs=((8, PAIR_LANES), F32, True),
+    wa_out=((2, 4, 2, 2, 2, SHARD, D), BF16, False),
+    wf_out=((2, 2, 2, 2, 2, SHARD, D), BF16, False),
+    qkv_out=((2, 3, GROUP_TOKENS, PAIR_LANES), BF16, False),
+    pa_out=((2, GROUP_TOKENS, PAIR_LANES), F32, False),
+    pt_out=((2, GROUP_TOKENS, PAIR_LANES), F32, False),
+    hid_out=((2, WIDE, D), BF16, False),
+    up_out=((2, WIDE, D), F32, False),
+    stat_out=((2, WIDE, PAIR_LANES), F32, False),
+    left_out=((2, WIDE, D), BF16, False),
+)
+FORE_SCRATCH = dict(
+    embeds=((4, TOKENS, D), BF16),
+    streams=((4, TOKENS, D), BF16),
+    att=((2, TOKENS, D), BF16),
+    picks=((2, GROUP_TOKENS, PAIR_LANES), BF16),
+    wa=((2, 4, 2, 2, 2, SHARD, D), BF16),
+    wf=((2, 2, 2, 2, 2, SHARD, D), BF16),
+    qkv=((2, 3, GROUP_TOKENS, PAIR_LANES), BF16),
+    pa=((2, GROUP_TOKENS, PAIR_LANES), F32),
+    pt=((2, GROUP_TOKENS, PAIR_LANES), F32),
+    hid=((2, WIDE, D), BF16),
+    up=((2, WIDE, D), F32),
+    stat=((2, WIDE, PAIR_LANES), F32),
+    left=((2, WIDE, D), BF16),
+    raw_up=((2, SHARD, FF), BF16),
+    small_src=((2, 32, PAIR_LANES), BF16),
+    small=((8, 2, 32, PAIR_LANES), BF16),
+    inner=((TOKENS, D), BF16),
+    proj_send=((4, PAIRS, TOKENS, PAIR_LANES), BF16),
+    att_send=((GROUP_TOKENS, PAIR_LANES), BF16),
+    att_recv=((2, PAIRS, TOKENS, PAIR_LANES), BF16),
+    active=((WIDE, D), F32),
+    columns=((WIDE, PAIR_LANES), F32),
+    stat_rows=((PAIR_LANES, WIDE), F32),
+    part_send=((4, TOKENS, D), BF16),
+    part_recv=((2, 4, TOKENS, D), BF16),
+    stat_send=((8, WIDE), F32),
+    stat_recv=((2, 4, 8, WIDE), F32),
+)
+FORE_SEMS = dict(
+    load_sem=(2, 3),
+    embeds_sem=(4,),
+    store_sem=(2, 13),
+    small_s=(8,),
+    small_r=(8,),
+    az_s=(4,),
+    az_r=(4,),
+    line_s=(6, 3),
+    line_r=(6, 3),
+    axy_s=(2, 4),
+    axy_r=(2, 4),
+    axs_s=(2, 4),
+    axs_r=(2, 4),
+    left_s=(4,),
+    left_r=(4,),
+    inner_s=(4,),
+    inner_r=(4,),
+    wide_s=(2, 4, PAIRS),
+    wide_r=(2, 3, 8),
+    att_s=(2, 8),
+    att_r=(2, PAIRS),
+    hid_s=(2, 4),
+    hid_r=(2, 4),
+    stat_s=(2, 4),
+    stat_r=(2, 4),
+    part_s=(2, 4),
+    part_r=(2, 4),
+    sub_s=(4,),
+    sub_r=(4,),
+)
+
+
+def make_picks(lengths_ref, section, my_pair, picks_ref):
+    tokens = lax.broadcasted_iota(jnp.int32, (GROUP_TOKENS, PAIR_LANES), 0)
+    lane = lax.broadcasted_iota(jnp.int32, (GROUP_TOKENS, PAIR_LANES), 1)
+    row_id = jnp.zeros_like(tokens)
+    first = jnp.zeros_like(tokens)
+    end = 0
+    for row in range(lengths_ref.shape[1]):
+        end = end + lengths_ref[section, row]
+        passed = tokens >= end
+        row_id = row_id + jnp.where(passed, 1, 0)
+        first = jnp.where(passed, end, first)
+    pos = (tokens - first).astype(F32)
+    number = lax.shift_right_logical(lane, 2)
+    row = lane - 4 * number
+    ratio = jnp.zeros(lane.shape, F32)
+    for i, each in enumerate(RATIOS):
+        ratio = jnp.where(number == i, float(each), ratio)
+    valid = ratio > 0.5
+    ratio = jnp.where(valid, ratio, 1.0)
+
+    def residue(values):
+        return values - ratio * jnp.floor((values + 0.5) / ratio)
+
+    residues = residue(pos)
+    for head in range(2):
+        wanted = residue(jnp.full(lane.shape, 2 * my_pair + head, jnp.int32).astype(F32))
+        fits = valid & (row == row_id) & (jnp.abs(residues - wanted) < 0.5)
+        picks_ref[head] = jnp.where(fits, 1.0, 0.0).astype(BF16)
+
+
+def forward_kernel(lengths, *refs):
+    b = Named([FORE_VMEM, FORE_ANY, FORE_OUT, FORE_SCRATCH, FORE_SEMS], refs)
+    p = Place()
+    me, section, peers, core = (p.me, p.section, p.peers, p.core)
+    chip, high, low = (p.chip, p.high, p.low)
+
+    barrier = pltpu.get_barrier_semaphore()
+    greet_all(barrier, section, me)
+
+    def block_from_qkv(layer):
+        return pltpu.make_async_copy(
+            b.qkv_w.at[layer, :, pl.ds(pl.multiple_of(lax.rem(section, 3) * D, D), D)],
+            b.wa.at[layer, section, high, low, core],
+            b.load_sem.at[layer, 0],
+        )
+
+    def block_from_out(layer):
+        return pltpu.make_async_copy(
+            b.out_w.at[layer], b.wa.at[layer, section, high, low, core], b.load_sem.at[layer, 0]
+        )
+
+    def load_up(layer):
+        return pltpu.make_async_copy(b.up_w.at[layer], b.raw_up.at[layer], b.load_sem.at[layer, 1])
+
+    def load_down(layer):
+        return pltpu.make_async_copy(
+            b.down_w.at[layer, pl.ds(pl.multiple_of(section * SHARD, SHARD), SHARD)],
+            b.wf.at[layer, 1, high, low, core],
+            b.load_sem.at[layer, 2],
+        )
+
+    def load_embeds(k):
+        return pltpu.make_async_copy(
+            b.embeds_in.at[peers[k]], b.embeds.at[k], b.embeds_sem.at[k]
+        )
+
+    for layer in range(2):
+
+        @pl.when(section != 3)
+        def _():
+            block_from_qkv(layer).start()
+
+        @pl.when(section == 3)
+        def _():
+            block_from_out(layer).start()
+
+        if layer == 0:
+            for k in range(4):
+                load_embeds(k).start()
+        load_up(layer).start()
+        load_down(layer).start()
+
+    def block_loaded(layer):
+        @pl.when(section != 3)
+        def _():
+            block_from_qkv(layer).wait()
+
+        @pl.when(section == 3)
+        def _():
+            block_from_out(layer).wait()
+
+    def pick_up(layer):
+        load_up(layer).wait()
+        load_down(layer).wait()
+        raw = b.raw_up[layer]
+        for s in range(4):
+
+            @pl.when(section == s)
+            def _():
+                b.wf[layer, 0, high, low, core] = jnp.concatenate(
+                    [
+                        raw[:, (4 * j + s) * SHARD : (4 * j + s + 1) * SHARD].astype(F32)
+                        for j in range(8)
+                    ],
+                    1,
+                ).astype(BF16)
+
+    def line_gather(number, base):
+        pairs = [(b.line_s.at[number, i], b.line_r.at[number, i]) for i in range(3)]
+        return LineGather(p, base, *pairs)
+
+    block = [line_gather(layer, b.wa.at[layer, section]) for layer in range(2)]
+    feed_lines = [
+        [line_gather(2 + 2 * layer + which, b.wf.at[layer, which]) for which in range(2)]
+        for layer in range(2)
+    ]
+
+    def first_z(step, source):
+        view = b.wa.at[0, section, lax.div(source, 2), lax.rem(source, 2), core]
+        return remote(
+            view,
+            view,
+            b.az_s.at[step],
+            b.az_r.at[step],
+            "seq",
+            2 * lax.rem(chip + step, 4) + core,
+        )
+
+    def block_plane(layer, k, slot):
+        view = b.wa.at[layer, slot, :, :, core]
+        return remote(view, view, b.axy_s.at[layer, k], b.axy_r.at[layer, k], "section", peers[k])
+
+    def block_across(layer, k, side):
+        view = b.wa.at[layer, peers[k], :, :, side]
+        return remote(view, view, b.axs_s.at[layer, k], b.axs_r.at[layer, k], "seq", p.sibling)
+
+    for layer in range(2):
+        gains = b.gains[layer].astype(F32)
+        biases = b.biases[layer].astype(F32)
+        hidden_gain = b.hgains[layer : layer + 1, :].astype(F32)
+        hidden_bias = b.hbiases[layer].astype(F32)
+        lines = [gains, biases]
+        for each in (hidden_gain, hidden_bias[0:1, :], hidden_bias[1:2, :]):
+            for s in range(4):
+                lines.append(each[:, s * SHARD : (s + 1) * SHARD])
+        lines.append(jnp.zeros((11, SHARD), F32))
+        packed = jnp.concatenate(lines, 0)
+        packed = jnp.concatenate([packed, jnp.zeros((32, PAIR_LANES - SHARD), F32)], 1)
+        b.small_src[layer] = packed.astype(BF16)
+    b.small[me] = b.small_src[...]
+    make_picks(lengths, section, p.my_pair, b.picks)
+    b.logs[...] = jnp.zeros_like(b.logs)
+    block_loaded(0)
+    pl.semaphore_wait(barrier, 31)
+
+    def small_copy(step):
+        return remote(
+            b.small_src,
+            b.small.at[me],
+            b.small_s.at[step],
+            b.small_r.at[step],
+            "seq",
+            lax.rem(me + step, 8),
+        )
+
+    for step in range(1, 8):
+        small_copy(step).start()
+    for step in range(1, 4):
+        first_z(step, chip).start()
+    pick_up(0)
+    for step in range(1, 8):
+        source = lax.rem(me + 8 - step, 8)
+        remote(
+            b.small_src,
+            b.small.at[source],
+            b.small_s.at[step],
+            b.small_r.at[step],
+            "seq",
+            source,
+        ).wait_recv()
+    for layer in range(2):
+        pieces = []
+        for j in range(8):
+            small = b.small[j, layer].astype(F32)
+            lines = [small[0:9]]
+            for third in range(3):
+                line = jnp.zeros((1, PAIR_LANES), F32)
+                for s in range(4):
+                    at = 9 + 4 * third + s
+                    line = line + jnp.where(section == s, small[at : at + 1], 0.0)
+                lines.append(line)
+            lines.append(jnp.zeros((4, PAIR_LANES), F32))
+            pieces.append(jnp.concatenate(lines, 0)[:, 0:SHARD])
+        b.vecs[layer] = jnp.concatenate(pieces, 1)
+
+    def stores(layer, chosen):
+        pairs = (
+            (b.wf.at[layer], b.wf_out.at[layer]),
+            (b.qkv.at[layer], b.qkv_out.at[layer]),
+            (b.pa.at[layer], b.pa_out.at[layer]),
+            (b.pt.at[layer], b.pt_out.at[layer]),
+            (b.hid.at[layer], b.hid_out.at[layer]),
+            (b.up.at[layer], b.up_out.at[layer]),
+            (b.stat.at[layer], b.stat_out.at[layer]),
+            (b.left.at[layer], b.left_out.at[layer]),
+            (b.att.at[layer], b.att_out.at[layer]),
+            (b.streams.at[pl.ds(2 * layer, 2)], b.streams_out.at[pl.ds(2 * layer, 2)]),
+            (b.picks.at[layer], b.picks_out.at[layer]),
+        )
+        return [
+            pltpu.make_async_copy(source, target, b.store_sem.at[layer, i])
+            for i, (source, target) in enumerate(pairs)
+            if i in chosen
+        ]
+
+    def store_block(layer, slot, number):
+        return pltpu.make_async_copy(
+            b.wa.at[layer, slot], b.wa_out.at[layer, slot], b.store_sem.at[layer, number]
+        )
+
+    def wide_copy(layer, k, pair):
+        return remote_both(
+            b.proj_send.at[k, pair],
+            b.qkv.at[layer, lax.rem(section, 3), rows_of(me)],
+            b.wide_s.at[layer, k, pair],
+            b.wide_r.at[layer, lax.rem(section, 3), me],
+            peers[k],
+            OWNERS[pair],
+        )
+
+    def project(layer, arrive):
+        vec = b.vecs.at[layer]
+
+        @pl.when(section != 3)
+        def _():
+            bias = jnp.where(section == 2, vec[6:7, :], 0.0)
+            for k in range(4):
+                if k > 0:
+                    arrive(k)
+                part = mul(b.left[layer, slot_rows(k), :], square(b.wa.at[layer, section])) + bias
+                part = part.astype(BF16)
+                for pair, owner in enumerate(OWNERS):
+                    b.proj_send[k, pair] = part[:, pair * PAIR_LANES : (pair + 1) * PAIR_LANES]
+                    if k > 0:
+                        wide_copy(layer, k, pair).start()
+                    else:
+
+                        @pl.when(me != owner)
+                        def _():
+                            wide_copy(layer, k, pair).start()
+
+                        @pl.when(me == owner)
+                        def _():
+                            b.qkv[layer, section, rows_of(me), :] = b.proj_send[k, pair]
+
+    def wait_projected(layer):
+        @pl.when(p.is_owner)
+        def _():
+            for third in range(3):
+                for source in range(8):
+
+                    @pl.when((section != third) | (me != source))
+                    def _():
+                        remote_both(
+                            b.proj_send.at[0, 0],
+                            b.qkv.at[layer, third, pl.ds(source * TOKENS, TOKENS)],
+                            b.wide_s.at[layer, 0, 0],
+                            b.wide_r.at[layer, third, source],
+                            third,
+                            source,
+                        ).wait_recv()
+
+        @pl.when(section != 3)
+        def _():
+            for k in range(4):
+                for pair, owner in enumerate(OWNERS):
+                    if k > 0:
+                        wide_copy(layer, k, pair).wait_send()
+                    else:
+
+                        @pl.when(me != owner)
+                        def _():
+                            wide_copy(layer, k, pair).wait_send()
+
+    def back_copy(layer, target):
+        return remote(
+            b.att_send.at[pl.ds(target * TOKENS, TOKENS)],
+            b.att_recv.at[layer, p.my_pair],
+            b.att_s.at[layer, target],
+            b.att_r.at[layer, p.my_pair],
+            "seq",
+            target,
+        )
+
+    def attend(layer):
+        lane = lax.broadcasted_iota(jnp.int32, (QUERY_STEP, PAIR_LANES), 1)
+        first_half = lane < HEAD_DIM
+        for step in range(GROUP_TOKENS // QUERY_STEP):
+            start = step * QUERY_STEP
+            keys_end = start + QUERY_STEP
+            rows = slice(start, keys_end)
+            query = b.qkv[layer, 0, rows, :] * jnp.asarray(SCALE, BF16)
+            keys = b.qkv[layer, 1, 0:keys_end, :]
+            values = b.qkv[layer, 2, 0:keys_end, :]
+            causal = lax.broadcasted_iota(jnp.int32, (QUERY_STEP, keys_end), 1) <= (
+                start + lax.broadcasted_iota(jnp.int32, (QUERY_STEP, keys_end), 0)
+            )
+            sums = []
+            totals = []
+            logs = jnp.zeros((1, PAIR_LANES), F32)
+            picked_sum = jnp.zeros((1, PAIR_LANES), F32)
+            for head in range(2):
+                mine = first_half if head == 0 else ~first_half
+                own_query = jnp.where(mine, query, jnp.zeros_like(query))
+                scores = mul_nt(own_query, keys)
+                raised = jnp.where(causal, jnp.exp(scores), 0.0)
+                pick_query = b.picks[head, rows, :]
+                pick_keys = b.picks[head, 0:keys_end, :]
+                counts = mul_nt(pick_query, pick_keys)
+                weighted = (raised * counts).astype(BF16)
+                sums.append(mul(weighted, values))
+                pattern = mul(raised.astype(BF16), pick_keys)
+                picked = pick_query.astype(F32)
+                totals.append(jnp.sum(pattern * picked, -1, keepdims=True))
+                chosen = picked > 0.5
+                logs = logs + jnp.sum(
+                    jnp.where(chosen, jnp.log(jnp.where(chosen, pattern, 1.0)), 0.0),
+                    0,
+                    keepdims=True,
+                )
+                picked_sum = picked_sum + jnp.sum(picked, 0, keepdims=True)
+            b.logs[layer : layer + 1, :] += logs
+            if layer == 0:
+                b.logs[2:3, :] += picked_sum
+            total = jnp.where(first_half, totals[0], totals[1])
+            attended = jnp.where(first_half, sums[0], sums[1]) / total
+            b.pa[layer, rows, :] = attended
+            b.pt[layer, rows, :] = total
+            b.att_send[rows, :] = attended.astype(BF16)
+            for target in (2 * step, 2 * step + 1):
+
+                @pl.when(me != target)
+                def _():
+                    back_copy(layer, target).start()
+
+                @pl.when(me == target)
+                def _():
+                    b.att_recv[layer, p.my_pair] = b.att_send[
+                        target * TOKENS : (target + 1) * TOKENS, :
+                    ]
+
+    def attention_rest(layer, inputs_ref, after):
+        vec = b.vecs.at[layer]
+        wait_projected(layer)
+        feed_lines[layer][0].start()
+        after()
+
+        @pl.when(p.is_owner)
+        def _():
+            attend(layer)
+
+        feed_lines[layer][0].pass_line()
+        for k in range(1, 4):
+
+            @pl.when(peers[k] == 3)
+            def _():
+                block_plane(layer, k, peers[k]).wait_recv()
+                block_across(layer, k, core).start()
+
+        for pair, owner in enumerate(OWNERS):
+
+            @pl.when(me != owner)
+            def _():
+                remote(
+                    b.att_send.at[pl.ds(0, TOKENS)],
+                    b.att_recv.at[layer, pair],
+                    b.att_s.at[layer, 0],
+                    b.att_r.at[layer, pair],
+                    "seq",
+                    owner,
+                ).wait_recv()
+
+            b.att[layer, :, pair * PAIR_LANES : (pair + 1) * PAIR_LANES] = b.att_recv[layer, pair]
+        inner_unit, unused = standardize(b.att[layer].astype(F32))
+        inner = (inner_unit * vec[1:2, :] + vec[4:5, :]).astype(BF16)
+        if layer == 0:
+            b.inner[...] = inner
+        for k in range(1, 4):
+
+            @pl.when(peers[k] == 3)
+            def _():
+                block_across(layer, k, 1 - core).wait_recv()
+
+        branch = mul(inner, square(b.wa.at[layer, 3])) + vec[7:8, :]
+        b.streams[2 * layer] = (inputs_ref[...].astype(F32) + branch).astype(BF16)
+
+    def attention_drain(layer):
+        @pl.when(p.is_owner)
+        def _():
+            for target in range(8):
+
+                @pl.when(me != target)
+                def _():
+                    back_copy(layer, target).wait_send()
+
+    def feed(layer, resting, parting):
+        vec = b.vecs.at[layer]
+        inputs = b.streams[2 * layer].astype(F32)
+        unit, unused = standardize(inputs)
+        b.hid[layer, slot_rows(0), :] = (unit * vec[2:3, :] + vec[5:6, :]).astype(BF16)
+        hidden_copies = [
+            remote(
+                b.hid.at[layer, pl.ds(0, TOKENS)],
+                b.hid.at[layer, pl.ds(k * TOKENS, TOKENS)],
+                b.hid_s.at[layer, k],
+                b.hid_r.at[layer, k],
+                "section",
+                peers[k],
+            )
+            for k in range(1, 4)
+        ]
+        for copy in hidden_copies:
+            copy.start()
+        up_line, down_line = feed_lines[layer]
+        up_line.pass_core()
+        down_line.start()
+        up_line.ready()
+        for k in range(4):
+            if k > 0:
+                hidden_copies[k - 1].wait_recv()
+            upward = mul(b.hid[layer, slot_rows(k), :], square(b.wf.at[layer, 0])) + vec[10:11, :]
+            b.up[layer, slot_rows(k), :] = upward
+            values, unused = gelu_parts(upward)
+            b.active[slot_rows(k), :] = values
+            mean = jnp.mean(values, -1, keepdims=True)
+            center = values - mean
+            b.columns[slot_rows(k), :] = two_columns(
+                mean, jnp.sum(center * center, -1, keepdims=True)
+            )
+            if k == 0:
+                down_line.pass_line()
+        stat_copies = share_stats(
+            b.columns[...],
+            b.stat_send,
+            b.stat_recv.at[layer],
+            b.stat_s.at[layer],
+            b.stat_r.at[layer],
+            peers,
+        )
+        down_line.pass_core()
+        resting()
+        for copy in stat_copies:
+            copy.wait_recv()
+        b.stat_rows[...] = jnp.zeros((PAIR_LANES, WIDE), F32)
+        for k in range(4):
+            means = [b.stat_recv[layer, other, 0:1, slot_rows(k ^ other)] for other in range(4)]
+            squares = [b.stat_recv[layer, other, 1:2, slot_rows(k ^ other)] for other in range(4)]
+            mean = (means[0] + means[1] + means[2] + means[3]) * 0.25
+            spread = squares[0] + squares[1] + squares[2] + squares[3]
+            for each in means:
+                spread = spread + D * (each - mean) * (each - mean)
+            b.stat_rows[0:1, slot_rows(k)] = mean
+            b.stat_rows[1:2, slot_rows(k)] = lax.rsqrt(spread * (1.0 / FF) + EPSILON)
+        b.stat[layer] = b.stat_rows[...].T
+        down_line.ready()
+        branch = None
+        part_copies = []
+        for k in (3, 1, 2, 0):
+            both = b.stat[layer, slot_rows(k), :]
+            inner = (
+                (b.active[slot_rows(k), :] - both[:, 0:1]) * both[:, 1:2] * vec[9:10, :]
+                + vec[11:12, :]
+            ).astype(BF16)
+            part = mul(inner, square(b.wf.at[layer, 1]))
+            if k == 0:
+                branch = part
+            else:
+                b.part_send[k] = part.astype(BF16)
+                part_copies.append(
+                    remote(
+                        b.part_send.at[k],
+                        b.part_recv.at[layer, k],
+                        b.part_s.at[layer, k],
+                        b.part_r.at[layer, k],
+                        "section",
+                        peers[k],
+                    )
+                )
+                part_copies[-1].start()
+        parting()
+        for k, copy in zip((3, 1, 2), part_copies):
+            copy.wait_recv()
+            branch = branch + b.part_recv[layer, k].astype(F32)
+        b.streams[2 * layer + 1] = (inputs + branch + vec[8:9, :]).astype(BF16)
+        for copy in hidden_copies + stat_copies + part_copies:
+            copy.wait_send()
+
+    def sub_away(number):
+        return remote(
+            b.streams.at[number],
+            b.sub.at[section],
+            b.sub_s.at[number],
+            b.sub_r.at[section],
+            "section",
+            number,
+        )
+
+    def sub_own(number):
+        return pltpu.make_async_copy(
+            b.streams.at[number], b.sub.at[section], b.sub_s.at[number]
+        )
+
+    def send_sub(number):
+        @pl.when(section != number)
+        def _():
+            sub_away(number).start()
+
+        @pl.when(section == number)
+        def _():
+            sub_own(number).start()
+
+    for k in range(4):
+        load_embeds(k).wait()
+
+        @pl.when(section != 3)
+        def _():
+            unit, unused = standardize(b.embeds[k].astype(F32))
+            b.left[0, slot_rows(k), :] = (
+                unit * b.vecs[0, 0:1, :] + b.vecs[0, 3:4, :]
+            ).astype(BF16)
+    pick_up(1)
+    for step in range(1, 4):
+        first_z(step, lax.rem(chip + 4 - step, 4)).wait_recv()
+    block[0].cores(core).start()
+
+    @pl.when(section == 3)
+    def _():
+        for k in range(1, 4):
+            block_plane(0, k, section).start()
+
+    block[0].ready()
+    project(0, lambda k: None)
+
+    attention_rest(0, b.embeds.at[0], lambda: None)
+
+    def resting_first():
+        block_loaded(1)
+        block[1].start()
+
+    def parting_first():
+        attention_drain(0)
+        block[1].pass_line()
+
+    feed(0, resting_first, parting_first)
+
+    second = b.vecs.at[1]
+    unit, unused = standardize(b.streams[1].astype(F32))
+    b.left[1, slot_rows(0), :] = (unit * second[0:1, :] + second[3:4, :]).astype(BF16)
+
+    def left_copy(k):
+        return remote(
+            b.left.at[1, pl.ds(0, TOKENS)],
+            b.left.at[1, pl.ds(k * TOKENS, TOKENS)],
+            b.left_s.at[k],
+            b.left_r.at[k],
+            "section",
+            peers[k],
+        )
+
+    for k in (3, 1, 2):
+
+        @pl.when(peers[k] != 3)
+        def _():
+            left_copy(k).start()
+
+    for copy in stores(0, (0, 1, 2, 3, 4, 5, 6, 8, 9, 10)):
+        copy.start()
+    block[1].pass_core()
+    for k in range(1, 4):
+
+        @pl.when(peers[k] != 3)
+        def _():
+            left_copy(k).wait_send()
+
+    @pl.when(section == 3)
+    def _():
+        for k in range(1, 4):
+            block_plane(1, k, section).start()
+
+    block[1].ready()
+    project(1, lambda k: left_copy(k).wait_recv())
+
+    def inner_copy(k):
+        return remote(
+            b.inner,
+            b.left.at[0, pl.ds(k * TOKENS, TOKENS)],
+            b.inner_s.at[k],
+            b.inner_r.at[k],
+            "section",
+            peers[k],
+        )
+
+    def after_second():
+        for k in range(1, 4):
+
+            @pl.when(peers[k] == 3)
+            def _():
+                inner_copy(k).start()
+
+        @pl.when(section == 3)
+        def _():
+            b.left[0, slot_rows(0), :] = b.inner[...]
+
+        send_sub(0)
+        send_sub(1)
+
+    attention_rest(1, b.streams.at[1], after_second)
+
+    def parting_second():
+        for copy in stores(1, (0, 1, 2, 3, 4, 5, 6, 7, 8, 10)):
+            copy.start()
+
+        @pl.when(section == 3)
+        def _():
+            for k in range(1, 4):
+                inner_copy(k).wait_recv()
+
+        for copy in stores(0, (7,)):
+            copy.start()
+        for layer in range(2):
+            store_block(layer, section, 11).start()
+
+            @pl.when(section != 3)
+            def _():
+                store_block(layer, 3, 12).start()
+
+        attention_drain(1)
+
+    feed(1, lambda: None, parting_second)
+    for copy in stores(1, (9,)):
+        copy.start()
+    for step in range(1, 8):
+        small_copy(step).wait_send()
+    for step in range(1, 4):
+        first_z(step, chip).wait_send()
+    block[0].cores(core).wait_send()
+    block[1].drain()
+    for layer in range(2):
+        for line in feed_lines[layer]:
+            line.drain()
+    for layer in range(2):
+        for k in range(1, 4):
+
+            @pl.when(section == 3)
+            def _():
+                block_plane(layer, k, section).wait_send()
+
+            @pl.when(peers[k] == 3)
+            def _():
+                block_across(layer, k, core).wait_send()
+
+    for k in range(1, 4):
+
+        @pl.when(peers[k] == 3)
+        def _():
+            inner_copy(k).wait_send()
+
+    for number in range(2):
+
+        @pl.when(section != number)
+        def _():
+            sub_away(number).wait_send()
+
+        @pl.when(section == number)
+        def _():
+            sub_own(number).wait()
+
+    @pl.when(section < 2)
+    def _():
+        for k in range(1, 4):
+            remote(
+                b.streams.at[0],
+                b.sub.at[peers[k]],
+                b.sub_s.at[0],
+                b.sub_r.at[peers[k]],
+                "section",
+                peers[k],
+            ).wait_recv()
+
+    for layer in range(2):
+        for copy in stores(layer, range(11)):
+            copy.wait()
+    for layer in range(2):
+        store_block(layer, section, 11).wait()
+
+        @pl.when(section != 3)
+        def _():
+            store_block(layer, 3, 12).wait()
+
+
+BACK_VMEM = dict(vecs=0, logs=0)
+BACK_ANY = dict(
+    cotangent_in=0,
+    embeds_in=0,
+    streams_in=0,
+    att_in=0,
+    picks_in=0,
+    wa_in=0,
+    wf_in=0,
+    qkv_in=0,
+    pa_in=0,
+    pt_in=0,
+    hid_in=0,
+    up_in=0,
+    stat_in=0,
+    left_in=0,
+)
+BACK_OUT = dict(
+    sub_f=((4, TOKENS, D), BF16, True),
+    sub_g=((4, TOKENS, D), BF16, True),
+    all_m=((6, 4, SHARD, D), BF16, True),
+    all_v=((2, 4, SHARD, PAIR_LANES), BF16, True),
+    log_total=((8, PAIR_LANES), F32, True),
+)
+BACK_SCRATCH = dict(
+    wa=((2, 2, 2, 2, 2, SHARD, D), BF16),
+    wf=((2, 2, 2, 2, SHARD, D), BF16),
+    qkv=((3, GROUP_TOKENS, PAIR_LANES), BF16),
+    pa=((GROUP_TOKENS, PAIR_LANES), F32),
+    pt=((GROUP_TOKENS, PAIR_LANES), F32),
+    hid=((WIDE, D), BF16),
+    up=((WIDE, D), F32),
+    stat=((WIDE, PAIR_LANES), F32),
+    xs=((5, TOKENS, D), BF16),
+    att=((2, TOKENS, D), BF16),
+    picks=((2, GROUP_TOKENS, PAIR_LANES), BF16),
+    cot=((TOKENS, D), BF16),
+    streams=((4, TOKENS, D), BF16),
+    grads=((WIDE, D), BF16),
+    units=((WIDE, D), F32),
+    unit_grads=((WIDE, D), F32),
+    inners=((WIDE, D), BF16),
+    lows=((WIDE, D), BF16),
+    columns=((WIDE, PAIR_LANES), F32),
+    stat_rows=((PAIR_LANES, WIDE), F32),
+    part_send=((4, TOKENS, D), BF16),
+    part_recv=((4, TOKENS, D), BF16),
+    stat_send=((8, WIDE), F32),
+    stat_recv=((4, 8, WIDE), F32),
+    do_send=((PAIRS, TOKENS, PAIR_LANES), BF16),
+    do_recv=((GROUP_TOKENS, PAIR_LANES), BF16),
+    key_sum=((GROUP_TOKENS, PAIR_LANES), F32),
+    value_sum=((GROUP_TOKENS, PAIR_LANES), F32),
+    d_send=((3, GROUP_TOKENS, PAIR_LANES), BF16),
+    d_recv=((2, 4, PAIRS, TOKENS, PAIR_LANES), BF16),
+    left_src=((TOKENS, D), BF16),
+    right_src=((TOKENS, D), BF16),
+    left=((2, WIDE, D), BF16),
+    right=((2, WIDE, D), BF16),
+    vec_rows=((2, PAIR_LANES, D), F32),
+    hidden_grad=((TOKENS, D), F32),
+    prod=((6, 2, 2, 2, SHARD, D), BF16),
+    prod_v=((2, 2, 2, 2, SHARD, PAIR_LANES), BF16),
+    pair=((6, 2, 2, SHARD, D), BF16),
+    pair_v=((2, 2, 2, SHARD, PAIR_LANES), BF16),
+    near=((6, 2, SHARD, D), BF16),
+    near_v=((2, 2, SHARD, PAIR_LANES), BF16),
+    far=((6, SHARD, D), BF16),
+    far_v=((2, SHARD, PAIR_LANES), BF16),
+    done=((6, SHARD, D), BF16),
+    done_v=((2, SHARD, PAIR_LANES), BF16),
+    log_line=((8, 8, PAIR_LANES), F32),
+    log_plane=((4, 8, PAIR_LANES), F32),
+)
+BACK_SEMS = dict(
+    load_sem=(24,),
+    block_sem=(2, 2),
+    left_sem=(2,),
+    g_s=(2, 4),
+    g_r=(2, 4),
+    stat_s=(2, 4),
+    stat_r=(2, 4),
+    part_s=(2, 4),
+    part_r=(2, 4),
+    do_s=(2, PAIRS),
+    do_r=(2, 8),
+    d_s=(2, 3, 8),
+    d_r=(2, 4, PAIRS),
+    left_s=(2, 4),
+    left_r=(2, 4),
+    right_s=(2, 4),
+    right_r=(2, 4),
+    back_s=(2, 4),
+    back_r=(2, 4),
+    subf_s=(4,),
+    subf_r=(4,),
+    subg_s=(4,),
+    subg_r=(4,),
+    own_sem=(2,),
+    pair_s=(8,),
+    pair_r=(8,),
+    near_s=(8,),
+    near_r=(8,),
+    far_s=(8,),
+    far_r=(8,),
+    all_s=(8, 4),
+    all_r=(8, 4),
+    log_s=(8,),
+    log_r=(8,),
+    log_plane_s=(4,),
+    log_plane_r=(4,),
+)
+
+
+def backward_kernel(*refs):
+    b = Named([BACK_VMEM, BACK_ANY, BACK_OUT, BACK_SCRATCH, BACK_SEMS], refs)
+    p = Place()
+    me, section, peers, core = (p.me, p.section, p.peers, p.core)
+    high, low = (p.high, p.low)
+
+    barrier = pltpu.get_barrier_semaphore()
+    greet_all(barrier, section, me)
+
+    def loads(first, pairs):
+        return [
+            pltpu.make_async_copy(source, target, b.load_sem.at[first + number])
+            for number, (source, target) in enumerate(pairs)
+        ]
+
+    def feed_loads(layer):
+        pairs = (
+            (b.hid_in.at[layer], b.hid),
+            (b.up_in.at[layer], b.up),
+            (b.stat_in.at[layer], b.stat),
+            (b.wf_in.at[layer], b.wf),
+        )
+        return loads(4 * layer, pairs)
+
+    def attention_loads(layer):
+        pairs = (
+            (b.qkv_in.at[layer], b.qkv),
+            (b.pa_in.at[layer], b.pa),
+            (b.pt_in.at[layer], b.pt),
+        )
+        return loads(8 + 3 * layer, pairs)
+
+    def common_loads():
+        pairs = (
+            (b.cotangent_in.at[section], b.cot),
+            (b.embeds_in.at[section], b.xs.at[0]),
+            (b.streams_in, b.xs.at[pl.ds(1, 4)]),
+            (b.att_in, b.att),
+            (b.picks_in, b.picks),
+        )
+        return loads(14, pairs)
+
+    def block_load(layer, number):
+        slot = 3 if number == 1 else section
+        return pltpu.make_async_copy(
+            b.wa_in.at[layer, slot], b.wa.at[layer, number], b.block_sem.at[layer, number]
+        )
+
+    def left_load(layer):
+        return pltpu.make_async_copy(b.left_in.at[layer], b.left.at[layer], b.left_sem.at[layer])
+
+    common = common_loads()
+    common[0].start()
+    for copy in feed_loads(1):
+        copy.start()
+    for layer in (1, 0):
+        for number in (1, 0):
+            block_load(layer, number).start()
+
+    @pl.when(section != 3)
+    def _():
+        left_load(1).start()
+
+    left_load(0).start()
+
+    for copy in common[1:] + attention_loads(1):
+        copy.start()
+    b.log_line[me] = b.logs[...]
+    common[0].wait()
+    b.grads[slot_rows(0), :] = b.cot[...]
+    pl.semaphore_wait(barrier, 31)
+
+    def log_copy(step):
+        return remote(
+            b.logs,
+            b.log_line.at[me],
+            b.log_s.at[step],
+            b.log_r.at[step],
+            "seq",
+            lax.rem(me + step, 8),
+        )
+
+    def log_plane_copy(k, slot):
+        return remote(
+            b.log_plane.at[slot],
+            b.log_plane.at[slot],
+            b.log_plane_s.at[k],
+            b.log_plane_r.at[k],
+            "section",
+            peers[k],
+        )
+
+    def start_logs():
+        for step in range(1, 8):
+            log_copy(step).start()
+
+    def sum_logs():
+        for step in range(1, 8):
+            source = lax.rem(me + 8 - step, 8)
+            remote(
+                b.logs,
+                b.log_line.at[source],
+                b.log_s.at[step],
+                b.log_r.at[step],
+                "seq",
+                source,
+            ).wait_recv()
+        total = b.log_line[0]
+        for j in range(1, 8):
+            total = total + b.log_line[j]
+        b.log_plane[section] = total
+        for k in range(1, 4):
+            log_plane_copy(k, section).start()
+
+    def finish_logs():
+        for k in range(1, 4):
+            log_plane_copy(k, peers[k]).wait_recv()
+        total = b.log_plane[0]
+        for other in range(1, 4):
+            total = total + b.log_plane[other]
+        b.log_total[...] = total
+        for step in range(1, 8):
+            log_copy(step).wait_send()
+        for k in range(1, 4):
+            log_plane_copy(k, section).wait_send()
+
+    class Matrix:
+        def __init__(self, number):
+            self.number = number
+            if number < 6:
+                self.i = number
+                refs = (b.prod, b.pair, b.near, b.far, b.done, b.all_m)
+            else:
+                self.i = number - 6
+                refs = (b.prod_v, b.pair_v, b.near_v, b.far_v, b.done_v, b.all_v)
+            self.prod, self.pair, self.near, self.far, self.done, self.all = refs
+
+        def store(self, value):
+            for j in range(8):
+                self.prod[self.i, j % 2, j // 4, j // 2 % 2] = value[
+                    j * SHARD : (j + 1) * SHARD, :
+                ].astype(BF16)
+
+        def pair_copy(self):
+            n = self.number
+            return remote(
+                self.prod.at[self.i, 1 - core],
+                self.pair.at[self.i],
+                b.pair_s.at[n],
+                b.pair_r.at[n],
+                "seq",
+                p.sibling,
+            )
+
+        def near_copy(self):
+            n = self.number
+            return remote(
+                self.prod.at[self.i, core, :, 1 - low],
+                self.near.at[self.i],
+                b.near_s.at[n],
+                b.near_r.at[n],
+                "seq",
+                p.next,
+            )
+
+        def far_copy(self):
+            n = self.number
+            return remote(
+                self.prod.at[self.i, core, 1 - high, low],
+                self.far.at[self.i],
+                b.far_s.at[n],
+                b.far_r.at[n],
+                "seq",
+                p.across,
+            )
+
+        def all_copy(self, k, slot):
+            n = self.number
+            return remote(
+                self.done.at[self.i],
+                self.all.at[self.i, slot],
+                b.all_s.at[n, k],
+                b.all_r.at[n, k],
+                "section",
+                peers[k],
+            )
+
+        def own_copy(self):
+            return pltpu.make_async_copy(
+                self.done.at[self.i], self.all.at[self.i, section], b.all_s.at[self.number, 0]
+            )
+
+        def step_near(self):
+            self.pair_copy().wait_recv()
+            i = self.i
+            for h in range(2):
+                for l in range(2):
+                    self.prod[i, core, h, l] = (
+                        self.prod[i, core, h, l].astype(F32) + self.pair[i, h, l].astype(F32)
+                    ).astype(BF16)
+            self.near_copy().start()
+
+        def step_far(self):
+            self.near_copy().wait_recv()
+            i = self.i
+            for h in range(2):
+                self.prod[i, core, h, low] = (
+                    self.prod[i, core, h, low].astype(F32) + self.near[i, h].astype(F32)
+                ).astype(BF16)
+            self.far_copy().start()
+
+        def step_plane(self):
+            self.far_copy().wait_recv()
+            i = self.i
+            self.done[i] = (
+                self.prod[i, core, high, low].astype(F32) + self.far[i].astype(F32)
+            ).astype(BF16)
+            for k in (3, 1, 2):
+                self.all_copy(k, section).start()
+            self.own_copy().start()
+
+        def step_end(self):
+            for k in range(1, 4):
+                self.all_copy(k, peers[k]).wait_recv()
+                self.all_copy(k, section).wait_send()
+            self.own_copy().wait()
+            self.pair_copy().wait_send()
+            self.near_copy().wait_send()
+            self.far_copy().wait_send()
+
+    matrices = [Matrix(number) for number in range(8)]
+    up1, down1, att1, up0, down0, att0, vec1, vec0 = matrices
+
+    def sub_copies(number, forward):
+        source = b.xs.at[pl.ds(1, 4)] if forward else b.streams
+        target = b.sub_f if forward else b.sub_g
+        send_sem = b.subf_s if forward else b.subg_s
+        recv_sem = b.subf_r if forward else b.subg_r
+
+        def away():
+            return remote(
+                source.at[number],
+                target.at[section],
+                send_sem.at[number],
+                recv_sem.at[section],
+                "section",
+                number,
+            )
+
+        def own():
+            return pltpu.make_async_copy(
+                source.at[number], target.at[section], b.own_sem.at[0 if forward else 1]
+            )
+
+        return away, own
+
+    def send_sub(number, forward):
+        @pl.when(section != number)
+        def _():
+            sub_copies(number, forward)[0]().start()
+
+        @pl.when(section == number)
+        def _():
+            sub_copies(number, forward)[1]().start()
+
+    def drain_sub(number, forward):
+        @pl.when(section != number)
+        def _():
+            sub_copies(number, forward)[0]().wait_send()
+
+        @pl.when(section == number)
+        def _():
+            sub_copies(number, forward)[1]().wait()
+
+    def receive_sub(source, forward):
+        target = b.sub_f if forward else b.sub_g
+
+        @pl.when(section != source)
+        def _():
+            remote(
+                b.streams.at[0],
+                target.at[source],
+                (b.subf_s if forward else b.subg_s).at[0],
+                (b.subf_r if forward else b.subg_r).at[source],
+                "section",
+                source,
+            ).wait_recv()
+
+    def feed_phase(layer, grad_ref, x_ref, hooks):
+        phase = 1 - layer
+        vec = b.vecs.at[layer]
+        rows = b.vec_rows.at[layer]
+        up_matrix = matrices[3 * phase]
+        down_matrix = matrices[3 * phase + 1]
+        early, middle, parting, late = hooks
+        if layer == 0:
+            b.grads[slot_rows(0), :] = grad_ref[...]
+        grad_copies = [
+            remote(
+                b.grads.at[pl.ds(0, TOKENS)],
+                b.grads.at[pl.ds(k * TOKENS, TOKENS)],
+                b.g_s.at[phase, k],
+                b.g_r.at[phase, k],
+                "section",
+                peers[k],
+            )
+            for k in range(1, 4)
+        ]
+        for k in (3, 1, 2):
+            grad_copies[k - 1].start()
+        rows[...] = jnp.zeros((PAIR_LANES, D), F32)
+        early()
+        feed_ready = feed_loads(layer)
+        for copy in feed_ready[:3]:
+            copy.wait()
+        for k in range(4):
+            both = b.stat[slot_rows(k), :]
+            upward = b.up[slot_rows(k), :]
+            values, below = gelu_parts(upward)
+            b.up[slot_rows(k), :] = below + upward * (
+                jnp.exp(-0.5 * upward * upward) * (0.5 / 3.141592653589793) ** 0.5
+            )
+            unit = (values - both[:, 0:1]) * both[:, 1:2]
+            b.units[slot_rows(k), :] = unit
+            b.inners[slot_rows(k), :] = (unit * vec[9:10, :] + vec[11:12, :]).astype(BF16)
+        feed_ready[3].wait()
+        gain_sum = jnp.zeros((1, D), F32)
+        bias_sum = jnp.zeros((1, D), F32)
+        for k in range(4):
+            if k > 0:
+                grad_copies[k - 1].wait_recv()
+            unit = b.units[slot_rows(k), :]
+            inner_grad = mul_nt(b.grads[slot_rows(k), :], square(b.wf.at[1]))
+            gain_sum = gain_sum + jnp.sum(inner_grad * unit, 0, keepdims=True)
+            bias_sum = bias_sum + jnp.sum(inner_grad, 0, keepdims=True)
+            unit_grad = inner_grad * vec[9:10, :]
+            b.unit_grads[slot_rows(k), :] = unit_grad
+            b.columns[slot_rows(k), :] = two_columns(
+                jnp.sum(unit_grad, -1, keepdims=True), jnp.sum(unit_grad * unit, -1, keepdims=True)
+            )
+        stat_copies = share_stats(
+            b.columns[...],
+            b.stat_send,
+            b.stat_recv,
+            b.stat_s.at[phase],
+            b.stat_r.at[phase],
+            peers,
+        )
+        rows[9:10, :] = gain_sum
+        rows[11:12, :] = bias_sum
+        down_matrix.store(mul_tn(b.inners[...], b.grads[...]))
+        down_matrix.pair_copy().start()
+        middle()
+        for copy in stat_copies:
+            copy.wait_recv()
+        b.stat_rows[...] = jnp.zeros((PAIR_LANES, WIDE), F32)
+        for k in range(4):
+            for line in range(2):
+                parts = [
+                    b.stat_recv[other, line : line + 1, slot_rows(k ^ other)]
+                    for other in range(4)
+                ]
+                b.stat_rows[line : line + 1, slot_rows(k)] = (
+                    parts[0] + parts[1] + parts[2] + parts[3]
+                ) * (1.0 / FF)
+        b.columns[...] = b.stat_rows[...].T
+        hidden_grad = None
+        low_sum = jnp.zeros((1, D), F32)
+        part_copies = []
+        for k in (3, 1, 2, 0):
+            rstd = b.stat[slot_rows(k), :][:, 1:2]
+            both = b.columns[slot_rows(k), :]
+            lowered = (
+                rstd
+                * (
+                    b.unit_grads[slot_rows(k), :]
+                    - both[:, 0:1]
+                    - b.units[slot_rows(k), :] * both[:, 1:2]
+                )
+                * b.up[slot_rows(k), :]
+            ).astype(BF16)
+            b.lows[slot_rows(k), :] = lowered
+            low_sum = low_sum + jnp.sum(lowered.astype(F32), 0, keepdims=True)
+            part = mul_nt(lowered, square(b.wf.at[0]))
+            if k == 0:
+                hidden_grad = part
+            else:
+                b.part_send[k] = part.astype(BF16)
+                part_copies.append(
+                    remote(
+                        b.part_send.at[k],
+                        b.part_recv.at[k],
+                        b.part_s.at[phase, k],
+                        b.part_r.at[phase, k],
+                        "section",
+                        peers[k],
+                    )
+                )
+                part_copies[-1].start()
+        rows[10:11, :] = low_sum
+        up_matrix.store(mul_tn(b.hid[...], b.lows[...]))
+        up_matrix.pair_copy().start()
+        unit, rstd = standardize(x_ref[...].astype(F32))
+        parting()
+        for k, copy in zip((3, 1, 2), part_copies):
+            copy.wait_recv()
+            hidden_grad = hidden_grad + b.part_recv[k].astype(F32)
+        grad = grad_ref[...].astype(F32)
+        number = 2 * layer + 1
+        b.streams[number] = (
+            grad + norm_back(unit, rstd, hidden_grad * vec[2:3, :])
+        ).astype(BF16)
+        rows[2:3, :] = jnp.sum(hidden_grad * unit, 0, keepdims=True)
+        rows[5:6, :] = jnp.sum(hidden_grad, 0, keepdims=True)
+        rows[8:9, :] = jnp.sum(grad, 0, keepdims=True)
+        for copy in grad_copies + stat_copies + part_copies:
+            copy.wait_send()
+        late()
+
+    def attention_phase(layer, grad_ref, x_ref, att_ref, hooks):
+        phase = 1 - layer
+        vec = b.vecs.at[layer]
+        rows = b.vec_rows.at[layer]
+        before, inside, after, during = hooks
+        grad = grad_ref[...]
+        inner_unit, inner_rstd = standardize(att_ref[...].astype(F32))
+        block_load(layer, 1).wait()
+        inner_grad = mul_nt(grad, square(b.wa.at[layer, 1]))
+        att_grad = norm_back(inner_unit, inner_rstd, inner_grad * vec[1:2, :]).astype(BF16)
+        for pair in range(PAIRS):
+            b.do_send[pair] = att_grad[:, pair * PAIR_LANES : (pair + 1) * PAIR_LANES]
+
+        def out_copy(pair):
+            return remote(
+                b.do_send.at[pair],
+                b.do_recv.at[rows_of(me)],
+                b.do_s.at[phase, pair],
+                b.do_r.at[phase, me],
+                "seq",
+                OWNERS[pair],
+            )
+
+        for pair, owner in enumerate(OWNERS):
+
+            @pl.when(me != owner)
+            def _():
+                out_copy(pair).start()
+
+            @pl.when(me == owner)
+            def _():
+                b.do_recv[rows_of(me), :] = b.do_send[pair]
+
+        def left_copy(k):
+            return remote(
+                b.left_src,
+                b.left.at[layer, pl.ds(k * TOKENS, TOKENS)],
+                b.left_s.at[phase, k],
+                b.left_r.at[phase, k],
+                "section",
+                peers[k],
+            )
+
+        def right_copy(k):
+            return remote(
+                b.right_src,
+                b.right.at[layer, pl.ds(k * TOKENS, TOKENS)],
+                b.right_s.at[phase, k],
+                b.right_r.at[phase, k],
+                "section",
+                peers[k],
+            )
+
+        unit, rstd = standardize(x_ref[...].astype(F32))
+        b.left_src[...] = (inner_unit * vec[1:2, :] + vec[4:5, :]).astype(BF16)
+        b.right_src[...] = grad
+        for k in range(1, 4):
+
+            @pl.when(peers[k] == 3)
+            def _():
+                right_copy(k).start()
+                if layer == 1:
+                    left_copy(k).start()
+
+        if layer == 1:
+
+            @pl.when(section == 3)
+            def _():
+                b.left[layer, slot_rows(0), :] = b.left_src[...]
+
+        rows[1:2, :] = jnp.sum(inner_grad * inner_unit, 0, keepdims=True)
+        rows[4:5, :] = jnp.sum(inner_grad, 0, keepdims=True)
+        rows[7:8, :] = jnp.sum(grad.astype(F32), 0, keepdims=True)
+        for copy in attention_loads(layer):
+            copy.wait()
+
+        def back_copy(third, target):
+            return remote_both(
+                b.d_send.at[third, pl.ds(target * TOKENS, TOKENS)],
+                b.d_recv.at[layer, section, p.my_pair],
+                b.d_s.at[phase, third, target],
+                b.d_r.at[phase, section, p.my_pair],
+                third,
+                target,
+            )
+
+        @pl.when(p.is_owner)
+        def _():
+            for source in range(8):
+
+                @pl.when(me != source)
+                def _():
+                    remote(
+                        b.do_send.at[0],
+                        b.do_recv.at[pl.ds(source * TOKENS, TOKENS)],
+                        b.do_s.at[phase, 0],
+                        b.do_r.at[phase, source],
+                        "seq",
+                        source,
+                    ).wait_recv()
+
+        before()
+
+        @pl.when(p.is_owner)
+        def _():
+            b.key_sum[...] = jnp.zeros((GROUP_TOKENS, PAIR_LANES), F32)
+            b.value_sum[...] = jnp.zeros((GROUP_TOKENS, PAIR_LANES), F32)
+            lane = lax.broadcasted_iota(jnp.int32, (QUERY_STEP, PAIR_LANES), 1)
+            first_half = lane < HEAD_DIM
+            for step in reversed(range(GROUP_TOKENS // QUERY_STEP)):
+                start = step * QUERY_STEP
+                keys_end = start + QUERY_STEP
+                block = slice(start, keys_end)
+                plain_query = b.qkv[0, block, :]
+                query = plain_query * jnp.asarray(SCALE, BF16)
+                keys = b.qkv[1, 0:keys_end, :]
+                values = b.qkv[2, 0:keys_end, :]
+                causal = lax.broadcasted_iota(jnp.int32, (QUERY_STEP, keys_end), 1) <= (
+                    start + lax.broadcasted_iota(jnp.int32, (QUERY_STEP, keys_end), 0)
+                )
+                head_grad = b.do_recv[block, :]
+                inverse = 1.0 / b.pt[block, :]
+                head_float = head_grad.astype(F32)
+                products = head_float * b.pa[block, :]
+                scaled = (head_float * inverse).astype(BF16)
+                key_lanes = lax.broadcasted_iota(jnp.int32, (keys_end, PAIR_LANES), 1) < HEAD_DIM
+                query_parts = []
+                key_parts = []
+                value_parts = []
+                for head in range(2):
+                    mine = first_half if head == 0 else ~first_half
+                    own_query = jnp.where(mine, query, jnp.zeros_like(query))
+                    own_grad = jnp.where(mine, head_grad, jnp.zeros_like(head_grad))
+                    delta = jnp.sum(jnp.where(mine, products, 0.0), -1, keepdims=True)
+                    own_inverse = jnp.max(jnp.where(mine, inverse, 0.0), -1, keepdims=True)
+                    counts = mul_nt(b.picks[head, block, :], b.picks[head, 0:keys_end, :])
+                    scores = mul_nt(own_query, keys)
+                    weighted = jnp.where(causal, jnp.exp(scores) * counts, 0.0)
+                    prob_grad = mul_nt(own_grad, values)
+                    score_grad = (weighted * own_inverse * (prob_grad - delta)).astype(BF16)
+                    query_parts.append(mul(score_grad, keys))
+                    key_parts.append(mul_tn(score_grad, plain_query))
+                    value_parts.append(mul_tn(weighted.astype(BF16), scaled))
+                b.key_sum[0:keys_end, :] += jnp.where(key_lanes, key_parts[0], key_parts[1])
+                b.value_sum[0:keys_end, :] += jnp.where(key_lanes, value_parts[0], value_parts[1])
+                query_grad = jnp.where(first_half, query_parts[0], query_parts[1]) * SCALE
+                b.d_send[0, block, :] = query_grad.astype(BF16)
+                b.d_send[1, block, :] = (b.key_sum[block, :] * SCALE).astype(BF16)
+                b.d_send[2, block, :] = b.value_sum[block, :].astype(BF16)
+                for third in range(3):
+                    for target in (2 * step, 2 * step + 1):
+                        away = (section != third) | (me != target)
+
+                        @pl.when(away)
+                        def _():
+                            back_copy(third, target).start()
+
+                        @pl.when(~away)
+                        def _():
+                            b.d_recv[layer, section, p.my_pair] = b.d_send[
+                                third, target * TOKENS : (target + 1) * TOKENS, :
+                            ]
+
+        inside()
+        after()
+        block_load(layer, 0).wait()
+
+        def part_copy(k):
+            return remote(
+                b.part_send.at[k],
+                b.part_recv.at[k],
+                b.back_s.at[phase, k],
+                b.back_r.at[phase, k],
+                "section",
+                peers[k],
+            )
+
+        @pl.when(section != 3)
+        def _():
+            if layer == 1:
+                left_load(layer).wait()
+            for k in (0, 2, 1, 3):
+                for pair, owner in enumerate(OWNERS):
+                    away = me != owner if k == 0 else True
+
+                    @pl.when(away)
+                    def _():
+                        remote_both(
+                            b.d_send.at[0, pl.ds(0, TOKENS)],
+                            b.d_recv.at[layer, peers[k], pair],
+                            b.d_s.at[phase, 0, 0],
+                            b.d_r.at[phase, peers[k], pair],
+                            peers[k],
+                            owner,
+                        ).wait_recv()
+
+                    b.right[layer, slot_rows(k), pair * PAIR_LANES : (pair + 1) * PAIR_LANES] = (
+                        b.d_recv[layer, peers[k], pair]
+                    )
+                part = mul_nt(b.right[layer, slot_rows(k), :], square(b.wa.at[layer, 0]))
+                if k == 0:
+                    b.hidden_grad[...] = part
+                else:
+                    b.part_send[k] = part.astype(BF16)
+                    part_copy(k).start()
+
+        @pl.when(section == 3)
+        def _():
+            b.right[layer, slot_rows(0), :] = b.right_src[...]
+            b.hidden_grad[...] = jnp.zeros((TOKENS, D), F32)
+            for k in range(1, 4):
+                right_copy(k).wait_recv()
+                if layer == 1:
+                    left_copy(k).wait_recv()
+
+        if layer == 0:
+            left_load(layer).wait()
+        matrix = matrices[3 * phase + 2]
+        matrix.store(mul_tn(b.left[layer], b.right[layer]))
+        matrix.pair_copy().start()
+        value_sum = jnp.sum(b.right[layer].astype(F32), 0, keepdims=True)
+        rows[6:7, :] = jnp.where(section == 2, value_sum, 0.0)
+        during()
+        for k in (3, 1, 2):
+
+            @pl.when(peers[k] != 3)
+            def _():
+                part_copy(k).wait_recv()
+                b.hidden_grad[...] += b.part_recv[k].astype(F32)
+
+        hidden_grad = b.hidden_grad[...]
+        b.streams[2 * layer] = (
+            grad.astype(F32) + norm_back(unit, rstd, hidden_grad * vec[0:1, :])
+        ).astype(BF16)
+        rows[0:1, :] = jnp.sum(hidden_grad * unit, 0, keepdims=True)
+        rows[3:4, :] = jnp.sum(hidden_grad, 0, keepdims=True)
+
+        def drain():
+            @pl.when(section != 3)
+            def _():
+                for k in range(1, 4):
+                    part_copy(k).wait_send()
+
+            for k in range(1, 4):
+
+                @pl.when(peers[k] == 3)
+                def _():
+                    right_copy(k).wait_send()
+                    if layer == 1:
+                        left_copy(k).wait_send()
+
+            for pair, owner in enumerate(OWNERS):
+
+                @pl.when(me != owner)
+                def _():
+                    out_copy(pair).wait_send()
+
+            @pl.when(p.is_owner)
+            def _():
+                for third in range(3):
+                    for target in range(8):
+
+                        @pl.when((section != third) | (me != target))
+                        def _():
+                            back_copy(third, target).wait_send()
+
+        return drain
+
+    def nothing():
+        pass
+
+    def middle_first():
+        for copy in common[1:]:
+            copy.wait()
+
+    def late_first():
+        for copy in feed_loads(0):
+            copy.start()
+
+    feed_phase(
+        1,
+        b.cot,
+        b.xs.at[3],
+        (start_logs, middle_first, down1.step_near, late_first),
+    )
+
+    def before_first():
+        down1.step_far()
+        send_sub(2, True)
+
+    def during_first():
+        up1.step_far()
+        sum_logs()
+
+    drain_first = attention_phase(
+        1,
+        b.streams.at[3],
+        b.xs.at[2],
+        b.att.at[1],
+        (before_first, down1.step_plane, up1.step_near, during_first),
+    )
+
+    def early_second():
+        vec1.store(b.vec_rows[1].T)
+        vec1.pair_copy().start()
+        drain_first()
+        for copy in attention_loads(0):
+            copy.start()
+        att1.step_near()
+
+    def middle_second():
+        att1.step_far()
+        vec1.step_near()
+        up1.step_plane()
+
+    def parting_second():
+        down0.step_near()
+        vec1.step_far()
+
+    feed_phase(
+        0,
+        b.streams.at[2],
+        b.xs.at[1],
+        (early_second, middle_second, parting_second, nothing),
+    )
+
+    def before_second():
+        down0.step_far()
+        send_sub(3, True)
+
+    def inside_second():
+        att1.step_plane()
+        vec1.step_plane()
+        down0.step_plane()
+        for number in (2, 1):
+            send_sub(number, False)
+
+        @pl.when(section == 3)
+        def _():
+            for k in range(4):
+                b.sub_g[peers[k]] = b.right[1, slot_rows(k), :]
+
+        finish_logs()
+
+    def during_second():
+        att0.step_near()
+        up0.step_far()
+
+    drain_second = attention_phase(
+        0,
+        b.streams.at[1],
+        b.xs.at[0],
+        b.att.at[0],
+        (before_second, inside_second, up0.step_near, during_second),
+    )
+    vec0.store(b.vec_rows[0].T)
+    vec0.pair_copy().start()
+    att0.step_far()
+    send_sub(0, False)
+    vec0.step_near()
+    up0.step_plane()
+    vec0.step_far()
+    att0.step_plane()
+    vec0.step_plane()
+    drain_second()
+    for matrix in matrices:
+        matrix.step_end()
+    for number in range(3):
+        drain_sub(number, False)
+
+    @pl.when(section != 3)
+    def _():
+        for source in range(4):
+            receive_sub(source, False)
+
+    drain_sub(2, True)
+    drain_sub(3, True)
+
+    @pl.when(section >= 2)
+    def _():
+        for source in range(4):
+            receive_sub(source, True)
+
+
+def finish_kernel(
+    all_m,
+    all_v,
+    sub_a,
+    sub_f,
+    sub_g,
+    log_total,
+    outputs_ref,
+    grads_ref,
+    qkv_ref,
+    out_ref,
+    up_ref,
+    down_ref,
+    gains_ref,
+    biases_ref,
+    hgains_ref,
+    hbiases_ref,
+    means_ref,
+):
+    outputs_ref[...] = jnp.where(lax.axis_index("section") >= 2, sub_f[...], sub_a[...])
+    grads_ref[...] = sub_g[...]
+    for layer in range(2):
+        up_i = 3 * (1 - layer)
+        down_i = up_i + 1
+        for source in range(4):
+            down_ref[layer, source * SHARD : (source + 1) * SHARD, :] = all_m[
+                down_i, source
+            ].astype(F32)
+        for j in range(8):
+            up_ref[layer, :, j * 4 * SHARD : (j + 1) * 4 * SHARD] = jnp.concatenate(
+                [
+                    all_m[up_i, source, :, j * SHARD : (j + 1) * SHARD].astype(F32)
+                    for source in range(4)
+                ],
+                1,
+            )
+        lines = []
+        for source in range(4):
+            block = all_m[up_i + 2, source].astype(F32)
+            if source < 3:
+                qkv_ref[layer, :, source * D : (source + 1) * D] = block
+            else:
+                out_ref[layer] = block
+            tail = all_v[1 - layer, source].astype(F32)
+            tail = jnp.concatenate([tail, jnp.zeros((PAIR_LANES - SHARD, PAIR_LANES), F32)], 0)
+            lines.append(tail.T)
+        model = lines[0] + lines[1] + lines[2] + lines[3]
+        gains_ref[layer] = model[0:3, 0:SHARD]
+        biases_ref[layer] = model[3:9, 0:SHARD]
+        hidden = jnp.concatenate([each[9:12, 0:SHARD] for each in lines], 1)
+        hgains_ref[layer : layer + 1, :] = hidden[0:1, :]
+        hbiases_ref[layer] = hidden[1:3, :]
+    lane = lax.broadcasted_iota(jnp.int32, (8, PAIR_LANES), 1)
+    number = lax.shift_right_logical(lane, 2)
+    sums = jnp.zeros((8, PAIR_LANES), F32)
+    for i in range(5):
+        part = jnp.sum(jnp.where(number == i, log_total[...], 0.0), -1, keepdims=True)
+        sums = sums + jnp.where(lane == i, part, 0.0)
+    means = sums[0:2, :] / jnp.where(lane[0:2, :] < 5, sums[2:3, :], 1.0)
+    means_ref[...] = means[:, 0:5]
+
+
+def run_remote(kernel, number, lengths, near, far, outs, scratch, sems):
+    vmem = pl.BlockSpec(memory_space=pltpu.VMEM)
+    anywhere = pl.BlockSpec(memory_space=pl.ANY)
+    smem = pl.BlockSpec(memory_space=pltpu.SMEM)
+    return pl.pallas_call(
+        kernel,
+        out_shape=[shaped(out[0], out[1]) for out in outs.values()],
+        in_specs=[smem] * len(lengths) + [vmem] * len(near) + [anywhere] * len(far),
+        out_specs=[vmem if out[2] else anywhere for out in outs.values()],
+        scratch_shapes=[pltpu.VMEM(item[0], item[1]) for item in scratch.values()]
+        + [pltpu.SemaphoreType.DMA(item) for item in sems.values()],
+        compiler_params=pltpu.CompilerParams(
+            collective_id=number, has_side_effects=True, vmem_limit_bytes=KERNEL_VMEM_BYTES
+        ),
+        cost_estimate=pl.CostEstimate(
+            flops=10**10, bytes_accessed=100_000_000, transcendentals=0
+        ),
+    )(*lengths, *near, *far)
+
+
+def run_finish(*args):
+    vmem = pl.BlockSpec(memory_space=pltpu.VMEM)
+    outs = [
+        shaped((4, TOKENS, D), BF16),
+        shaped((4, TOKENS, D), BF16),
+        shaped((2, SHARD, 3 * D), F32),
+        shaped((2, SHARD, D), F32),
+        shaped((2, SHARD, FF), F32),
+        shaped((2, 4 * SHARD, D), F32),
+        shaped((2, 3, SHARD), F32),
+        shaped((2, 6, SHARD), F32),
+        shaped((2, 4 * SHARD), F32),
+        shaped((2, 2, 4 * SHARD), F32),
+        shaped((2, 5), F32),
+    ]
+    return pl.pallas_call(
+        finish_kernel,
+        out_shape=outs,
+        in_specs=[vmem] * len(args),
+        out_specs=[vmem] * len(outs),
+        compiler_params=pltpu.CompilerParams(vmem_limit_bytes=KERNEL_VMEM_BYTES),
+    )(*args)
+
+
+def quick_body(
+    embeds,
+    row_lengths,
+    qkv_weight,
+    out_weight,
+    up_weight,
+    down_weight,
+    model_gains,
+    model_biases,
+    hidden_gains,
+    hidden_biases,
+    cotangent,
+):
+    fore = Named(
+        [FORE_OUT],
+        run_remote(
+            forward_kernel,
+            10,
+            (row_lengths,),
+            (model_gains, model_biases, hidden_gains, hidden_biases),
+            (embeds, qkv_weight, out_weight, up_weight, down_weight),
+            FORE_OUT,
+            FORE_SCRATCH,
+            FORE_SEMS,
+        ),
+    )
+    back = Named(
+        [BACK_OUT],
+        run_remote(
+            backward_kernel,
+            20,
+            (),
+            (fore.vecs, fore.logs),
+            (
+                cotangent,
+                embeds,
+                fore.streams_out,
+                fore.att_out,
+                fore.picks_out,
+                fore.wa_out,
+                fore.wf_out,
+                fore.qkv_out,
+                fore.pa_out,
+                fore.pt_out,
+                fore.hid_out,
+                fore.up_out,
+                fore.stat_out,
+                fore.left_out,
+            ),
+            BACK_OUT,
+            BACK_SCRATCH,
+            BACK_SEMS,
+        ),
+    )
+    results = run_finish(
+        back.all_m, back.all_v, fore.sub, back.sub_f, back.sub_g, back.log_total
+    )
+    return (results[0][None], results[1][None]) + tuple(results[2:])
+
+
+def fits_quick(mesh):
+    return mesh.shape["section"] == 4 and mesh.shape["seq"] == 8
+
+
 def solution(mesh):
     return jax.shard_map(
-        body,
+        quick_body if fits_quick(mesh) else body,
         mesh=mesh,
         in_specs=(
             P(None, "seq", None),

time: 3570 us -> 363 us (0.10)
  the two profiles are of different devices: /device:TPU:14 before, /device:TPU:3 now
where the time goes in v3:
time: 363 us; the launch traced here: 357 us
  Pallas kernels  351 us (97%)
  local copies, waits for them, and re-layouts  5.1 us (1%)
    pallas_call x2, Pallas kernels, run_remote(): pl.pallas_call(kernel, out_shape=[shaped(out[0], out[1]) for out in outs....  344 us

profile of v3, /device:TPU:3, one launch (start us, length us, event | category | flops | bytes accessed | tf_op | source)
XLA Modules:
  0.0 356.7 jit_solution(17101492024021848928)
XLA Ops:
  0.6 1.3 copy.22.refs_0_
  1.9 1.3 copy.23.refs_1_
  3.2 165.5 %shard_map.194 = (bf16[4,128,768]{2,1,0:T(8,128)(2,1)}, bf16[4,128,768]{2,1,0:T(8,128)(2,1)}, bf16[2,128,768]{2,1,0:T(8,128)(2,1)}, f32[2,16,768]{2,1,0:T(8,128)...) custom-call(s32[4,4]{1,0:T(4,128)} %lengths.1, ...), custom_call_target="tpu_custom_call" | custom-call | flops 10000000000 | bytes 100000000 | tf_op jit(solution)/shard_map/pallas_call | solution.py:2572
  168.7 178.2 %shard_map.195 = (bf16[4,128,768]{2,1,0:T(8,128)(2,1)}, bf16[4,128,768]{2,1,0:T(8,128)(2,1)}, bf16[6,4,96,768]{3,2,1,0:T(8,128)(2,1)}, bf16[2,4,96,128]{3,2,1,0:T(8,128)(2,1)}, f32[8,128]{1,0:T(8,128)}) custom-call(f32[2,16,768]{2,1,0:T(8,128)} %get-tuple-element.42.refs_0_, f32[8,128]{1,0:T(8,128)} %get-tuple-element.43.refs_1_, ...), custom_call_target="tpu_custom_call" | custom-call | flops 10000000000 | bytes 100000000 | tf_op jit(solution)/shard_map/pallas_call | solution.py:2572
  346.9 6.9 %shard_map.196 = (bf16[4,128,768]{2,1,0:T(8,128)(2,1)}, bf16[4,128,768]{2,1,0:T(8,128)(2,1)}, f32[2,96,2304]{2,1,0:T(8,128)}, f32[2,96,768]{2,1,0:T(8,128)}, f32...) custom-call(bf16[6,4,96,768]{3,2,1,0:T(8,128)(2,1)} %get-tuple-eleme, ...), custom_call_target="tpu_custom_call" | custom-call | tf_op jit(solution)/shard_map/pallas_call | solution.py:2603
  353.9 1.3 copy.24
  355.1 1.3 copy.25
